TPU v7x, 32 devices: a whole 2x2x4 slice. The times are simulated.
32 devices in a mesh: dp: 8 (over y, x, core), tensor: 4 (over z).
Axes of the slice: x: 2, y: 2, z: 4, core: 2. Of those that a mesh axis runs over, the one named last changes fastest.
Arguments:
- hidden_in: bfloat16 [8, 1024, 1152], P('dp', 'tensor'), may hold values from -6 to 6
- time_embed: float32 [8, 6, 1152], P('dp'), may hold values from -3 to 3
- caption_table: bfloat16 [32128, 1152], P('dp', 'tensor'), may hold values from -6 to 6
- caption_ids: int32 [8, 120], P('dp'), may hold values from 0 to 32127
- owners: int32 [64], replicated, may hold values from 0 to 7, as said below
- master: float32 [128, 288, 1152], P('dp', 'tensor')
- first_moment: float32 [128, 288, 1152], P('dp', 'tensor')
- second_moment: float32 [128, 288, 1152], P('dp', 'tensor'), as said below
- mod_table: float32 [6, 1152], replicated, may hold values from -3 to 3
- mod_first: float32 [6, 1152], replicated
- mod_second: float32 [6, 1152], replicated, as said below
- out_grad: bfloat16 [8, 1024, 1152], P('dp', 'tensor'), may hold values from -6 to 6
Outputs:
- block_out: float32 [8, 1024, 1152], P('dp', 'tensor')
- input_grad: float32 [8, 1024, 1152], P('dp', 'tensor')
- new_first: float32 [128, 288, 1152], P('dp', 'tensor')
- new_second: float32 [128, 288, 1152], P('dp', 'tensor')
- new_master: float32 [128, 288, 1152], P('dp', 'tensor')
- mod_new_first: float32 [6, 1152], replicated
- mod_new_second: float32 [6, 1152], replicated
- mod_new: float32 [6, 1152], replicated
Inputs may be any that keep to these rules, and one draw needn't show every extreme that they name: `owners`: each index of dp owns at most 16 row blocks, and some index owns exactly 16. `second_moment`: positive in every entry. `mod_second`: positive in every entry.
All inputs are finite; a program needn't handle non-finite values.
Results may differ from a plain program's by a relative error of at most 0.03.
Values may be sent and summed in bfloat16 or wider, within the bound.
No kernel may reach another device: no remote copies, remote signals or barrier semaphores. Data moves between devices by JAX's collectives and lax.ppermute only.
A program may use at most 256 MiB of HBM per device.

v0:
```python
import math

import jax
import jax.numpy as jnp
import numpy as np
from jax import lax
from jax.experimental import pallas as pl
from jax.experimental.pallas import tpu as pltpu
from jax.sharding import PartitionSpec as P

HEAD_DIM = 72
STEP = 10


norm_eps = 1e-06
beta_one = 0.9
beta_two = 0.999
rate = 0.03
table_rate = 0.3
decay = 0.01
adam_eps = 1e-08
low = jnp.bfloat16


def ranks_of(owners):
    index = jnp.arange(owners.shape[0])
    before = (owners[None, :] == owners[:, None]) & (index[None, :] < index[:, None])
    return jnp.sum(before.astype(jnp.int32), axis=1)


def layer_norm(values):
    center = values - jnp.mean(values, axis=-1, keepdims=True)
    inverse = lax.rsqrt(jnp.mean(center * center, axis=-1, keepdims=True) + norm_eps)
    return (center * inverse, inverse)


def norm_back(grad_rows, normed, inverse, scale_row):
    scaled = grad_rows * (1.0 + scale_row)
    mean_one = jnp.mean(scaled, axis=-1, keepdims=True)
    mean_two = jnp.mean(scaled * normed, axis=-1, keepdims=True)
    return inverse * (scaled - mean_one - normed * mean_two)


def project(rows, weight):
    return jnp.einsum("ld,rd->lr", rows, weight, preferred_element_type=jnp.float32)


def expand(rows, weight):
    return jnp.einsum("lr,rd->ld", rows, weight, preferred_element_type=jnp.float32)


def outer(left, right):
    return jnp.einsum("lr,ld->rd", left, right, preferred_element_type=jnp.float32)


def shift(values, step):
    count = lax.axis_size("tensor")
    return lax.ppermute(values, "tensor", [(i, (i + step) % count) for i in range(count)])


def ring(values):
    return [values] + [shift(values, k) for k in range(1, lax.axis_size("tensor"))]


def to_ring(stacked):
    count = stacked.shape[0]
    twice = jnp.concatenate([stacked, stacked], axis=0)
    return lax.dynamic_slice_in_dim(twice, lax.axis_index("tensor"), count, 0)


def from_ring(stacked, sign):
    count = stacked.shape[0]
    me = lax.axis_index("tensor")
    place = lax.rem(sign * (jnp.arange(count) - me) + 2 * count, count)
    return jnp.take(stacked, place, axis=0, mode="clip")


cheap = pl.CostEstimate(flops=1000, bytes_accessed=1000, transcendentals=0)
costly = pl.CostEstimate(flops=10**10, bytes_accessed=10**7, transcendentals=0)


def self_attend(qkv, share):
    length = qkv.shape[0]
    rows = min(512, length)
    curve = HEAD_DIM ** (-0.5) * math.log2(math.e)
    heads = share // HEAD_DIM

    def body(qkv_ref, out_ref, log_ref):
        @pl.loop(0, length // rows)
        def _(step):
            here = pl.ds(pl.multiple_of(step * rows, rows), rows)
            parts = []
            for head in range(heads):
                at = head * HEAD_DIM
                q = qkv_ref[here, at : at + HEAD_DIM]
                k = qkv_ref[:, share + at : share + at + HEAD_DIM]
                v = qkv_ref[:, 2 * share + at : 2 * share + at + HEAD_DIM]
                scores = dot(k, q, nt)
                top = jnp.max(scores, axis=0, keepdims=True)
                expo = jnp.exp2((scores - top) * curve)
                total = jnp.sum(expo, axis=0, keepdims=True)
                log_ref[head : head + 1, here] = top * curve + jnp.log2(total)
                parts.append((dot(v, expo.astype(low), tn) * (1.0 / total)).T)
            out_ref[here, :] = jnp.concatenate(parts, axis=1).astype(low)

    return pl.pallas_call(
        body,
        out_shape=[
            jax.ShapeDtypeStruct((length, share), low),
            jax.ShapeDtypeStruct((heads, length), jnp.float32),
        ],
        compiler_params=pltpu.CompilerParams(vmem_limit_bytes=40 * 2**20),
        cost_estimate=cheap,
        name="self_attend",
    )(qkv)


def self_attend_back(qkv, grads, mixed, logs, share, begin, end):
    length = qkv.shape[0]
    rows = length // len(grads)
    span = end - begin
    scale = HEAD_DIM ** (-0.5)
    curve = scale * math.log2(math.e)

    def body(qkv_ref, mixed_ref, log_ref, *refs):
        grad_refs, (out_ref, grad_k, grad_v) = refs[: len(grads)], refs[len(grads) :]
        for step, grad_ref in enumerate(grad_refs):
            here = slice(step * rows, (step + 1) * rows)
            parts = []
            for head, at in enumerate(range(begin, end, HEAD_DIM)):
                q = qkv_ref[here, at : at + HEAD_DIM]
                k = qkv_ref[:, share + at : share + at + HEAD_DIM]
                v = qkv_ref[:, 2 * share + at : 2 * share + at + HEAD_DIM]
                g = grad_ref[0:rows, at : at + HEAD_DIM]
                o = mixed_ref[here, at : at + HEAD_DIM]
                inner = g.astype(jnp.float32) * o.astype(jnp.float32)
                inner = jnp.sum(inner.T, axis=0, keepdims=True)
                which = begin // HEAD_DIM + head
                probs = jnp.exp2(dot(k, q, nt) * curve - log_ref[which : which + 1, here])
                grad_scores = (probs * (dot(v, g, nt) - inner)).astype(low)
                to_v = dot(probs.astype(low), g)
                to_k = dot(grad_scores, q)
                if step:
                    grad_v[head] += to_v
                    grad_k[head] += to_k
                else:
                    grad_v[head] = to_v
                    grad_k[head] = to_k
                parts.append((dot(k, grad_scores, tn) * scale).T)
            out_ref[here, 0:span] = jnp.concatenate(parts, axis=1).astype(low)
        heads = range(span // HEAD_DIM)
        both = [grad_k[head] * scale for head in heads]
        out_ref[:, span : 2 * span] = jnp.concatenate(both, axis=1).astype(low)
        both = [grad_v[head] for head in heads]
        out_ref[:, 2 * span :] = jnp.concatenate(both, axis=1).astype(low)

    return pl.pallas_call(
        body,
        out_shape=jax.ShapeDtypeStruct((length, 3 * span), low),
        scratch_shapes=[pltpu.VMEM((span // HEAD_DIM, length, HEAD_DIM), jnp.float32)] * 2,
        compiler_params=pltpu.CompilerParams(vmem_limit_bytes=40 * 2**20),
        cost_estimate=costly,
        name="self_attend_back",
    )(qkv, mixed, logs, *grads)


def mlp_core(rows_in, grads_in, w_mlp, after):
    groups = len(rows_in)
    tokens, width = rows_in[0].shape
    hidden = w_mlp.shape[0] // 2
    chunk = 384 if hidden % 384 == 0 else hidden
    steps = hidden // chunk
    curve = 0.7978845608028654

    def body(*refs):
        rows, grads = refs[:groups], refs[groups : 2 * groups]
        up, down = refs[2 * groups : 2 * groups + 2]
        act, grad_pre, *outs = refs[2 * groups + 2 + len(after) : -1]
        total = refs[-1]
        step = pl.program_id(0)
        for i in range(groups):
            pre = lax.dot_general(
                rows[i][...], up[...], (((1,), (1,)), ((), ())), preferred_element_type=jnp.float32
            )
            square = pre * pre
            bend = jnp.tanh(curve * pre * (1.0 + 0.044715 * square))
            half = 0.5 * (1.0 + bend)
            here = pl.ds(i * tokens, tokens)
            act[here, :] = (pre * half).astype(low)
            slope = half + (0.5 * curve) * pre * (1.0 - bend * bend) * (1.0 + 0.134145 * square)
            grad_act = lax.dot_general(
                grads[i][...], down[...], (((1,), (1,)), ((), ())), preferred_element_type=jnp.float32
            )
            grad_low = (grad_act * slope).astype(low)
            grad_pre[here, :] = grad_low
            term = jnp.dot(grad_low, up[...], preferred_element_type=jnp.float32)

            @pl.when(step == 0)
            def _():
                total[here, :] = term

            @pl.when(step > 0)
            def _():
                total[here, :] += term

            @pl.when(step == steps - 1)
            def _():
                outs[i][...] = total[here, :].astype(low)

    whole = pl.BlockSpec((tokens, width), lambda s: (0, 0))
    across = pl.BlockSpec((groups * tokens, chunk), lambda s: (0, s))
    return pl.pallas_call(
        body,
        grid=(steps,),
        in_specs=[whole] * (2 * groups)
        + [
            pl.BlockSpec((chunk, width), lambda s: (s, 0)),
            pl.BlockSpec((chunk, width), lambda s: (steps + s, 0)),
        ]
        + [pl.BlockSpec(memory_space=pl.ANY)] * len(after),
        out_specs=[across, across] + [whole] * groups,
        out_shape=[jax.ShapeDtypeStruct((groups * tokens, hidden), low)] * 2
        + [jax.ShapeDtypeStruct((tokens, width), low)] * groups,
        scratch_shapes=[pltpu.VMEM((groups * tokens, width), jnp.float32)],
        compiler_params=pltpu.CompilerParams(vmem_limit_bytes=60 * 2**20),
        cost_estimate=cheap,
        name="mlp_core",
    )(*rows_in, *grads_in, w_mlp, w_mlp, *after)


nt = (((1,), (1,)), ((), ()))
tn = (((0,), (0,)), ((), ()))


def dot(left, right, dims=(((1,), (0,)), ((), ()))):
    return lax.dot_general(left, right, dims, preferred_element_type=jnp.float32)


def softmax_keys(keys, queries):
    scores = dot(keys, queries, nt) * HEAD_DIM ** (-0.5)
    expo = jnp.exp(scores - jnp.max(scores, axis=0, keepdims=True))
    return expo * (1.0 / jnp.sum(expo, axis=0, keepdims=True))


def cuts_of(width):
    size = 384 if width % 384 == 0 else width
    return [slice(i, i + size) for i in range(0, width, size)]


def in_smem():
    return pl.BlockSpec(memory_space=pltpu.SMEM)


def in_vmem():
    return pl.BlockSpec(memory_space=pltpu.VMEM)


def line_slots(place, own, ups, downs, rows):
    count = len(ups) + 1
    tokens, width = own.shape

    def body(place_ref, *refs):
        own_ref, up_refs, down_refs = refs[0], refs[1:count], refs[count : 2 * count - 1]
        rows_ref, outs, out = refs[2 * count - 1], refs[2 * count : -1], refs[-1]
        me = place_ref[0]

        def modulate(slot, ref):
            value = ref[...].astype(jnp.float32)
            value = value * (1.0 + rows_ref[1:2, :]) + rows_ref[0:1, :]
            out[slot * tokens : (slot + 1) * tokens, :] = value.astype(low)

        modulate(0, own_ref)
        for k in range(1, count):
            for side, ref in ((me >= k, up_refs[k - 1]), (me < k, down_refs[count - k - 1])):

                @pl.when(side)
                def _():
                    outs[k - 1][...] = ref[...]
                    modulate(k, ref)

    shapes = [(tokens, width)] * (count - 1) + [(count * tokens, width)]
    return pl.pallas_call(
        body,
        in_specs=[in_smem()] + [in_vmem()] * (2 * count),
        out_shape=[jax.ShapeDtypeStruct(shape, low) for shape in shapes],
        compiler_params=pltpu.CompilerParams(vmem_limit_bytes=32 * 2**20),
        cost_estimate=cheap,
        name="line_slots",
    )(place, own, *ups, *downs, rows)


def cross_block(place, mixed, hidden, rows, text, w_out, c_query, c_value, c_out):
    count, share = len(mixed), mixed[0].shape[1]
    tokens, width = hidden.shape
    words = text.shape[0]
    per = share // HEAD_DIM

    def body(place_ref, *refs):
        parts = refs[:count]
        x_ref, rows_ref, text_ref = refs[count : count + 3]
        far = refs[count + 3 : count + 7]
        outs = refs[count + 7 : count + 16]
        inverse = refs[count + 16]
        wo, wq, wv, wc, *own = refs[count + 17 : -3]
        held, read, sems = refs[-3:]
        branch, res_low, cq, ck, cv, crossed, res, normed, out = own
        me = place_ref[0]
        loads = [
            pltpu.make_async_copy(source, target, read.at[i])
            for i, (source, target) in enumerate(zip(far, (wo, wq, wv, wc)))
        ]
        stores = [
            pltpu.make_async_copy(source, target, sems.at[i])
            for i, (source, target) in enumerate(zip(own, outs))
        ]
        for load in loads:
            load.start()
        loads[0].wait()
        for cut in cuts_of(width):
            total = jnp.zeros((tokens, cut.stop - cut.start), jnp.float32)
            for k in range(count):
                rank = lax.rem(me + k, count)
                here = pl.ds(pl.multiple_of(rank * share, 32), share)
                total += dot(parts[k][0:tokens, :], wo[here, cut])
            branch[:, cut] = total
            first = x_ref[:, cut].astype(jnp.float32) + rows_ref[0:1, cut] * total
            res[:, cut] = first
            res_low[:, cut] = first.astype(low)
        stores[0].start()
        stores[1].start()
        loads[1].wait()
        loads[2].wait()
        for cut in cuts_of(width):
            cq[:, cut] = dot(res_low[...], wq[cut, :], nt).astype(low)
            cv[:, cut] = dot(text_ref[...], wv[cut, :], nt).astype(low)
        for k in range(count):
            held[lax.rem(me + k, count)] = parts[k][tokens:, :]
        ck[...] = jnp.concatenate([held[rank] for rank in range(count)], axis=1)
        for i in (2, 3, 4):
            stores[i].start()
        parts_out = []
        for at in range(0, width, HEAD_DIM):
            head = slice(at, at + HEAD_DIM)
            probs = softmax_keys(ck[:, head], cq[:, head]).astype(low)
            parts_out.append(dot(cv[:, head], probs, tn).T)
        crossed[...] = jnp.concatenate(parts_out, axis=1).astype(low)
        stores[5].start()
        loads[3].wait()
        for cut in cuts_of(width):
            res[:, cut] += dot(crossed[...], wc[:, cut])
        second = res[...]
        center = second - jnp.mean(second, axis=-1, keepdims=True)
        spread = lax.rsqrt(jnp.mean(center * center, axis=-1, keepdims=True) + norm_eps)
        inverse[...] = spread
        scaled = center * spread
        normed[...] = scaled
        stores[6].start()
        stores[7].start()
        out[...] = (scaled * (1.0 + rows_ref[2:3, :]) + rows_ref[1:2, :]).astype(low)
        stores[8].start()
        for store in stores:
            store.wait()

    wide = (tokens, width)
    shapes = [
        (wide, jnp.float32),
        (wide, low),
        (wide, low),
        ((words, width), low),
        ((words, width), low),
        (wide, low),
        (wide, jnp.float32),
        (wide, jnp.float32),
        (wide, low),
    ]
    anywhere = pl.BlockSpec(memory_space=pl.ANY)
    return pl.pallas_call(
        body,
        in_specs=[in_smem()] + [in_vmem()] * (count + 3) + [anywhere] * 4,
        out_specs=[anywhere] * len(shapes) + [in_vmem()],
        out_shape=[jax.ShapeDtypeStruct(*item) for item in shapes]
        + [jax.ShapeDtypeStruct((tokens, 1), jnp.float32)],
        scratch_shapes=[pltpu.VMEM((width, width), low)] * 4
        + [pltpu.VMEM(*item) for item in shapes]
        + [
            pltpu.VMEM((count, words, share), low),
            pltpu.SemaphoreType.DMA((4,)),
            pltpu.SemaphoreType.DMA((len(shapes),)),
        ],
        compiler_params=pltpu.CompilerParams(vmem_limit_bytes=60 * 2**20),
        cost_estimate=cheap,
        name="cross_block",
    )(place, *mixed, hidden, rows, text, w_out, c_query, c_value, c_out)


def cross_back(
    place, terms, grad, rows, normed, inverse, branch, cq, ck, cv, c_out, c_query, w_out, after
):
    count = len(terms)
    tokens, width = grad.shape
    words = ck.shape[0]
    share = width // count
    scale = HEAD_DIM ** (-0.5)

    def body(place_ref, *refs):
        parts = refs[:count]
        grad_ref, rows_ref, i_ref, k_ref, v_ref = refs[count : count + 5]
        far = refs[count + 5 : count + 11]
        refs = refs[: count + 11] + refs[count + 11 + len(after) :]
        stored = refs[count + 11 : count + 15]
        grad_v, sums = refs[count + 15 : count + 17]
        outs = refs[count + 17 : 2 * count + 17]
        near = refs[2 * count + 17 : 2 * count + 23]
        n_ref, wc, q_ref, wq, wo, b_ref = near
        own = refs[2 * count + 23 : 2 * count + 27]
        first, cross_low, grad_q, attn_low = own
        back, held, read, sems = refs[2 * count + 27 :]
        me = place_ref[0]
        loads = [
            pltpu.make_async_copy(source, target, read.at[i])
            for i, (source, target) in enumerate(zip(far, near))
        ]
        stores = [
            pltpu.make_async_copy(source, target, sems.at[i])
            for i, (source, target) in enumerate(zip(own, stored))
        ]
        for load in loads:
            load.start()
        loads[0].wait()
        total = parts[0][...].astype(jnp.float32)
        for part in parts[1:]:
            total += part[...].astype(jnp.float32)
        n = n_ref[...]
        sums[1:2, :] = jnp.sum(total, axis=0, keepdims=True)
        sums[2:3, :] = jnp.sum(total * n, axis=0, keepdims=True)
        second = grad_ref[...].astype(jnp.float32) + norm_back(total, n, i_ref[...], rows_ref[2:3, :])
        first[...] = second
        cross_low[...] = second.astype(low)
        stores[1].start()
        loads[1].wait()
        loads[2].wait()
        for cut in cuts_of(width):
            back[:, cut] = dot(cross_low[...], wc[cut, :], nt).astype(low)
        grads = ([], [], [])
        for at in range(0, width, HEAD_DIM):
            head = slice(at, at + HEAD_DIM)
            q, k, v, g = q_ref[:, head], k_ref[:, head], v_ref[:, head], back[:, head]
            probs = softmax_keys(k, q)
            grad_probs = dot(v, g, nt)
            inner = jnp.sum(probs * grad_probs, axis=0, keepdims=True)
            grad_scores = (probs * (grad_probs - inner)).astype(low)
            grads[0].append((dot(k, grad_scores, tn) * scale).T)
            grads[1].append(dot(grad_scores, q) * scale)
            grads[2].append(dot(probs.astype(low), g))
        grad_q[...] = jnp.concatenate(grads[0], axis=1).astype(low)
        grad_v[...] = jnp.concatenate(grads[2], axis=1).astype(low)
        heads = share // HEAD_DIM
        for rank in range(count):
            pieces = grads[1][rank * heads : (rank + 1) * heads]
            held[rank] = jnp.concatenate(pieces, axis=1).astype(low)
        stores[2].start()
        for load in loads[3:]:
            load.wait()
        for cut in cuts_of(width):
            whole = first[:, cut] + dot(grad_q[...], wq[:, cut])
            first[:, cut] = whole
            attn_low[:, cut] = (rows_ref[0:1, cut] * whole).astype(low)
            sums[0:1, cut] = jnp.sum(b_ref[:, cut] * whole, axis=0, keepdims=True)
        stores[0].start()
        stores[3].start()
        for k in range(count):
            rank = lax.rem(me + k, count)
            here = pl.ds(pl.multiple_of(rank * share, 32), share)
            outs[k][0:tokens, :] = dot(attn_low[...], wo[here, :], nt).astype(low)
            outs[k][tokens:, :] = held[rank]
        for store in stores:
            store.wait()

    wide, square = (tokens, width), (width, width)
    shapes = [
        (wide, jnp.float32),
        (wide, low),
        (wide, low),
        (wide, low),
        ((words, width), low),
        ((3, width), jnp.float32),
    ] + [((tokens + words, share), low)] * count
    anywhere = pl.BlockSpec(memory_space=pl.ANY)
    loaded = [
        pltpu.VMEM(wide, jnp.float32),
        pltpu.VMEM(square, low),
        pltpu.VMEM(wide, low),
        pltpu.VMEM(square, low),
        pltpu.VMEM(square, low),
        pltpu.VMEM(wide, jnp.float32),
    ]
    return pl.pallas_call(
        body,
        in_specs=[in_smem()] + [in_vmem()] * (count + 5) + [anywhere] * (6 + len(after)),
        out_specs=[anywhere] * 4 + [in_vmem()] * (2 + count),
        out_shape=[jax.ShapeDtypeStruct(*item) for item in shapes],
        scratch_shapes=loaded
        + [pltpu.VMEM(*item) for item in shapes[:4]]
        + [
            pltpu.VMEM(wide, low),
            pltpu.VMEM((count, words, share), low),
            pltpu.SemaphoreType.DMA((6,)),
            pltpu.SemaphoreType.DMA((4,)),
        ],
        compiler_params=pltpu.CompilerParams(vmem_limit_bytes=60 * 2**20),
        cost_estimate=costly,
        name="cross_back",
    )(
        place,
        *terms,
        grad,
        rows,
        inverse,
        ck,
        cv,
        normed,
        c_out,
        cq,
        c_query,
        w_out,
        branch,
        *after,
    )


def outer_halves(place, pairs, parts, name):
    width = pairs[0][1].shape[1]
    high = [sum(piece[2] for piece in left) for left, _ in pairs]
    size = high[0] // parts
    tokens = [right.shape[0] for _, right in pairs]
    flat = []

    def index_of(array):
        for i, other in enumerate(flat):
            if other is array:
                return i
        flat.append(array)
        return len(flat) - 1

    plans = [
        ([(index_of(array), *rest) for array, *rest in left], index_of(right))
        for left, right in pairs
    ]
    amount = len(pairs)

    def body(place_ref, *refs):
        ins, (kept, given), (held, sems) = refs[: len(flat)], refs[len(flat) :][:2], refs[-2:]
        turned = refs[len(flat) + 2 : -2]
        me, core = place_ref[0], place_ref[1]
        for i, (left, right) in enumerate(plans):
            for k, (which, lane, lanes, row) in enumerate(left):
                piece = ins[which][0 : tokens[i], lane : lane + lanes]
                piece = piece.astype(jnp.float32).T.astype(low)
                if row is None:
                    rank = lax.rem(me + k, len(left))
                    turned[i][pl.ds(pl.multiple_of(rank * lanes, 32), lanes), :] = piece
                else:
                    turned[i][row : row + lanes, :] = piece
            for part in range(parts):
                at = i * parts + part
                tile = dot(turned[i][part * size : (part + 1) * size, :], ins[right][...])
                held[at] = tile.astype(low)
                for out, side in ((kept, 0), (given, 1)):

                    @pl.when((core ^ (i & 1)) == side)
                    def _():
                        pltpu.make_async_copy(
                            held.at[at], out.at[i // 2, part], sems.at[at]
                        ).start()

        for at in range(amount * parts):
            pltpu.make_async_copy(held.at[at], kept.at[0, 0], sems.at[at]).wait()

    out = jax.ShapeDtypeStruct((amount // 2, parts, size, width), low)
    return pl.pallas_call(
        body,
        in_specs=[in_smem()] + [in_vmem()] * len(flat),
        out_specs=[pl.BlockSpec(memory_space=pl.ANY)] * 2,
        out_shape=[out, out],
        scratch_shapes=[pltpu.VMEM((high[i], tokens[i]), low) for i in range(amount)]
        + [
            pltpu.VMEM((amount * parts, size, width), low),
            pltpu.SemaphoreType.DMA((amount * parts,)),
        ],
        compiler_params=pltpu.CompilerParams(vmem_limit_bytes=60 * 2**20),
        cost_estimate=cheap if parts > 1 else costly,
        name=name,
    )(place, *flat)


def mlp_grads(grad_pres, acts, rows_in, grads_in):
    pieces, rights = len(acts), len(rows_in)
    tokens, width = rows_in[0].shape
    hidden = acts[0].shape[1]
    chunk = 384 if hidden % 384 == 0 else hidden
    steps = hidden // chunk

    def body(*refs):
        step = pl.program_id(0)
        lefts_up, lefts_down = refs[:pieces], refs[pieces : 2 * pieces]
        rights_up = refs[2 * pieces : 2 * pieces + rights]
        rights_down = refs[2 * pieces + rights : -1]
        out = refs[-1]

        def terms(lefts, turn, others):
            here = pl.ds(pl.multiple_of(turn * chunk, chunk), chunk)
            total = jnp.zeros((chunk, width), jnp.float32)
            cursor = 0
            for left in lefts:
                for i in range(left.shape[0] // tokens):
                    total += dot(left[i * tokens : (i + 1) * tokens, here], others[cursor][...], tn)
                    cursor += 1
            out[...] = total.astype(low)

        @pl.when(step < steps)
        def _():
            terms(lefts_up, step, rights_up)

        @pl.when(step >= steps)
        def _():
            terms(lefts_down, step - steps, rights_down)

    arrays = (*grad_pres, *acts, *rows_in, *grads_in)
    chunked = pl.BlockSpec((chunk, width), lambda s: (s, 0))
    return pl.pallas_call(
        body,
        grid=(2 * steps,),
        in_specs=[pl.BlockSpec(array.shape, lambda s: (0, 0)) for array in arrays],
        out_specs=chunked,
        out_shape=jax.ShapeDtypeStruct((2 * hidden, width), low),
        compiler_params=pltpu.CompilerParams(vmem_limit_bytes=60 * 2**20),
        cost_estimate=cheap,
        name="mlp_grads",
    )(*arrays)


def ranked_terms(place, lefts, order, pieces, weight, factors, name):
    tokens, width = factors[0].shape
    count = len(factors)

    def body(place_ref, *refs):
        ins, weight_ref = refs[: len(lefts)], refs[len(lefts)]
        others = refs[len(lefts) + 1 : len(lefts) + 1 + count]
        out, sums = refs[-2:]
        me = place_ref[0]
        for i, slot in enumerate(order):
            rank = lax.rem(me - slot + count, count)
            for cut in cuts_of(width):
                term = jnp.zeros((tokens, cut.stop - cut.start), jnp.float32)
                for which, row, lane, start, depth in pieces[i]:
                    term += dot(
                        ins[which][row : row + tokens, lane : lane + depth],
                        weight_ref[start : start + depth, cut],
                    )
                out[rank, :, cut] = term.astype(low)
                one = jnp.sum(term, axis=0, keepdims=True)
                two = jnp.sum(term * others[i][:, cut].astype(jnp.float32), axis=0, keepdims=True)
                if i:
                    one, two = one + sums[0:1, cut], two + sums[1:2, cut]
                sums[0:1, cut], sums[1:2, cut] = one, two

    return pl.pallas_call(
        body,
        in_specs=[in_smem()] + [in_vmem()] * (len(lefts) + 1 + count),
        out_shape=[
            jax.ShapeDtypeStruct((count, tokens, width), low),
            jax.ShapeDtypeStruct((2, width), jnp.float32),
        ],
        compiler_params=pltpu.CompilerParams(vmem_limit_bytes=60 * 2**20),
        cost_estimate=cheap if len(lefts) > 2 else costly,
        name=name,
    )(place, *lefts, weight, *factors)


def sum_split(place, kept, got):
    count, unit_rows, width = kept.shape[1], kept.shape[4], kept.shape[5]

    def body(place_ref, one, two, keep_x, give_x, keep_y, give_y):
        x, y = place_ref[0], place_ref[1]

        def total(*index):
            return (one[index].astype(jnp.float32) + two[index].astype(jnp.float32)).astype(low)

        for j in range(2):
            keep_x[0, j] = total(0, 0, j, x)
            give_x[0, j] = total(0, 0, j, 1 - x)
            keep_y[0, j] = total(1, 0, y, j)
            give_y[0, j] = total(1, 0, 1 - y, j)

    block = pl.BlockSpec((2, 1, 2, 2, unit_rows, width), lambda r, *_: (0, r, 0, 0, 0, 0))
    part = pl.BlockSpec((1, 2, unit_rows, width), lambda r, *_: (r, 0, 0, 0))
    return pl.pallas_call(
        body,
        grid_spec=pltpu.PrefetchScalarGridSpec(
            num_scalar_prefetch=1, grid=(count,), in_specs=[block] * 2, out_specs=[part] * 4
        ),
        out_shape=[jax.ShapeDtypeStruct((count, 2, unit_rows, width), low)] * 4,
        compiler_params=pltpu.CompilerParams(vmem_limit_bytes=60 * 2**20),
        cost_estimate=costly,
        name="sum_split",
    )(place, kept, got)


def update_slots(master, first_moment, second_moment, filled, which, position, sources):
    capacity, unit_rows, width = master.shape

    group = math.gcd(capacity, 2)
    steps = capacity // group

    def body(filled_ref, which_ref, position_ref, weight, one, two, *rest):
        ins = rest[: len(sources)]
        new_one, new_two, new_weight, held, sems = rest[len(sources) :]
        step = pl.program_id(0)

        def fetch(turn):
            for i in range(group):
                slot = turn * group + i
                for source, ref in enumerate(ins):

                    @pl.when(which_ref[slot] == source)
                    def _():
                        pltpu.make_async_copy(
                            ref.at[position_ref[slot]], held.at[turn % 2, i], sems.at[turn % 2, i]
                        ).start()

        @pl.when(step == 0)
        def _():
            fetch(step)

        @pl.when(step < steps - 1)
        def _():
            fetch(step + 1)

        for i in range(group):
            pltpu.make_async_copy(
                ins[0].at[0], held.at[step % 2, i], sems.at[step % 2, i]
            ).wait()
            mask = (filled_ref[step * group + i] > 0).astype(jnp.float32)
            grad = held[step % 2, i].astype(jnp.float32)
            results = adamw(weight[i], one[i], two[i], grad, mask, rate)
            new_one[i], new_two[i], new_weight[i] = results

    block = pl.BlockSpec((group, unit_rows, width), lambda s, *_: (s, 0, 0))
    return pl.pallas_call(
        body,
        grid_spec=pltpu.PrefetchScalarGridSpec(
            num_scalar_prefetch=3,
            grid=(steps,),
            in_specs=[block] * 3 + [pl.BlockSpec(memory_space=pl.ANY)] * len(sources),
            out_specs=[block] * 3,
            scratch_shapes=[
                pltpu.VMEM((2, group, unit_rows, width), low),
                pltpu.SemaphoreType.DMA((2, group)),
            ],
        ),
        out_shape=[jax.ShapeDtypeStruct(master.shape, jnp.float32)] * 3,
        compiler_params=pltpu.CompilerParams(vmem_limit_bytes=56 * 2**20),
        cost_estimate=cheap,
        name="update_slots",
    )(filled, which, position, master, first_moment, second_moment, *sources)


def adamw(weight, moment_one, moment_two, gradient, filled, step_rate):
    new_one = beta_one * moment_one + (1.0 - beta_one) * gradient
    new_two = beta_two * moment_two + (1.0 - beta_two) * gradient * gradient
    fixed_one = new_one / (1.0 - beta_one**STEP)
    fixed_two = new_two / (1.0 - beta_two**STEP)
    updated = weight - step_rate * (fixed_one / (jnp.sqrt(fixed_two) + adam_eps) + decay * weight)
    return (new_one * filled, new_two * filled, updated * filled)


def swap(values, axis, bit):
    count = lax.axis_size(axis)
    return lax.ppermute(values, axis, [(i, i ^ (1 << bit)) for i in range(count)])


def choose(values, index, axis):
    return lax.dynamic_index_in_dim(values, index, axis, keepdims=False)


def total_sum(values):
    for axis in ("dp", "tensor"):
        for bit in range(lax.axis_size(axis).bit_length() - 1):
            values = values + swap(values, axis, bit)
    return values


def pick_units(master, slot_unit, state, kind, place, sizes, after=()):
    capacity, unit_rows, width = master.shape
    units = state.shape[0]

    def body(slot_ref, state_ref, kind_ref, place_ref, blocks, *rest):
        outs = rest[len(after) : len(after) + len(sizes)]
        highs, lows, zeros, read, sems = rest[len(after) + len(sizes) :]

        def start(source, unit):
            for which, out in enumerate(outs):

                @pl.when(kind_ref[unit] == which)
                def _():
                    pltpu.make_async_copy(source, out.at[place_ref[unit]], sems.at[unit]).start()

        @pl.loop(0, capacity)
        def _(slot):
            @pl.when(slot_ref[slot] >= 0)
            def _():
                pltpu.make_async_copy(blocks.at[slot], highs.at[slot], read.at[slot]).start()

        zeros[...] = jnp.zeros_like(zeros)

        @pl.loop(0, units)
        def _(unit):
            @pl.when(state_ref[unit] == 0)
            def _():
                start(zeros, unit)

        @pl.loop(0, capacity)
        def _(slot):
            @pl.when(slot_ref[slot] >= 0)
            def _():
                pltpu.make_async_copy(blocks.at[slot], highs.at[slot], read.at[slot]).wait()
                lows[slot] = highs[slot].astype(low)
                start(lows.at[slot], slot_ref[slot])

        @pl.loop(0, units)
        def _(unit):
            @pl.when(state_ref[unit] < 2)
            def _():
                pltpu.make_async_copy(zeros, outs[0].at[0], sems.at[unit]).wait()

    return pl.pallas_call(
        body,
        grid_spec=pltpu.PrefetchScalarGridSpec(
            num_scalar_prefetch=4,
            grid=(1,),
            in_specs=[pl.BlockSpec(memory_space=pl.ANY)] * (1 + len(after)),
            out_specs=[pl.BlockSpec(memory_space=pl.ANY)] * len(sizes),
            scratch_shapes=[
                pltpu.VMEM((capacity, unit_rows, width), jnp.float32),
                pltpu.VMEM((capacity, unit_rows, width), low),
                pltpu.VMEM((unit_rows, width), low),
                pltpu.SemaphoreType.DMA((capacity,)),
                pltpu.SemaphoreType.DMA((units,)),
            ],
        ),
        out_shape=[jax.ShapeDtypeStruct((size, unit_rows, width), low) for size in sizes],
        compiler_params=pltpu.CompilerParams(vmem_limit_bytes=56 * 2**20),
        cost_estimate=cheap,
        name="pick_units",
    )(slot_unit, state, kind, place, master, *after)


def place_blocks(sources, which, position, parts=1):
    amount = which.shape[0]
    shape = sources[0].shape[1:]
    size = amount // parts

    def body(which_ref, position_ref, *rest):
        ins, outs = rest[: len(sources)], rest[len(sources) : len(sources) + parts]
        held, read, sems = rest[len(sources) + parts :]

        @pl.loop(0, amount)
        def _(i):
            for source, ref in enumerate(ins):

                @pl.when(which_ref[i] == source)
                def _():
                    pltpu.make_async_copy(ref.at[position_ref[i]], held.at[i], read.at[i]).start()

        for part, out in enumerate(outs):

            @pl.loop(0, size)
            def _(j):
                i = part * size + j
                pltpu.make_async_copy(ins[0].at[0], held.at[i], read.at[i]).wait()
                pltpu.make_async_copy(held.at[i], out.at[j], sems.at[i]).start()

        @pl.loop(0, amount)
        def _(i):
            pltpu.make_async_copy(held.at[i], outs[0].at[0], sems.at[i]).wait()

    return pl.pallas_call(
        body,
        grid_spec=pltpu.PrefetchScalarGridSpec(
            num_scalar_prefetch=2,
            grid=(1,),
            in_specs=[pl.BlockSpec(memory_space=pl.ANY)] * len(sources),
            out_specs=[pl.BlockSpec(memory_space=pl.ANY)] * parts,
            scratch_shapes=[
                pltpu.VMEM((amount,) + shape, low),
                pltpu.SemaphoreType.DMA((amount,)),
                pltpu.SemaphoreType.DMA((amount,)),
            ],
        ),
        out_shape=[jax.ShapeDtypeStruct((size,) + shape, low)] * parts,
        compiler_params=pltpu.CompilerParams(vmem_limit_bytes=56 * 2**20),
        cost_estimate=cheap,
        name="place_blocks",
    )(which, position, *sources)


def stack_pairs(pairs):
    shape = (len(pairs),) + pairs[0].shape[1:]

    def body(*refs):
        for i, pair in enumerate(refs[:-2]):
            for half in range(2):
                refs[half - 2][i] = pair[half]

    return pl.pallas_call(
        body,
        out_shape=[jax.ShapeDtypeStruct(shape, low)] * 2,
        cost_estimate=costly,
        name="stack_pairs",
    )(*pairs)


def hops(values, step, turn):
    count = lax.axis_size("tensor")
    if step > 0:
        pairs = [(i, i + 1) for i in range(turn - 1, count - 1)]
    else:
        pairs = [(i, i - 1) for i in range(1, count - turn + 1)]
    return lax.ppermute(values, "tensor", pairs)


fence = lax.optimization_barrier


def in_pool(member, inner, inner_count):
    me = lax.axis_index("dp")
    half, core = member >> 3, ((member >> 2) & 1) ^ (me & 1)
    far_y, far_x = ((member >> 1) & 1) ^ ((me >> 2) & 1), (member & 1) ^ ((me >> 1) & 1)
    where_first = (far_y * 2 + far_x) * inner_count
    where_second = (4 + far_x * 2 + far_y) * inner_count
    return (core, jnp.where(half == 0, where_first, where_second) + inner)


def on_device(
    hidden_in,
    time_embed,
    caption_table,
    caption_ids,
    owners,
    master,
    first_moment,
    second_moment,
    mod_table,
    mod_first,
    mod_second,
    out_grad,
):
    count = lax.axis_size("tensor")
    dp_count = lax.axis_size("dp")
    me_dp = lax.axis_index("dp")
    me_tensor = lax.axis_index("tensor")
    capacity, unit_rows, width = master.shape
    units = owners.shape[0]
    tokens = hidden_in.shape[1]
    text_count = caption_ids.shape[1]
    share = width // count
    per = share // unit_rows
    ups = (units - 8 * per) // 2
    rank_of = ranks_of(owners)
    mine = owners == me_dp
    match = (rank_of[None, :] == jnp.arange(capacity)[:, None]) & mine[None, :]
    filled = jnp.any(match, axis=1)
    unit_of_slot = jnp.sum(jnp.where(match, jnp.arange(units)[None, :], 0), axis=1)

    square = [list(range(i * per, (i + 1) * per)) for i in range(8)]
    group_attn = square[0] + square[1] + square[2] + square[5]
    group_full = square[3] + square[4] + square[6] + square[7]
    group_mlp = list(range(8 * per, units))
    members = len(group_attn)
    plane = dp_count == 8 and members == 16 and len(group_mlp) % dp_count == 0
    member_of = np.zeros(units, np.int32)
    member_of[group_attn] = np.arange(members)
    member_of[group_full] = np.arange(members)
    is_attn = np.zeros(units, bool)
    is_attn[group_attn] = True
    is_mlp = np.zeros(units, bool)
    is_mlp[group_mlp] = True

    latent_in = hidden_in[0].astype(jnp.float32)
    modulate = mod_table + time_embed[0]

    def mod_row(which_row):
        return modulate[which_row][None, :]

    normed_one, inverse_one = layer_norm(latent_in)
    bits = dp_count.bit_length() - 1
    vocab_rows = caption_table.shape[0]

    def caption_terms(ids):
        chosen = ids.reshape(-1) - me_dp * vocab_rows
        onehot = (chosen[:, None] == jnp.arange(vocab_rows)[None, :]).astype(low)
        terms = jnp.dot(onehot, caption_table, preferred_element_type=jnp.float32).astype(low)
        return terms.reshape(dp_count, text_count, -1)

    def modulated(normed):
        return (normed.astype(jnp.float32) * (1.0 + mod_row(1)) + mod_row(0)).astype(low)

    def whole_text(text_ring):
        return from_ring(text_ring, -1).transpose(1, 0, 2).reshape(text_count, width)

    def own_keys(text_low, w_attn):
        return project(text_low, w_attn)[:, 3 * share :].astype(low)

    def exchanged(attended, keys):
        parts = [
            jnp.concatenate([attended[k * tokens : (k + 1) * tokens], keys]) for k in range(count)
        ]
        return [parts[0]] + [shift(parts[k], count - k) for k in range(1, count)]

    where = jnp.stack([me_tensor, me_dp & 1]).astype(jnp.int32)

    n_low = normed_one.astype(low)
    if plane:
        core, far_x, far_y = (
            ((member_of >> 2) & 1) ^ (me_dp & 1),
            (member_of & 1) ^ ((me_dp >> 1) & 1),
            ((member_of >> 1) & 1) ^ ((me_dp >> 2) & 1),
        )
        place = jnp.where(is_attn, far_x * 4 + far_y * 2, 8 + far_y * 4 + far_x * 2)
        place = jnp.where(is_mlp, np.arange(units) - 8 * per, place + (member_of >> 3))
        kind = jnp.where(is_mlp, 0, core)
        slot_mlp = unit_of_slot >= 8 * per
        owned_state = mine.astype(jnp.int32)
        ids = lax.all_gather(caption_ids, "dp", axis=0, tiled=True)
        ids = jnp.take(ids, me_dp ^ jnp.arange(dp_count), axis=0, mode="clip")
        up, down = hops(n_low, 1, 1), hops(n_low, -1, 1)
        kept, given = pick_units(
            master,
            jnp.where(filled & ~slot_mlp, unit_of_slot, -1),
            jnp.where(is_mlp, 2, owned_state),
            kind,
            place,
            (members, members),
        )
        got = swap(given, "dp", 0)
        (mlp_part,) = pick_units(
            master,
            jnp.where(filled & slot_mlp, unit_of_slot, -1),
            jnp.where(is_mlp, owned_state, 2),
            kind,
            place,
            (len(group_mlp),),
            (kept,),
        )
        mlp_part = lax.psum_scatter(mlp_part, "dp", scatter_dimension=0, tiled=True)
        n_up, n_down = [up], [down]
        kept, got, up, down, ids = fence((kept, got, up, down, ids))
        pieces = [kept[i : i + 4] + got[i : i + 4] for i in range(0, members, 4)]
        attn_two, attn_send, full_two, full_send = fence(tuple(pieces))
        up, down = hops(up, 1, 2), hops(down, -1, 2)
        attn_got = swap(attn_send, "dp", 1)
        full_got = swap(full_send, "dp", 2)
        text = caption_terms(ids)
        text = text[0:4] + swap(text[4:8], "dp", 2)
        n_up.append(up), n_down.append(down)
        attn_two, attn_got, full_two, full_got, up, down, text = fence(
            (attn_two, attn_got, full_two, full_got, up, down, text)
        )
        pieces = [x[i : i + 2] + y[i : i + 2] for x, y in ((attn_two, attn_got), (full_two, full_got)) for i in (0, 2)]
        attn_one, attn_send, full_one, full_send = fence(tuple(pieces))
        up, down = hops(up, 1, 3), hops(down, -1, 3)
        attn_got = swap(attn_send, "dp", 2)
        full_got = swap(full_send, "dp", 1)
        text = text[0:2] + swap(text[2:4], "dp", 1)
        n_up.append(up), n_down.append(down)
        attn_one, attn_got, full_one, full_got, up, down, text, mlp_part = fence(
            (attn_one, attn_got, full_one, full_got, up, down, text, mlp_part)
        )
        attn_one, full_one = attn_one + attn_got, full_one + full_got
        n_up[-1], n_down[-1] = up, down
        w_mlp = lax.all_gather(mlp_part, "dp", axis=0, tiled=True)
        first_ring, second_ring = stack_pairs(ring(full_one))
        first = jnp.concatenate([attn_one[0:1], swap(attn_one[0:1], "dp", 1)])
        second = jnp.concatenate([attn_one[1:2], swap(attn_one[1:2], "dp", 2)])
        pool = jnp.concatenate([first, swap(first, "dp", 2), second, swap(second, "dp", 1)])
        other = swap(pool, "dp", 0)
        text = text[0] + swap(text[1], "dp", 0)
        *n_slots, h_one_all = line_slots(
            where, n_low, n_up, n_down, jnp.concatenate([mod_row(0), mod_row(1)])
        )
        n_slots = [n_low] + n_slots
        grad_own = out_grad[0]
        pool, other, first_ring, second_ring, h_one_all, text, grad_own = fence(
            (pool, other, first_ring, second_ring, h_one_all, text, grad_own)
        )
        grad_whole = lax.all_gather(grad_own, "tensor", axis=0)
        first, second = first_ring, second_ring
        first_got = swap(first, "dp", 1)
        second_got = swap(second, "dp", 2)
        text_ring = ring(text)
        (w_attn,) = place_blocks((pool, other), *in_pool(np.arange(members), 0, 1))
        w_attn = w_attn.reshape(-1, width)
        qkv = project(h_one_all, w_attn).astype(low)
        attended, logs = self_attend(qkv, share)
        first = jnp.concatenate([first, first_got])
        second = jnp.concatenate([second, second_got])
        first, second, text_ring, attended, logs, w_attn, w_mlp = fence(
            (first, second, text_ring, attended, logs, w_attn, w_mlp)
        )
        first_far, second_far = swap(first, "dp", 2), swap(second, "dp", 1)
        text_low = whole_text(jnp.stack(text_ring))
        mixed = exchanged(attended, own_keys(text_low, w_attn))
        first_far, second_far, mixed = fence((first_far, second_far, mixed))
        first_other, second_other = swap(first, "dp", 0), swap(second, "dp", 0)
        first_last, second_last = swap(first_far, "dp", 0), swap(second_far, "dp", 0)
        listing = np.arange(count * members)
        matrix, rank, head = listing // (count * per), listing // per % count, listing % per
        slot = lax.rem(me_tensor - rank + count, count)
        which, position = in_pool(matrix * per + head, slot, count)
        blocks = 2 * count
        w_full = place_blocks(
            (first, first_far, second, second_far, first_other, first_last, second_other, second_last),
            which * 4 + position // blocks,
            position % blocks,
            parts=4,
        )
        w_full = [part.reshape(width, width) for part in w_full]
        w_full[3], grad_whole = fence((w_full[3], grad_whole))
    else:
        slots_low = master.astype(low)
        rows = jnp.take(slots_low, rank_of, axis=0, mode="clip")
        rows = lax.psum(jnp.where(mine[:, None, None], rows, jnp.zeros((), low)), "dp")
        w_attn = rows[np.array(group_attn)].reshape(-1, width)
        w_full = lax.all_gather(rows[np.array(group_full)], "tensor", axis=0)
        w_full = w_full.reshape(count, 4, share, width).swapaxes(0, 1).reshape(4, width, width)
        w_full = [w_full[i] for i in range(4)]
        w_mlp = rows[8 * per :]
        n_slots = ring(n_low)
        normed_all = jnp.concatenate(n_slots)
        grad_whole = lax.all_gather(out_grad[0], "tensor", axis=0)
        ids = caption_ids
        for bit in range(bits):
            ids = jnp.concatenate([ids, swap(ids, "dp", bit)])
        text = caption_terms(ids)
        for bit in reversed(range(bits)):
            text = text[: 1 << bit] + swap(text[1 << bit :], "dp", bit)
        text_low = whole_text(jnp.stack(ring(text[0])))
        h_one_all = modulated(normed_all)
        qkv = project(h_one_all, w_attn).astype(low)
        attended, logs = self_attend(qkv, share)
        mixed = exchanged(attended, own_keys(text_low, w_attn))
    w_cross = w_full
    w_out, c_query, c_value, c_out = w_full
    w_mlp = w_mlp.reshape(-1, width)

    rows = jnp.concatenate([mod_row(2), mod_row(3), mod_row(4)])
    (
        branch_one,
        first_low,
        cq_rows,
        ck_rows,
        cv_rows,
        crossed,
        second_res,
        normed_two,
        h_two,
        inverse_two,
    ) = cross_block(
        where, mixed, hidden_in[0], rows, text_low, *w_cross
    )

    h_slots = {0: h_two}
    out_slots = [
        choose(grad_whole, lax.rem(me_tensor - k + count, count), 0) for k in range(count)
    ]
    grad_slots = [(mod_row(5) * item.astype(jnp.float32)).astype(low) for item in out_slots]
    near = [k for k in range(1, count) if 2 * k != count]
    far = [k for k in range(1, count) if 2 * k == count]
    acts, grad_pres, grad_terms, order = [], [], [], []
    for k in near:
        h_slots[k] = shift(h_two, k)
    for members_now in ([0], near, far):
        act, grad_pre, *terms = mlp_core(
            [h_slots[k] for k in members_now],
            [grad_slots[k] for k in members_now],
            w_mlp,
            acts[-1:],
        )
        if members_now == [0]:
            h_two, act = fence((h_two, act))
            for k in far:
                h_slots[k] = shift(h_two, k)
        acts.append(act), grad_pres.append(grad_pre)
        order += members_now
        grad_terms += [
            shift(term, count - k) if k else term for k, term in zip(members_now, terms)
        ]
    mlp_grad = mlp_grads(
        grad_pres, acts, [h_slots[k] for k in order], [grad_slots[k] for k in order]
    ).reshape(-1, unit_rows, width)
    hidden_share = w_mlp.shape[0] // 2
    pieces = [
        [(which, row, 0, hidden_share, hidden_share)]
        for which, act in enumerate(acts)
        for row in range(0, act.shape[0], tokens)
    ]
    branch_terms, branch_sums = ranked_terms(
        where, acts, order, pieces, w_mlp, [out_slots[k] for k in order], "mlp_out"
    )
    branch_row = branch_sums[1]
    grad_terms, branch_terms = fence((grad_terms, branch_terms))
    if plane:
        mlp_sum = lax.psum_scatter(mlp_grad, "dp", scatter_dimension=0, tiled=True)

    (
        first_grad,
        cross_low,
        grad_cq,
        attn_low,
        grad_cv,
        row_sums,
        *grad_mixed,
    ) = cross_back(
        where,
        grad_terms,
        out_grad[0],
        rows,
        normed_two,
        inverse_two,
        branch_one,
        cq_rows,
        ck_rows,
        cv_rows,
        c_out,
        c_query,
        w_out,
        (mlp_grad,),
    )

    grad_parts = [grad_mixed[0]] + [shift(grad_mixed[k], k) for k in range(1, count)]
    full_pairs = [
        ([(item, 0, share, None) for item in mixed], attn_low),
        ([(grad_cq, 0, width, 0)], first_low),
        ([(grad_cv, 0, width, 0)], text_low),
        ([(crossed, 0, width, 0)], cross_low),
    ]
    half = (share // HEAD_DIM // 2) * HEAD_DIM
    spans = [(0, half), (half, share)]

    def attention_pairs(grads, grad_parts):
        keys = sum(item[tokens:].astype(jnp.float32) for item in grad_parts).astype(low)
        pairs = [
            (
                [
                    (item, i * (end - begin), end - begin, begin)
                    for item, (begin, end) in zip(grads, spans)
                ],
                h_one_all,
            )
            for i in range(3)
        ]
        return pairs + [([(keys, 0, share, 0)], text_low)]

    def input_terms(grads):
        pieces = [
            [
                (which, slot * tokens, i * (end - begin), i * share + begin, end - begin)
                for which, (begin, end) in enumerate(spans)
                for i in range(3)
            ]
            for slot in range(count)
        ]
        return ranked_terms(where, grads, range(count), pieces, w_attn, n_slots, "attn_terms")

    if plane:
        x_bit, y_bit = (me_dp >> 1) & 1, (me_dp >> 2) & 1

        def split(total, bit, axis):
            return (choose(total, bit, axis), choose(total, 1 - bit, axis))

        kept, given = outer_halves(where, full_pairs, count, "full_grads")
        got = swap(given, "dp", 0)
        grad_parts, kept, got, branch_terms = fence((grad_parts, kept, got, branch_terms))
        branch_two = lax.psum_scatter(
            branch_terms.reshape(-1, width), "tensor", scatter_dimension=0, tiled=True
        )
        box = (2, count, 2, 2, unit_rows, width)
        bits_here = jnp.stack([x_bit, y_bit]).astype(jnp.int32)
        kept_one, given_one, kept_two, given_two = sum_split(
            bits_here, kept.reshape(box), got.reshape(box)
        )
        got_one, got_two = swap(given_one, "dp", 1), swap(given_two, "dp", 2)
        grads_early = self_attend_back(qkv, grad_parts, attended, logs, share, *spans[0])
        kept_one, got_one, kept_two, got_two, grads_early, grad_parts = fence(
            (kept_one, got_one, kept_two, got_two, grads_early, grad_parts)
        )
        kept_one, given_one = split(kept_one + got_one, y_bit, 1)
        kept_two, given_two = split(kept_two + got_two, x_bit, 1)
        kept_one, given_one, kept_two, given_two, grad_parts = fence(
            (kept_one, given_one, kept_two, given_two, grad_parts)
        )
        got_one, got_two = swap(given_one, "dp", 2), swap(given_two, "dp", 1)
        grads_late = self_attend_back(qkv, grad_parts, attended, logs, share, *spans[1])
        kept_one, got_one, kept_two, got_two, grads_early, grads_late, mlp_sum = fence(
            (kept_one, got_one, kept_two, got_two, grads_early, grads_late, mlp_sum)
        )
        mlp_sum = lax.all_gather(mlp_sum, "dp", axis=0, tiled=True)
        full_parts = to_ring(jnp.stack([kept_one + got_one, kept_two + got_two], axis=1))
        full_parts = [full_parts[k] for k in range(count)]
        full_parts, grads_early, grads_late = fence((full_parts, grads_early, grads_late))
        grads_qkv = [grads_early, grads_late]
        full_got = [shift(full_parts[k], k) for k in range(1, count)]
        attn_kept, attn_given = outer_halves(
            where, attention_pairs(grads_qkv, grad_parts), 1, "attn_grads"
        )
        attn_got = swap(attn_given, "dp", 0)
        grad_h_terms, grad_h_sums = input_terms(grads_qkv)
        mod_terms = jnp.concatenate([grad_h_sums, row_sums, branch_row[None]])
        grad_h_one = lax.psum_scatter(
            grad_h_terms.reshape(-1, width), "tensor", scatter_dimension=0, tiled=True
        )
        attn_kept, attn_got, mod_terms, branch_two = fence(
            (attn_kept, attn_got, mod_terms, branch_two)
        )
        attn_all = (attn_kept + attn_got).reshape(2, 2, 2, unit_rows, width)
        one_kept, one_given = split(attn_all[0], x_bit, 1)
        two_kept, two_given = split(attn_all[1], y_bit, 0)
        one_got, two_got = swap(one_given, "dp", 1), swap(two_given, "dp", 2)
        mod_terms = mod_terms + swap(mod_terms, "dp", 0)
        full_own = full_parts[0]
        one_kept, one_got, two_kept, two_got, mod_terms, full_own, full_got = fence(
            (one_kept, one_got, two_kept, two_got, mod_terms, full_own, full_got)
        )
        full_sum = full_own.astype(jnp.float32)
        for part in full_got:
            full_sum = full_sum + part.astype(jnp.float32)
        full_sum = full_sum.astype(low)
        one_kept, one_given = split(one_kept + one_got, y_bit, 0)
        two_kept, two_given = split(two_kept + two_got, x_bit, 0)
        one_got, two_got = swap(one_given, "dp", 2), swap(two_given, "dp", 1)
        mod_terms = mod_terms + swap(mod_terms, "dp", 1)
        one_kept, one_got, two_kept, two_got, full_sum, mod_terms, mlp_sum = fence(
            (one_kept, one_got, two_kept, two_got, full_sum, mod_terms, mlp_sum)
        )
        first = jnp.stack([one_kept + one_got, full_sum[0]])
        second = jnp.stack([two_kept + two_got, full_sum[1]])
        first_got, second_got = swap(first, "dp", 1), swap(second, "dp", 2)
        first = jnp.concatenate([first, first_got])
        second = jnp.concatenate([second, second_got])
        mod_terms = mod_terms + swap(mod_terms, "dp", 2)
        first, second, mod_terms = fence((first, second, mod_terms))
        first_far, second_far = swap(first, "dp", 2), swap(second, "dp", 1)
        mod_terms = mod_terms + swap(mod_terms, "tensor", 0)
        first, first_far, second, second_far, mod_terms = fence(
            (first, first_far, second, second_far, mod_terms)
        )
        pool = jnp.concatenate([first, first_far, second, second_far])
        other = swap(pool, "dp", 0)
        for bit in range(1, count.bit_length() - 1):
            mod_terms = mod_terms + swap(mod_terms, "tensor", bit)
        pool, other, mod_grad = fence((pool, other, mod_terms))
        which, position = in_pool(member_of, np.where(is_attn, 0, 1), 2)
        which = jnp.where(is_mlp, 2, which)
        position = jnp.where(is_mlp, np.arange(units) - 8 * per, position)
        own = jnp.sum(jnp.where(match[:, :, None], jnp.stack([which, position], 1)[None], 0), axis=1)
        new_first, new_second, new_master = update_slots(
            master,
            first_moment,
            second_moment,
            filled.astype(jnp.int32),
            own[:, 0],
            own[:, 1],
            (pool, other, mlp_sum),
        )
    else:
        branch_two = lax.psum_scatter(
            branch_terms.reshape(-1, width), "tensor", scatter_dimension=0, tiled=True
        )
        grads_qkv = [self_attend_back(qkv, grad_parts, attended, logs, share, *span) for span in spans]
        attn_grads = [
            outer(array[:, lane : lane + lanes], right).astype(low)
            for left, right in attention_pairs(grads_qkv, grad_parts)
            for array, lane, lanes, row in left
        ]
        grad_h_terms, grad_h_sums = input_terms(grads_qkv)
        grad_h_one = lax.psum_scatter(
            grad_h_terms.reshape(-1, width), "tensor", scatter_dimension=0, tiled=True
        )
        mixed_all = from_ring(jnp.stack([item[:tokens] for item in mixed]), 1)
        mixed_all = mixed_all.transpose(1, 0, 2).reshape(tokens, width)
        full_grads = [outer(mixed_all, attn_low)]
        full_grads += [outer(left[0][0], right) for left, right in full_pairs[1:]]
        full_sum = [g.astype(low).reshape(count, share, width) for g in full_grads]
        full_sum = jnp.stack(full_sum, axis=1)
        full_sum = lax.psum_scatter(full_sum, "tensor", scatter_dimension=0, tiled=True)
        order = np.array(group_attn + group_full + group_mlp)
        sums = jnp.concatenate(
            [jnp.concatenate(attn_grads), full_sum.reshape(-1, width), mlp_grad.reshape(-1, width)]
        )
        sums = lax.psum(sums.reshape(units, unit_rows, width), "dp")
        owned = jnp.take(sums, jnp.array(np.argsort(order))[unit_of_slot], axis=0, mode="clip")
        mod_grad = total_sum(jnp.concatenate([grad_h_sums, row_sums, branch_row[None]]))
        new_first, new_second, new_master = adamw(
            master,
            first_moment,
            second_moment,
            owned.astype(jnp.float32),
            filled.astype(jnp.float32)[:, None, None],
            rate,
        )
    branch_two, second_res, grad_h_one, new_first = fence(
        (branch_two, second_res, grad_h_one, new_first)
    )
    grad_h_one = grad_h_one.astype(jnp.float32)
    block_out = second_res + mod_row(5) * branch_two.astype(jnp.float32)
    input_grad = first_grad + norm_back(grad_h_one, normed_one, inverse_one, mod_row(1))
    mod_new_first, mod_new_second, mod_new = adamw(
        mod_table, mod_first, mod_second, mod_grad, 1.0, table_rate
    )
    return (
        block_out[None],
        input_grad[None],
        new_first,
        new_second,
        new_master,
        mod_new_first,
        mod_new_second,
        mod_new,
    )


def solution(mesh):
    in_specs = (
        P("dp", "tensor", None),
        P("dp", None, None),
        P("dp", "tensor"),
        P("dp", None),
        P(),
        P("dp", "tensor", None),
        P("dp", "tensor", None),
        P("dp", "tensor", None),
        P(),
        P(),
        P(),
        P("dp", "tensor", None),
    )
    out_specs = (
        P("dp", "tensor", None),
        P("dp", "tensor", None),
        P("dp", "tensor", None),
        P("dp", "tensor", None),
        P("dp", "tensor", None),
        P(),
        P(),
        P(),
    )
    return jax.shard_map(
        on_device, mesh=mesh, in_specs=in_specs, out_specs=out_specs, check_vma=False
    )
```

profile of v0, /device:TPU:0, one launch (start us, length us, event | category | flops | bytes accessed | tf_op | source)
XLA Modules:
  0.0 614.5 jit_solution(11021954595635931741)
XLA Ops:
  12.1 4.2 pick_units.2
  16.3 4.4 pick_units.3
  23.9 6.4 %collective-permute-start.1 = (bf16[256,1152]{1,0:T(8,128)(2,1)S(1)}, bf16[256,1152]{1,0:T(8,128)(2,1)}, u32[]{:S(2)}, u32[]{:S(2)}) collective-permute-start(bf16[256,1152]{1,0:T(8,128)(2,1)S(1)} %fusion.6.refs_0_.refs_3_), channel_id=1, source_target_pairs={{0,1},{1,2},{2,3},{4,5},{5,6},{6,7},{8,9},{9,10},{10,11},{12,13},{... | collective-permute-start | bytes 1769480 | tf_op jit(solution)/shard_map/ppermute | solution.py:929
  30.4 9.5 %all-gather.1 = s32[8,1,120]{2,1,0:T(1,128)S(1)} all-gather(s32[1,1,120]{2,1,0:T(1,128)S(1)} %bitcast.151), channel_id=1, replica_groups=mesh['dp'=8,'tensor'=4] {'dp'}, dimensions={0}, use_global_device_ids=true | all-gather | bytes 4320 | tf_op jit(solution)/shard_map/all_gather | solution.py:1034
  42.1 4.1 slice_add_fusion
  56.9 29.2 %collective-permute-done.7 = bf16[4,120,288]{1,2,0:T(8,128)(2,1)S(1)} collective-permute-done((bf16[4,120,288]{1,2,0:T(8,128)(2,1)S(1)}, bf16[4,120,288]{1,2,0:T(8,128)(2,1)S(1)}, u32[]{:S(2)}, u32[]{:S(2)}) %collective-permute-start.7) | collective-permute-done | bytes 276512 | tf_op jit(solution)/shard_map/ppermute | solution.py:779
  93.6 6.8 %collective-permute-done.8 = bf16[2,72,1152]{2,1,0:T(8,128)(2,1)S(1)} collective-permute-done((bf16[2,72,1152]{2,1,0:T(8,128)(2,1)S(1)}, bf16[2,72,1152]{2,1,0:T(8,128)(2,1)S(1)}, u32[]{:S(2)}, u32[]{:S(2)}) %collective-permute-start.8) | collective-permute-done | bytes 331808 | tf_op jit(solution)/shard_map/ppermute | solution.py:779
  100.5 3.9 collective-permute-done.11.refs_6_
  114.8 8.5 %collective-permute-done.15 = bf16[1,72,1152]{2,1,0:T(8,128)(2,1)S(1)} collective-permute-done((bf16[1,72,1152]{2,1,0:T(8,128)(2,1)S(1)}, bf16[1,72,1152]{2,1,0:T(8,128)(2,1)S(1)}, u32[]{:S(2)}, u32[]{:S(2)}) %collective-permute-start.15) | collective-permute-done | bytes 165920 | tf_op jit(solution)/shard_map/ppermute | solution.py:779
  125.6 3.9 collective-permute-done.14
  149.4 3.7 place_blocks.2
  153.1 5.5 convolution_convert_fusion.qkv_ref
  159.6 8.3 %self_attend.1 = (bf16[1024,288]{1,0:T(8,128)(2,1)S(1)}, f32[4,1024]{1,0:T(4,128)S(1)}) custom-call(bf16[1024,1152]{1,0:T(8,128)(2,1)S(1)} %convolution_convert_fusion.qkv_ref), custom_call_target="tpu_custom_call" | custom-call | flops 1000 | bytes 1000 | tf_op jit(solution)/shard_map/self_attend/pallas_call | solution.py:106
  185.0 13.4 %collective-permute-done.31.refs_3_ = bf16[376,288]{1,0:T(8,128)(2,1)} collective-permute-done((bf16[376,288]{1,0:T(8,128)(2,1)S(1)}, bf16[376,288]{1,0:T(8,128)(2,1)}, u32[]{:S(2)}, u32[]{:S(2)}) %collective-permute-start.31) | collective-permute-done | bytes 216608 | tf_op jit(solution)/shard_map/ppermute | solution.py:58
  198.4 10.6 %collective-permute-done.29.refs_1_ = bf16[376,288]{1,0:T(8,128)(2,1)} collective-permute-done((bf16[376,288]{1,0:T(8,128)(2,1)S(1)}, bf16[376,288]{1,0:T(8,128)(2,1)}, u32[]{:S(2)}, u32[]{:S(2)}) %collective-permute-start.29) | collective-permute-done | bytes 216608 | tf_op jit(solution)/shard_map/ppermute | solution.py:58
  209.0 19.8 %collective-permute-done.30.refs_2_ = bf16[376,288]{1,0:T(8,128)(2,1)} collective-permute-done((bf16[376,288]{1,0:T(8,128)(2,1)S(1)}, bf16[376,288]{1,0:T(8,128)(2,1)}, u32[]{:S(2)}, u32[]{:S(2)}) %collective-permute-start.30) | collective-permute-done | bytes 216608 | tf_op jit(solution)/shard_map/ppermute | solution.py:58
  234.1 9.7 %place_blocks.3 = (bf16[16,72,1152]{2,1,0:T(8,128)(2,1)}, bf16[16,72,1152]{2,1,0:T(8,128)(2,1)}, bf16[16,72,1152]{2,1,0:T(8,128)(2,1)}, bf16[16,72,1152]{2,1,0:T(8,128)(2,1)}) custom-call(s32[64]{0:T(128)} %multiply_add_fusion.1.which_ref, s32[64]{0:T(128)} %get-tuple-element.405.position_ref, bf16[8,72,1152]{2,1,0:T(8,128)(2,1)} %pad_maximum_fusion.rest_0_, ...), custom_call_target="tpu_custom_call" | custom-call | flops 1000 | bytes 1000 | tf_op jit(solution)/shard_map/place_blocks/pallas_call | solution.py:887
  243.9 13.2 %cross_block.1 = (f32[256,1152]{1,0:T(8,128)}, bf16[256,1152]{1,0:T(8,128)(2,1)}, bf16[256,1152]{1,0:T(8,128)(2,1)}, bf16[120,1152]{1,0:T(8,128)(2,1)}, bf16[120...) custom-call(s32[2]{0:T(128)} %copy-done.10, ...), custom_call_target="tpu_custom_call" | custom-call | flops 1000 | bytes 1000 | tf_op jit(solution)/shard_map/cross_block/pallas_call | solution.py:377
  259.6 3.8 multiply_convert_fusion
  263.4 7.1 %mlp_core.3 = (bf16[256,1152]{1,0:T(8,128)(2,1)}, bf16[256,1152]{1,0:T(8,128)(2,1)}, bf16[256,1152]{1,0:T(8,128)(2,1)}) custom-call(bf16[256,1152]{1,0:T(8,128)(2,1)} %get-tuple-element.268.refs_0_.refs_6_, bf16[256,1152]{1,0:T(8,128)(2,1)} %get-tuple-element.417.refs_1_.refs_10_, bf16[2304,1152]{1,0:T(8,128)(2,1)} %bitcast.117, bf16[2304,1152]{1,0:T(8,128)(2,1)} %bitcast.118), custom_call_target="tpu_custom_call" | custom-call | flops 1000 | bytes 1000 | tf_op jit(solution)/shard_map/mlp_core/pallas_call | solution.py:212
  270.6 15.0 %collective-permute-done.37.refs_1_.refs_8_ = bf16[256,1152]{1,0:T(8,128)(2,1)} collective-permute-done((bf16[256,1152]{1,0:T(8,128)(2,1)}, bf16[256,1152]{1,0:T(8,128)(2,1)}, u32[]{:S(2)}, u32[]{:S(2)}) %collective-permute-start.37) | collective-permute-done | bytes 589856 | tf_op jit(solution)/shard_map/ppermute | solution.py:58
  285.6 11.8 %mlp_core.4 = (bf16[512,1152]{1,0:T(8,128)(2,1)}, bf16[512,1152]{1,0:T(8,128)(2,1)}, bf16[256,1152]{1,0:T(8,128)(2,1)}, bf16[256,1152]{1,0:T(8,128)(2,1)}) custom-call(bf16[256,1152]{1,0:T(8,128)(2,1)} %collective-permute-done.36.refs_0_.refs_7_, bf16[256,1152]{1,0:T(8,128)(2,1)} %collective-permute-done.37.refs_1_.refs_8_, ...), custom_call_target="tpu_custom_call" | custom-call | flops 1000 | bytes 1000 | tf_op jit(solution)/shard_map/mlp_core/pallas_call | solution.py:212
  297.4 12.5 %collective-permute-done.40.refs_0_.refs_9_ = bf16[256,1152]{1,0:T(8,128)(2,1)} collective-permute-done((bf16[256,1152]{1,0:T(8,128)(2,1)}, bf16[256,1152]{1,0:T(8,128)(2,1)}, u32[]{:S(2)}, u32[]{:S(2)}) %collective-permute-start.40) | collective-permute-done | bytes 589856 | tf_op jit(solution)/shard_map/ppermute | solution.py:58
  309.9 7.1 %mlp_core.5 = (bf16[256,1152]{1,0:T(8,128)(2,1)}, bf16[256,1152]{1,0:T(8,128)(2,1)}, bf16[256,1152]{1,0:T(8,128)(2,1)}) custom-call(bf16[256,1152]{1,0:T(8,128)(2,1)} %collective-permute-done.40.refs_0_.refs_9_, bf16[256,1152]{1,0:T(8,128)(2,1)} %get-tuple-element.397.refs_1_.refs_13_, bf16[2304,1152]{1,0:T(8,128)(2,1)} %bitcast.121, ...), custom_call_target="tpu_custom_call" | custom-call | flops 1000 | bytes 1000 | tf_op jit(solution)/shard_map/mlp_core/pallas_call | solution.py:212
  317.0 12.3 %mlp_grads.1 = bf16[2304,1152]{1,0:T(8,128)(2,1)} custom-call(bf16[256,1152]{1,0:T(8,128)(2,1)} %get-tuple-element.283.refs_0_, bf16[512,1152]{1,0:T(8,128)(2,1)} %get-tuple-element.284.refs_1_, bf16[256,1152]{1,0:T(8,128)(2,1)} %get-tuple-element.285.refs_2_, bf16[256,1152]{1,0:T(8,128)(2,1)} %get-tuple-element.265.refs_6_.refs_0_.refs_3_, ...), custom_call_target="tpu_custom_call" | custom-call | flops 1000 | bytes 1000 | tf_op jit(solution)/shard_map/mlp_grads/pallas_call | solution.py:630
  329.3 3.5 collective-permute-start.38
  333.7 9.8 %mlp_out.1 = (bf16[4,256,1152]{2,1,0:T(8,128)(2,1)}, f32[2,1152]{1,0:T(2,128)}) custom-call(s32[2]{0:T(128)} %copy-done.10, bf16[256,1152]{1,0:T(8,128)(2,1)} %get-tuple-element.265.refs_6_.refs_0_.refs_3_, bf16[512,1152]{1,0:T(8,128)(2,1)} %get-tuple-element.269.refs_4_.refs_1_, bf16[256,1152]{1,0:T(8,128)(2,1)} %get-tuple-element.271.refs_2_.refs_5_, ...), custom_call_target="tpu_custom_call" | custom-call | flops 1000 | bytes 1000 | tf_op jit(solution)/shard_map/mlp_out/pallas_call | solution.py:667
  343.5 3.5 collective-permute-done.38.refs_1_
  347.0 13.1 %collective-permute-done.39.refs_2_ = bf16[256,1152]{1,0:T(8,128)(2,1)} collective-permute-done((bf16[256,1152]{1,0:T(8,128)(2,1)}, bf16[256,1152]{1,0:T(8,128)(2,1)}, u32[]{:S(2)}, u32[]{:S(2)}) %collective-permute-start.39) | collective-permute-done | bytes 589856 | tf_op jit(solution)/shard_map/ppermute | solution.py:58
  360.1 22.9 %collective-permute-done.41.refs_3_ = bf16[256,1152]{1,0:T(8,128)(2,1)} collective-permute-done((bf16[256,1152]{1,0:T(8,128)(2,1)}, bf16[256,1152]{1,0:T(8,128)(2,1)}, u32[]{:S(2)}, u32[]{:S(2)}) %collective-permute-start.41) | collective-permute-done | bytes 589856 | tf_op jit(solution)/shard_map/ppermute | solution.py:58
  383.0 14.3 %cross_back.1 = (f32[256,1152]{1,0:T(8,128)}, bf16[256,1152]{1,0:T(8,128)(2,1)}, bf16[256,1152]{1,0:T(8,128)(2,1)}, bf16[256,1152]{1,0:T(8,128)(2,1)}, bf16[120,...) custom-call(s32[2]{0:T(128)} %copy-done.10, ...), custom_call_target="tpu_custom_call" | custom-call | flops 10000000000 | bytes 10000000 | tf_op jit(solution)/shard_map/cross_back/pallas_call | solution.py:497
  397.3 7.1 %full_grads.1 = (bf16[2,4,288,1152]{3,2,1,0:T(8,128)(2,1)}, bf16[2,4,288,1152]{3,2,1,0:T(8,128)(2,1)}) custom-call(s32[2]{0:T(128)} %copy-done.10, bf16[376,288]{1,0:T(8,128)(2,1)} %get-tuple-element.248.refs_0_, bf16[376,288]{1,0:T(8,128)(2,1)} %collective-permute-done.29.refs_1_, bf16[376,288]{1,0:T(8,128)(2,1)} %collective-permute-done.30.refs_2_, ...), custom_call_target="tpu_custom_call" | custom-call | flops 1000 | bytes 1000 | tf_op jit(solution)/shard_map/full_grads/pallas_call | solution.py:580
  408.4 7.9 %collective-permute-done.42.refs_1_ = bf16[376,288]{1,0:T(8,128)(2,1)S(1)} collective-permute-done((bf16[376,288]{1,0:T(8,128)(2,1)}, bf16[376,288]{1,0:T(8,128)(2,1)S(1)}, u32[]{:S(2)}, u32[]{:S(2)}) %collective-permute-start.42) | collective-permute-done | bytes 216608 | tf_op jit(solution)/shard_map/ppermute | solution.py:58
  417.1 10.8 %collective-permute-done.43.refs_2_ = bf16[376,288]{1,0:T(8,128)(2,1)S(1)} collective-permute-done((bf16[376,288]{1,0:T(8,128)(2,1)S(1)}, bf16[376,288]{1,0:T(8,128)(2,1)S(1)}, u32[]{:S(2)}, u32[]{:S(2)}) %collective-permute-start.43) | collective-permute-done | bytes 216608 | tf_op jit(solution)/shard_map/ppermute | solution.py:58
  430.0 7.6 %sum_split.1 = (bf16[4,2,72,1152]{3,2,1,0:T(8,128)(2,1)}, bf16[4,2,72,1152]{3,2,1,0:T(8,128)(2,1)}, bf16[4,2,72,1152]{3,2,1,0:T(8,128)(2,1)}, bf16[4,2,72,1152]{3,2,1,0:T(8,128)(2,1)}) custom-call(s32[2]{0:T(128)} %pad_add_fusion.2.place_ref, bf16[2,4,2,2,72,1152]{5,4,3,2,1,0:T(8,128)(2,1)} %bitcast.152, bf16[2,4,2,2,72,1152]{5,4,3,2,1,0:T(8,128)(2,1)} %bitcast.32.two), custom_call_target="tpu_custom_call" | custom-call | flops 10000000000 | bytes 10000000 | tf_op jit(solution)/shard_map/sum_split/pallas_call | solution.py:697
  443.6 5.8 self_attend_back.2.refs_0_
  449.3 18.8 %collective-permute-done.46 = bf16[4,2,72,1152]{3,2,1,0:T(8,128)(2,1)} collective-permute-done((bf16[4,2,72,1152]{3,2,1,0:T(8,128)(2,1)}, bf16[4,2,72,1152]{3,2,1,0:T(8,128)(2,1)}, u32[]{:S(2)}, u32[]{:S(2)}) %collective-permute-start.46) | collective-permute-done | bytes 1327136 | tf_op jit(solution)/shard_map/ppermute | solution.py:779
  477.0 6.0 self_attend_back.3.refs_1_
  484.0 5.7 collective-permute-done.48
  496.9 6.2 %attn_grads.1 = (bf16[2,1,288,1152]{3,2,1,0:T(8,128)(2,1)}, bf16[2,1,288,1152]{3,2,1,0:T(8,128)(2,1)}) custom-call(s32[2]{0:T(128)} %copy-done.10, bf16[1024,432]{1,0:T(8,128)(2,1)} %copy-done.16, bf16[1024,432]{1,0:T(8,128)(2,1)} %copy-done.17, bf16[1024,1152]{1,0:T(8,128)(2,1)} %copy-done.11, bf16[120,288]{1,0:T(8,128)(2,1)} %add_convert_fusion.1.refs_3_, ...), custom_call_target="tpu_custom_call" | custom-call | flops 10000000000 | bytes 10000000 | tf_op jit(solution)/shard_map/attn_grads/pallas_call | solution.py:580
  503.2 7.2 %collective-permute-start.54 = (bf16[2,72,1152]{2,1,0:T(8,128)(2,1)}, bf16[2,72,1152]{2,1,0:T(8,128)(2,1)S(1)}, u32[]{:S(2)}, u32[]{:S(2)}) collective-permute-start(bf16[2,72,1152]{2,1,0:T(8,128)(2,1)} %get-tuple-element.351), channel_id=1, source_target_pairs={{0,1},{1,2},{2,3},{3,0},{4,5},{5,6},{6,7},{7,4},{8,9},{9,10},{10,1... | collective-permute-start | bytes 995336 | tf_op jit(solution)/shard_map/ppermute | solution.py:58
  512.9 9.6 %attn_terms.1 = (bf16[4,256,1152]{2,1,0:T(8,128)(2,1)}, f32[2,1152]{1,0:T(2,128)}) custom-call(s32[2]{0:T(128)} %copy-done.10, bf16[1024,432]{1,0:T(8,128)(2,1)} %copy-done.16, bf16[1024,432]{1,0:T(8,128)(2,1)} %copy-done.17, bf16[1152,1152]{1,0:T(8,128)(2,1)} %bitcast.129, bf16[256,1152]{1,0:T(8,128)(2,1)} %copy-done.2, bf16[256,1152]{1,0:T(8,128)(2,1)} %copy-done.13, ...), custom_call_target="tpu_custom_call" | custom-call | flops 10000000000 | bytes 10000000 | tf_op jit(solution)/shard_map/attn_terms/pallas_call | solution.py:667
  528.0 5.0 collective-permute-done.55
  533.0 7.7 %collective-permute-done.52 = bf16[2,72,1152]{2,1,0:T(8,128)(2,1)S(1)} collective-permute-done((bf16[2,72,1152]{2,1,0:T(8,128)(2,1)S(1)}, bf16[2,72,1152]{2,1,0:T(8,128)(2,1)S(1)}, u32[]{:S(2)}, u32[]{:S(2)}) %collective-permute-start.52) | collective-permute-done | bytes 331808 | tf_op jit(solution)/shard_map/ppermute | solution.py:779
  552.5 6.6 %collective-permute-done.62 = f32[6,1152]{1,0:T(8,128)S(1)} collective-permute-done((f32[6,1152]{1,0:T(8,128)S(1)}, f32[6,1152]{1,0:T(8,128)S(1)}, u32[]{:S(2)}, u32[]{:S(2)}) %collective-permute-start.62) | collective-permute-done | bytes 27680 | tf_op jit(solution)/shard_map/ppermute | solution.py:779
  566.2 7.1 %collective-permute-done.63 = bf16[4,72,1152]{2,1,0:T(8,128)(2,1)S(1)} collective-permute-done((bf16[4,72,1152]{2,1,0:T(8,128)(2,1)S(1)}, bf16[4,72,1152]{2,1,0:T(8,128)(2,1)S(1)}, u32[]{:S(2)}, u32[]{:S(2)}) %collective-permute-start.63) | collective-permute-done | bytes 663584 | tf_op jit(solution)/shard_map/ppermute | solution.py:779
  578.4 4.7 collective-permute-done.67
  584.5 16.8 %update_slots.1 = (f32[16,72,1152]{2,1,0:T(8,128)}, f32[16,72,1152]{2,1,0:T(8,128)}, f32[16,72,1152]{2,1,0:T(8,128)}) custom-call(s32[16]{0:T(128)} %convert_element_type.102.filled_ref, s32[16]{0:T(128)} %get-tuple-element.459.which_ref, s32[16]{0:T(128)} %get-tuple-element.458.position_ref, f32[16,72,1152]{2,1,0:T(8,128)} %weight.1, f32[16,72,1152]{2,1,0:T(8,128)} %one.1, ...), custom_call_target="tpu_custom_call" | custom-call | flops 1000 | bytes 1000 | tf_op jit(solution)/shard_map/update_slots/pallas_call | solution.py:749
  (374 shorter events, 156.3 us)
Async XLA Ops:
  7.2 97.2 %reduce-scatter.5.cloned.1.call-start = ((), (), s32[]{:S(2)}) async-start(), calls=%async_computation.4 | async-start | bytes 5971968 | tf_op jit(solution)/shard_map/reduce_scatter | solution.py:1055
  20.8 151.8 %all-gather.6.cloned.1.call-start = ((), (), s32[]{:S(2)}) async-start(), calls=%async_computation.5 | async-start | bytes 5971968 | tf_op jit(solution)/shard_map/all_gather | solution.py:1081
  20.9 21.3 %collective-permute-start = (bf16[16,72,1152]{2,1,0:T(8,128)(2,1)}, bf16[16,72,1152]{2,1,0:T(8,128)(2,1)}, u32[]{:S(2)}, u32[]{:S(2)}) collective-permute-start(bf16[16,72,1152]{2,1,0:T(8,128)(2,1)} %get-tuple-element.200), channel_id=1, source_target_pairs={{0,4},{4,0},{8,12},{12,8},{16,20},{20,16},{24,28},{28,24},{1,5},{5... | collective-permute-start | bytes 7962632 | tf_op jit(solution)/shard_map/ppermute | solution.py:779
  22.6 18.3 %collective-permute-start.2 = (bf16[256,1152]{1,0:T(8,128)(2,1)S(1)}, bf16[256,1152]{1,0:T(8,128)(2,1)S(1)}, u32[]{:S(2)}, u32[]{:S(2)}) collective-permute-start(bf16[256,1152]{1,0:T(8,128)(2,1)S(1)} %fusion.6.refs_0_.refs_3_), channel_id=1, source_target_pairs={{1,0},{2,1},{3,2},{5,4},{6,5},{7,6},{9,8},{10,9},{11,10},{13,12},{... | collective-permute-start | bytes 1769480 | tf_op jit(solution)/shard_map/ppermute | solution.py:929
  23.9 18.2 %collective-permute-start.1 = (bf16[256,1152]{1,0:T(8,128)(2,1)S(1)}, bf16[256,1152]{1,0:T(8,128)(2,1)}, u32[]{:S(2)}, u32[]{:S(2)}) collective-permute-start(bf16[256,1152]{1,0:T(8,128)(2,1)S(1)} %fusion.6.refs_0_.refs_3_), channel_id=1, source_target_pairs={{0,1},{1,2},{2,3},{4,5},{5,6},{6,7},{8,9},{9,10},{10,11},{12,13},{... | collective-permute-start | bytes 1769480 | tf_op jit(solution)/shard_map/ppermute | solution.py:929
  46.3 39.8 %collective-permute-start.5 = (bf16[256,1152]{1,0:T(8,128)(2,1)}, bf16[256,1152]{1,0:T(8,128)(2,1)}, u32[]{:S(2)}, u32[]{:S(2)}) collective-permute-start(bf16[256,1152]{1,0:T(8,128)(2,1)} %collective-permute-done.1.refs_1_), channel_id=1, source_target_pairs={{1,2},{2,3},{5,6},{6,7},{9,10},{10,11},{13,14},{14,15},{17,18},{18... | collective-permute-start | bytes 1769480 | tf_op jit(solution)/shard_map/ppermute | solution.py:929
  47.8 38.3 %collective-permute-start.6 = (bf16[256,1152]{1,0:T(8,128)(2,1)S(1)}, bf16[256,1152]{1,0:T(8,128)(2,1)}, u32[]{:S(2)}, u32[]{:S(2)}) collective-permute-start(bf16[256,1152]{1,0:T(8,128)(2,1)S(1)} %collective-permute-done.2.refs_4_), channel_id=1, source_target_pairs={{1,0},{2,1},{5,4},{6,5},{9,8},{10,9},{13,12},{14,13},{17,16},{18,1... | collective-permute-start | bytes 1769480 | tf_op jit(solution)/shard_map/ppermute | solution.py:929
  49.0 37.0 %collective-permute-start.3 = (bf16[4,72,1152]{2,1,0:T(8,128)(2,1)}, bf16[4,72,1152]{2,1,0:T(8,128)(2,1)}, u32[]{:S(2)}, u32[]{:S(2)}) collective-permute-start(bf16[4,72,1152]{2,1,0:T(8,128)(2,1)} %get-tuple-element.204), channel_id=1, source_target_pairs={{0,8},{4,12},{8,0},{12,4},{16,24},{20,28},{24,16},{28,20},{1,9},{5... | collective-permute-start | bytes 1990664 | tf_op jit(solution)/shard_map/ppermute | solution.py:779
  50.9 35.2 %collective-permute-start.4 = (bf16[4,72,1152]{2,1,0:T(8,128)(2,1)}, bf16[4,72,1152]{2,1,0:T(8,128)(2,1)}, u32[]{:S(2)}, u32[]{:S(2)}) collective-permute-start(bf16[4,72,1152]{2,1,0:T(8,128)(2,1)} %get-tuple-element.206), channel_id=1, source_target_pairs={{0,16},{4,20},{8,24},{12,28},{16,0},{20,4},{24,8},{28,12},{1,17},{... | collective-permute-start | bytes 1990664 | tf_op jit(solution)/shard_map/ppermute | solution.py:779
  56.2 29.8 %collective-permute-start.7 = (bf16[4,120,288]{1,2,0:T(8,128)(2,1)S(1)}, bf16[4,120,288]{1,2,0:T(8,128)(2,1)S(1)}, u32[]{:S(2)}, u32[]{:S(2)}) collective-permute-start(bf16[4,120,288]{1,2,0:T(8,128)(2,1)S(1)} %copy.61), channel_id=1, source_target_pairs={{0,16},{4,20},{8,24},{12,28},{16,0},{20,4},{24,8},{28,12},{1,17},{... | collective-permute-start | bytes 829448 | tf_op jit(solution)/shard_map/ppermute | solution.py:779
  88.4 16.0 %collective-permute-start.11 = (bf16[256,1152]{1,0:T(8,128)(2,1)}, bf16[256,1152]{1,0:T(8,128)(2,1)S(1)}, u32[]{:S(2)}, u32[]{:S(2)}) collective-permute-start(bf16[256,1152]{1,0:T(8,128)(2,1)} %collective-permute-done.6.refs_5_), channel_id=1, source_target_pairs={{1,0},{5,4},{9,8},{13,12},{17,16},{21,20},{25,24},{29,28}} | collective-permute-start | bytes 1769480 | tf_op jit(solution)/shard_map/ppermute | solution.py:929
  104.4 139.5 %all-gather.10.cloned.1.call-start = ((), (), s32[]{:S(2)}) async-start(), calls=%async_computation.10 | async-start | bytes 2949120 | tf_op jit(solution)/shard_map/all_gather | solution.py:1096
  109.4 29.8 %collective-permute-start.20 = (bf16[2,72,1152]{2,1,0:T(8,128)(2,1)S(1)}, bf16[2,72,1152]{2,1,0:T(8,128)(2,1)S(1)}, u32[]{:S(2)}, u32[]{:S(2)}) collective-permute-start(bf16[2,72,1152]{2,1,0:T(8,128)(2,1)S(1)} %add.300.refs_0_), channel_id=1, source_target_pairs={{0,3},{1,0},{2,1},{3,2},{4,7},{5,4},{6,5},{7,6},{8,11},{9,8},{10,9... | collective-permute-start | bytes 995336 | tf_op jit(solution)/shard_map/ppermute | solution.py:58
  112.0 27.2 %collective-permute-start.19 = (bf16[2,72,1152]{2,1,0:T(8,128)(2,1)S(1)}, bf16[2,72,1152]{2,1,0:T(8,128)(2,1)S(1)}, u32[]{:S(2)}, u32[]{:S(2)}) collective-permute-start(bf16[2,72,1152]{2,1,0:T(8,128)(2,1)S(1)} %add.300.refs_0_), channel_id=1, source_target_pairs={{0,2},{1,3},{2,0},{3,1},{4,6},{5,7},{6,4},{7,5},{8,10},{9,11},{10,... | collective-permute-start | bytes 995336 | tf_op jit(solution)/shard_map/ppermute | solution.py:58
  112.0 28.7 %collective-permute-start.18 = (bf16[2,72,1152]{2,1,0:T(8,128)(2,1)S(1)}, bf16[2,72,1152]{2,1,0:T(8,128)(2,1)}, u32[]{:S(2)}, u32[]{:S(2)}) collective-permute-start(bf16[2,72,1152]{2,1,0:T(8,128)(2,1)S(1)} %add.300.refs_0_), channel_id=1, source_target_pairs={{0,1},{1,2},{2,3},{3,0},{4,5},{5,6},{6,7},{7,4},{8,9},{9,10},{10,1... | collective-permute-start | bytes 995336 | tf_op jit(solution)/shard_map/ppermute | solution.py:58
  114.1 15.5 %collective-permute-start.14 = (bf16[2,72,1152]{2,1,0:T(8,128)(2,1)S(1)}, bf16[2,72,1152]{2,1,0:T(8,128)(2,1)S(1)}, u32[]{:S(2)}, u32[]{:S(2)}) collective-permute-start(bf16[2,72,1152]{2,1,0:T(8,128)(2,1)S(1)} %pad_maximum_fusion.8), channel_id=1, source_target_pairs={{0,16},{4,20},{8,24},{12,28},{16,0},{20,4},{24,8},{28,12},{1,17},{... | collective-permute-start | bytes 995336 | tf_op jit(solution)/shard_map/ppermute | solution.py:779
  143.1 29.6 %collective-permute-start.26 = (bf16[120,288]{0,1:T(8,128)(2,1)S(1)}, bf16[120,288]{0,1:T(8,128)(2,1)S(1)}, u32[]{:S(2)}, u32[]{:S(2)}) collective-permute-start(bf16[120,288]{0,1:T(8,128)(2,1)S(1)} %bitcast_add_fusion), channel_id=1, source_target_pairs={{0,3},{1,0},{2,1},{3,2},{4,7},{5,4},{6,5},{7,6},{8,11},{9,8},{10,9... | collective-permute-start | bytes 207368 | tf_op jit(solution)/shard_map/ppermute | solution.py:58
  146.3 26.4 %collective-permute-start.25 = (bf16[120,288]{0,1:T(8,128)(2,1)S(1)}, bf16[120,288]{0,1:T(8,128)(2,1)S(1)}, u32[]{:S(2)}, u32[]{:S(2)}) collective-permute-start(bf16[120,288]{0,1:T(8,128)(2,1)S(1)} %bitcast_add_fusion), channel_id=1, source_target_pairs={{0,2},{1,3},{2,0},{3,1},{4,6},{5,7},{6,4},{7,5},{8,10},{9,11},{10,... | collective-permute-start | bytes 207368 | tf_op jit(solution)/shard_map/ppermute | solution.py:58
  147.1 20.8 %collective-permute-start.22 = (bf16[4,72,1152]{2,1,0:T(8,128)(2,1)}, bf16[4,72,1152]{2,1,0:T(8,128)(2,1)}, u32[]{:S(2)}, u32[]{:S(2)}) collective-permute-start(bf16[4,72,1152]{2,1,0:T(8,128)(2,1)} %get-tuple-element.231), channel_id=1, source_target_pairs={{0,8},{4,12},{8,0},{12,4},{16,24},{20,28},{24,16},{28,20},{1,9},{5... | collective-permute-start | bytes 1990664 | tf_op jit(solution)/shard_map/ppermute | solution.py:779
  148.9 21.4 %collective-permute-start.23 = (bf16[4,72,1152]{2,1,0:T(8,128)(2,1)}, bf16[4,72,1152]{2,1,0:T(8,128)(2,1)}, u32[]{:S(2)}, u32[]{:S(2)}) collective-permute-start(bf16[4,72,1152]{2,1,0:T(8,128)(2,1)} %get-tuple-element.232), channel_id=1, source_target_pairs={{0,16},{4,20},{8,24},{12,28},{16,0},{20,4},{24,8},{28,12},{1,17},{... | collective-permute-start | bytes 1990664 | tf_op jit(solution)/shard_map/ppermute | solution.py:779
  149.1 341.9 %reduce-scatter.7.cloned.1.call-start = ((), (), s32[]{:S(2)}) async-start(), calls=%async_computation.6 | async-start | bytes 5971968 | tf_op jit(solution)/shard_map/reduce_scatter | solution.py:1213
  172.6 56.1 %collective-permute-start.27 = (bf16[8,72,1152]{2,1,0:T(8,128)(2,1)}, bf16[8,72,1152]{2,1,0:T(8,128)(2,1)}, u32[]{:S(2)}, u32[]{:S(2)}) collective-permute-start(bf16[8,72,1152]{2,1,0:T(8,128)(2,1)} %pad_maximum_fusion.rest_0_), channel_id=1, source_target_pairs={{0,16},{4,20},{8,24},{12,28},{16,0},{20,4},{24,8},{28,12},{1,17},{... | collective-permute-start | bytes 3981320 | tf_op jit(solution)/shard_map/ppermute | solution.py:779
  173.9 54.8 %collective-permute-start.28 = (bf16[8,72,1152]{2,1,0:T(8,128)(2,1)}, bf16[8,72,1152]{2,1,0:T(8,128)(2,1)}, u32[]{:S(2)}, u32[]{:S(2)}) collective-permute-start(bf16[8,72,1152]{2,1,0:T(8,128)(2,1)} %pad_maximum_fusion.1.rest_2_), channel_id=1, source_target_pairs={{0,8},{4,12},{8,0},{12,4},{16,24},{20,28},{24,16},{28,20},{1,9},{5... | collective-permute-start | bytes 3981320 | tf_op jit(solution)/shard_map/ppermute | solution.py:779
  180.6 17.8 %collective-permute-start.31 = (bf16[376,288]{1,0:T(8,128)(2,1)S(1)}, bf16[376,288]{1,0:T(8,128)(2,1)}, u32[]{:S(2)}, u32[]{:S(2)}) collective-permute-start(bf16[376,288]{1,0:T(8,128)(2,1)S(1)} %get-tuple-element.452), channel_id=1, source_target_pairs={{0,1},{1,2},{2,3},{3,0},{4,5},{5,6},{6,7},{7,4},{8,9},{9,10},{10,1... | collective-permute-start | bytes 649736 | tf_op jit(solution)/shard_map/ppermute | solution.py:58
  182.9 26.1 %collective-permute-start.29 = (bf16[376,288]{1,0:T(8,128)(2,1)S(1)}, bf16[376,288]{1,0:T(8,128)(2,1)}, u32[]{:S(2)}, u32[]{:S(2)}) collective-permute-start(bf16[376,288]{1,0:T(8,128)(2,1)S(1)} %get-tuple-element.453), channel_id=1, source_target_pairs={{0,3},{1,0},{2,1},{3,2},{4,7},{5,4},{6,5},{7,6},{8,11},{9,8},{10,9... | collective-permute-start | bytes 649736 | tf_op jit(solution)/shard_map/ppermute | solution.py:58
  184.6 44.1 %collective-permute-start.30 = (bf16[376,288]{1,0:T(8,128)(2,1)S(1)}, bf16[376,288]{1,0:T(8,128)(2,1)}, u32[]{:S(2)}, u32[]{:S(2)}) collective-permute-start(bf16[376,288]{1,0:T(8,128)(2,1)S(1)} %get-tuple-element.454), channel_id=1, source_target_pairs={{0,2},{1,3},{2,0},{3,1},{4,6},{5,7},{6,4},{7,5},{8,10},{9,11},{10,... | collective-permute-start | bytes 649736 | tf_op jit(solution)/shard_map/ppermute | solution.py:58
  198.4 33.5 %collective-permute-start.32 = (bf16[8,72,1152]{2,1,0:T(8,128)(2,1)}, bf16[8,72,1152]{2,1,0:T(8,128)(2,1)}, u32[]{:S(2)}, u32[]{:S(2)}) collective-permute-start(bf16[8,72,1152]{2,1,0:T(8,128)(2,1)} %pad_maximum_fusion.rest_0_), channel_id=1, source_target_pairs={{0,4},{4,0},{8,12},{12,8},{16,20},{20,16},{24,28},{28,24},{1,5},{5... | collective-permute-start | bytes 3981320 | tf_op jit(solution)/shard_map/ppermute | solution.py:779
  209.0 22.9 %collective-permute-start.34 = (bf16[8,72,1152]{2,1,0:T(8,128)(2,1)}, bf16[8,72,1152]{2,1,0:T(8,128)(2,1)}, u32[]{:S(2)}, u32[]{:S(2)}) collective-permute-start(bf16[8,72,1152]{2,1,0:T(8,128)(2,1)} %pad_maximum_fusion.1.rest_2_), channel_id=1, source_target_pairs={{0,4},{4,0},{8,12},{12,8},{16,20},{20,16},{24,28},{28,24},{1,5},{5... | collective-permute-start | bytes 3981320 | tf_op jit(solution)/shard_map/ppermute | solution.py:779
  257.1 28.5 %collective-permute-start.37 = (bf16[256,1152]{1,0:T(8,128)(2,1)}, bf16[256,1152]{1,0:T(8,128)(2,1)}, u32[]{:S(2)}, u32[]{:S(2)}) collective-permute-start(bf16[256,1152]{1,0:T(8,128)(2,1)} %get-tuple-element.268.refs_0_.refs_6_), channel_id=1, source_target_pairs={{0,3},{1,0},{2,1},{3,2},{4,7},{5,4},{6,5},{7,6},{8,11},{9,8},{10,9... | collective-permute-start | bytes 1769480 | tf_op jit(solution)/shard_map/ppermute | solution.py:58
  258.0 27.6 %collective-permute-start.36 = (bf16[256,1152]{1,0:T(8,128)(2,1)}, bf16[256,1152]{1,0:T(8,128)(2,1)}, u32[]{:S(2)}, u32[]{:S(2)}) collective-permute-start(bf16[256,1152]{1,0:T(8,128)(2,1)} %get-tuple-element.268.refs_0_.refs_6_), channel_id=1, source_target_pairs={{0,1},{1,2},{2,3},{3,0},{4,5},{5,6},{6,7},{7,4},{8,9},{9,10},{10,1... | collective-permute-start | bytes 1769480 | tf_op jit(solution)/shard_map/ppermute | solution.py:58
  270.5 39.4 %collective-permute-start.40 = (bf16[256,1152]{1,0:T(8,128)(2,1)}, bf16[256,1152]{1,0:T(8,128)(2,1)}, u32[]{:S(2)}, u32[]{:S(2)}) collective-permute-start(bf16[256,1152]{1,0:T(8,128)(2,1)} %get-tuple-element.268.refs_0_.refs_6_), channel_id=1, source_target_pairs={{0,2},{1,3},{2,0},{3,1},{4,6},{5,7},{6,4},{7,5},{8,10},{9,11},{10,... | collective-permute-start | bytes 1769480 | tf_op jit(solution)/shard_map/ppermute | solution.py:58
  329.3 194.0 %reduce-scatter.9.cloned.1.call-start = ((), (), s32[]{:S(2)}) async-start(), calls=%async_computation.7 | async-start | bytes 2949120 | tf_op jit(solution)/shard_map/reduce_scatter | solution.py:1284
  329.3 17.6 %collective-permute-start.38 = (bf16[256,1152]{1,0:T(8,128)(2,1)}, bf16[256,1152]{1,0:T(8,128)(2,1)}, u32[]{:S(2)}, u32[]{:S(2)}) collective-permute-start(bf16[256,1152]{1,0:T(8,128)(2,1)} %get-tuple-element.266), channel_id=1, source_target_pairs={{0,3},{1,0},{2,1},{3,2},{4,7},{5,4},{6,5},{7,6},{8,11},{9,8},{10,9... | collective-permute-start | bytes 1769480 | tf_op jit(solution)/shard_map/ppermute | solution.py:58
  332.9 27.2 %collective-permute-start.39 = (bf16[256,1152]{1,0:T(8,128)(2,1)}, bf16[256,1152]{1,0:T(8,128)(2,1)}, u32[]{:S(2)}, u32[]{:S(2)}) collective-permute-start(bf16[256,1152]{1,0:T(8,128)(2,1)} %get-tuple-element.267), channel_id=1, source_target_pairs={{0,1},{1,2},{2,3},{3,0},{4,5},{5,6},{6,7},{7,4},{8,9},{9,10},{10,1... | collective-permute-start | bytes 1769480 | tf_op jit(solution)/shard_map/ppermute | solution.py:58
  333.1 50.0 %collective-permute-start.41 = (bf16[256,1152]{1,0:T(8,128)(2,1)}, bf16[256,1152]{1,0:T(8,128)(2,1)}, u32[]{:S(2)}, u32[]{:S(2)}) collective-permute-start(bf16[256,1152]{1,0:T(8,128)(2,1)} %get-tuple-element.270), channel_id=1, source_target_pairs={{0,2},{1,3},{2,0},{3,1},{4,6},{5,7},{6,4},{7,5},{8,10},{9,11},{10,... | collective-permute-start | bytes 1769480 | tf_op jit(solution)/shard_map/ppermute | solution.py:58
  404.4 25.0 %collective-permute-start.45 = (bf16[2,4,288,1152]{3,2,1,0:T(8,128)(2,1)}, bf16[2,4,288,1152]{3,2,1,0:T(8,128)(2,1)}, u32[]{:S(2)}, u32[]{:S(2)}) collective-permute-start(bf16[2,4,288,1152]{3,2,1,0:T(8,128)(2,1)} %get-tuple-element.297), channel_id=1, source_target_pairs={{0,4},{4,0},{8,12},{12,8},{16,20},{20,16},{24,28},{28,24},{1,5},{5... | collective-permute-start | bytes 15925256 | tf_op jit(solution)/shard_map/ppermute | solution.py:779
  404.5 23.4 %collective-permute-start.43 = (bf16[376,288]{1,0:T(8,128)(2,1)S(1)}, bf16[376,288]{1,0:T(8,128)(2,1)S(1)}, u32[]{:S(2)}, u32[]{:S(2)}) collective-permute-start(bf16[376,288]{1,0:T(8,128)(2,1)S(1)} %copy-done.67), channel_id=1, source_target_pairs={{0,2},{1,3},{2,0},{3,1},{4,6},{5,7},{6,4},{7,5},{8,10},{9,11},{10,... | collective-permute-start | bytes 649736 | tf_op jit(solution)/shard_map/ppermute | solution.py:58
  407.8 20.8 %collective-permute-start.44 = (bf16[376,288]{1,0:T(8,128)(2,1)S(1)}, bf16[376,288]{1,0:T(8,128)(2,1)S(1)}, u32[]{:S(2)}, u32[]{:S(2)}) collective-permute-start(bf16[376,288]{1,0:T(8,128)(2,1)S(1)} %copy-done.66), channel_id=1, source_target_pairs={{0,3},{1,0},{2,1},{3,2},{4,7},{5,4},{6,5},{7,6},{8,11},{9,8},{10,9... | collective-permute-start | bytes 649736 | tf_op jit(solution)/shard_map/ppermute | solution.py:58
  429.4 119.3 %all-gather.8.cloned.1.call-start = ((), (), s32[]{:S(2)}) async-start(), calls=%async_computation.9 | async-start | bytes 5971968 | tf_op jit(solution)/shard_map/all_gather | solution.py:1307
  437.6 30.5 %collective-permute-start.46 = (bf16[4,2,72,1152]{3,2,1,0:T(8,128)(2,1)}, bf16[4,2,72,1152]{3,2,1,0:T(8,128)(2,1)}, u32[]{:S(2)}, u32[]{:S(2)}) collective-permute-start(bf16[4,2,72,1152]{3,2,1,0:T(8,128)(2,1)} %get-tuple-element.302), channel_id=1, source_target_pairs={{0,8},{4,12},{8,0},{12,4},{16,24},{20,28},{24,16},{28,20},{1,9},{5... | collective-permute-start | bytes 3981320 | tf_op jit(solution)/shard_map/ppermute | solution.py:779
  439.2 30.3 %collective-permute-start.47 = (bf16[4,2,72,1152]{3,2,1,0:T(8,128)(2,1)}, bf16[4,2,72,1152]{3,2,1,0:T(8,128)(2,1)}, u32[]{:S(2)}, u32[]{:S(2)}) collective-permute-start(bf16[4,2,72,1152]{3,2,1,0:T(8,128)(2,1)} %get-tuple-element.304), channel_id=1, source_target_pairs={{0,16},{4,20},{8,24},{12,28},{16,0},{20,4},{24,8},{28,12},{1,17},{... | collective-permute-start | bytes 3981320 | tf_op jit(solution)/shard_map/ppermute | solution.py:779
  474.8 14.9 %collective-permute-start.48 = (bf16[4,72,1152]{2,1,0:T(8,128)(2,1)S(1)}, bf16[4,72,1152]{2,1,0:T(8,128)(2,1)}, u32[]{:S(2)}, u32[]{:S(2)}) collective-permute-start(bf16[4,72,1152]{2,1,0:T(8,128)(2,1)S(1)} %get-tuple-element.319), channel_id=1, source_target_pairs={{0,16},{4,20},{8,24},{12,28},{16,0},{20,4},{24,8},{28,12},{1,17},{... | collective-permute-start | bytes 1990664 | tf_op jit(solution)/shard_map/ppermute | solution.py:779
  476.4 14.6 %collective-permute-start.49 = (bf16[4,72,1152]{2,1,0:T(8,128)(2,1)S(1)}, bf16[4,72,1152]{2,1,0:T(8,128)(2,1)}, u32[]{:S(2)}, u32[]{:S(2)}) collective-permute-start(bf16[4,72,1152]{2,1,0:T(8,128)(2,1)S(1)} %get-tuple-element.321), channel_id=1, source_target_pairs={{0,8},{4,12},{8,0},{12,4},{16,24},{20,28},{24,16},{28,20},{1,9},{5... | collective-permute-start | bytes 1990664 | tf_op jit(solution)/shard_map/ppermute | solution.py:779
  491.0 111.1 %reduce-scatter.11.cloned.1.call-start = ((), (), s32[]{:S(2)}) async-start(), calls=%async_computation.8 | async-start | bytes 2949120 | tf_op jit(solution)/shard_map/reduce_scatter | solution.py:1319
  503.1 20.1 %collective-permute-start.50 = (bf16[2,1,288,1152]{3,2,1,0:T(8,128)(2,1)}, bf16[2,1,288,1152]{3,2,1,0:T(8,128)(2,1)S(1)}, u32[]{:S(2)}, u32[]{:S(2)}) collective-permute-start(bf16[2,1,288,1152]{3,2,1,0:T(8,128)(2,1)} %get-tuple-element.336), channel_id=1, source_target_pairs={{0,4},{4,0},{8,12},{12,8},{16,20},{20,16},{24,28},{28,24},{1,5},{5... | collective-permute-start | bytes 3981320 | tf_op jit(solution)/shard_map/ppermute | solution.py:779
  503.2 24.8 %collective-permute-start.54 = (bf16[2,72,1152]{2,1,0:T(8,128)(2,1)}, bf16[2,72,1152]{2,1,0:T(8,128)(2,1)S(1)}, u32[]{:S(2)}, u32[]{:S(2)}) collective-permute-start(bf16[2,72,1152]{2,1,0:T(8,128)(2,1)} %get-tuple-element.351), channel_id=1, source_target_pairs={{0,1},{1,2},{2,3},{3,0},{4,5},{5,6},{6,7},{7,4},{8,9},{9,10},{10,1... | collective-permute-start | bytes 995336 | tf_op jit(solution)/shard_map/ppermute | solution.py:58
  510.5 22.6 %collective-permute-start.55 = (bf16[2,72,1152]{2,1,0:T(8,128)(2,1)}, bf16[2,72,1152]{2,1,0:T(8,128)(2,1)S(1)}, u32[]{:S(2)}, u32[]{:S(2)}) collective-permute-start(bf16[2,72,1152]{2,1,0:T(8,128)(2,1)} %get-tuple-element.352), channel_id=1, source_target_pairs={{0,2},{1,3},{2,0},{3,1},{4,6},{5,7},{6,4},{7,5},{8,10},{9,11},{10,... | collective-permute-start | bytes 995336 | tf_op jit(solution)/shard_map/ppermute | solution.py:58
  510.6 22.4 %collective-permute-start.56 = (bf16[2,72,1152]{2,1,0:T(8,128)(2,1)}, bf16[2,72,1152]{2,1,0:T(8,128)(2,1)S(1)}, u32[]{:S(2)}, u32[]{:S(2)}) collective-permute-start(bf16[2,72,1152]{2,1,0:T(8,128)(2,1)} %get-tuple-element.353), channel_id=1, source_target_pairs={{0,3},{1,0},{2,1},{3,2},{4,7},{5,4},{6,5},{7,6},{8,11},{9,8},{10,9... | collective-permute-start | bytes 995336 | tf_op jit(solution)/shard_map/ppermute | solution.py:58
  (95 other events, 1095.6 us)
Sparse Core Ops, SparseCore 0:
  20.9 71.0 reduce-scatter.4
  104.5 45.9 all-gather.5
  152.2 74.6 all-gather.9
  329.4 58.1 reduce-scatter.6
  429.5 51.2 reduce-scatter.8
  491.1 48.2 all-gather.7
  552.6 49.4 reduce-scatter.10
where the time goes:
time: 624 us; the launch traced here: 615 us
  waiting for transfers between devices  253 us (41%)
  Pallas kernels  170 us (27%)
  starting transfers between devices  82 us (13%)
  other arithmetic  45 us (7%)
  local copies, waits for them, and re-layouts  28.7 us (5%)
  between operations  15.6 us (2%)
  matrix products  11.6 us (2%)
  blocking collectives  9.55 us (2%)
    ppermute x21, waiting for transfers between devices, shift(): lax.ppermute(values, 'tensor', [(i, (i + step) % count) for i in range(co...  135 us
    ppermute x41, waiting for transfers between devices, swap(): return lax.ppermute(values, axis, [(i, i ^ 1 << bit) for i in range(count)])  111 us
    ppermute x41, starting transfers between devices, swap(): return lax.ppermute(values, axis, [(i, i ^ 1 << bit) for i in range(count)])  36 us
    ppermute x21, starting transfers between devices, shift(): lax.ppermute(values, 'tensor', [(i, (i + step) % count) for i in range(co...  33.1 us
    pallas_call x3, Pallas kernels, mlp_core(): pl.pallas_call(body, grid=(steps,), in_specs=[whole] * (2 * groups) + [pl...  25.9 us
    pallas_call x2, Pallas kernels, ranked_terms(): pl.pallas_call(body, in_specs=[in_smem()] + [in_vmem()] * (len(lefts) + 1...  19.4 us
    unnamed x143, local copies, waits for them, and re-layouts  18.9 us
    pallas_call x1, Pallas kernels, update_slots(): pl.pallas_call(body, grid_spec=pltpu.PrefetchScalarGridSpec(num_scalar_pr...  16.8 us
  transfers between devices with their start and end apart: 75, of which 34 were waited for; matrix products, arithmetic and copies ran while one was open for 10% of the time, Pallas kernels for 21%

commit v1 on v0

--- a/solution.py
+++ b/solution.py
@@ -593,7 +593,7 @@
     )(place, *flat)
 
 
-def mlp_grads(grad_pres, acts, rows_in, grads_in):
+def mlp_grads(grad_pres, acts, rows_in, grads_in, after):
     pieces, rights = len(acts), len(rows_in)
     tokens, width = rows_in[0].shape
     hidden = acts[0].shape[1]
@@ -604,7 +604,7 @@
         step = pl.program_id(0)
         lefts_up, lefts_down = refs[:pieces], refs[pieces : 2 * pieces]
         rights_up = refs[2 * pieces : 2 * pieces + rights]
-        rights_down = refs[2 * pieces + rights : -1]
+        rights_down = refs[2 * pieces + rights : 2 * pieces + 2 * rights]
         out = refs[-1]
 
         def terms(lefts, turn, others):
@@ -630,13 +630,14 @@
     return pl.pallas_call(
         body,
         grid=(2 * steps,),
-        in_specs=[pl.BlockSpec(array.shape, lambda s: (0, 0)) for array in arrays],
+        in_specs=[pl.BlockSpec(array.shape, lambda s: (0, 0)) for array in arrays]
+        + [pl.BlockSpec(memory_space=pl.ANY)] * len(after),
         out_specs=chunked,
         out_shape=jax.ShapeDtypeStruct((2 * hidden, width), low),
         compiler_params=pltpu.CompilerParams(vmem_limit_bytes=60 * 2**20),
         cost_estimate=cheap,
         name="mlp_grads",
-    )(*arrays)
+    )(*arrays, *after)
 
 
 def ranked_terms(place, lefts, order, pieces, weight, factors, name):
@@ -1196,7 +1197,11 @@
             shift(term, count - k) if k else term for k, term in zip(members_now, terms)
         ]
     mlp_grad = mlp_grads(
-        grad_pres, acts, [h_slots[k] for k in order], [grad_slots[k] for k in order]
+        grad_pres,
+        acts,
+        [h_slots[k] for k in order],
+        [grad_slots[k] for k in order],
+        grad_terms[1:2],
     ).reshape(-1, unit_rows, width)
     hidden_share = w_mlp.shape[0] // 2
     pieces = [
@@ -1234,7 +1239,7 @@
         c_out,
         c_query,
         w_out,
-        (mlp_grad,),
+        (),
     )
 
     grad_parts = [grad_mixed[0]] + [shift(grad_mixed[k], k) for k in range(1, count)]
@@ -1326,7 +1331,8 @@
         one_kept, one_given = split(attn_all[0], x_bit, 1)
         two_kept, two_given = split(attn_all[1], y_bit, 0)
         one_got, two_got = swap(one_given, "dp", 1), swap(two_given, "dp", 2)
-        mod_terms = mod_terms + swap(mod_terms, "dp", 0)
+        for bit in range(2):
+            mod_terms = mod_terms + swap(mod_terms, "dp", bit)
         full_own = full_parts[0]
         one_kept, one_got, two_kept, two_got, mod_terms, full_own, full_got = fence(
             (one_kept, one_got, two_kept, two_got, mod_terms, full_own, full_got)
@@ -1338,7 +1344,7 @@
         one_kept, one_given = split(one_kept + one_got, y_bit, 0)
         two_kept, two_given = split(two_kept + two_got, x_bit, 0)
         one_got, two_got = swap(one_given, "dp", 2), swap(two_given, "dp", 1)
-        mod_terms = mod_terms + swap(mod_terms, "dp", 1)
+        mod_terms = mod_terms + swap(mod_terms, "dp", 2)
         one_kept, one_got, two_kept, two_got, full_sum, mod_terms, mlp_sum = fence(
             (one_kept, one_got, two_kept, two_got, full_sum, mod_terms, mlp_sum)
         )
@@ -1347,18 +1353,18 @@
         first_got, second_got = swap(first, "dp", 1), swap(second, "dp", 2)
         first = jnp.concatenate([first, first_got])
         second = jnp.concatenate([second, second_got])
-        mod_terms = mod_terms + swap(mod_terms, "dp", 2)
+        mod_terms = mod_terms + swap(mod_terms, "tensor", 0)
         first, second, mod_terms = fence((first, second, mod_terms))
         first_far, second_far = swap(first, "dp", 2), swap(second, "dp", 1)
-        mod_terms = mod_terms + swap(mod_terms, "tensor", 0)
+        for bit in range(1, count.bit_length() - 1):
+            mod_terms = mod_terms + swap(mod_terms, "tensor", bit)
         first, first_far, second, second_far, mod_terms = fence(
             (first, first_far, second, second_far, mod_terms)
         )
         pool = jnp.concatenate([first, first_far, second, second_far])
         other = swap(pool, "dp", 0)
-        for bit in range(1, count.bit_length() - 1):
-            mod_terms = mod_terms + swap(mod_terms, "tensor", bit)
-        pool, other, mod_grad = fence((pool, other, mod_terms))
+        mod_grad = mod_terms
+        pool, other = fence((pool, other))
         which, position = in_pool(member_of, np.where(is_attn, 0, 1), 2)
         which = jnp.where(is_mlp, 2, which)
         position = jnp.where(is_mlp, np.arange(units) - 8 * per, position)

time: 624 us -> 624 us (level)
  starting transfers between devices: 82 us -> 90.2 us
  waiting for transfers between devices: 253 us -> 246 us
    ppermute x21, waiting for transfers between devices: 135 us -> 125 us  [shift(): lax.ppermute(values, 'tensor', [(i, (i + step) % count) for i in range(co...]
    ppermute x21, starting transfers between devices: 33.1 us -> 41.2 us  [shift(): lax.ppermute(values, 'tensor', [(i, (i + step) % count) for i in range(co...]
    unnamed x143 -> x147, local copies, waits for them, and re-layouts: 18.9 us -> 18.9 us
  transfers between devices with their start and end apart: 75 -> 75, of which waited for: 34 -> 39; matrix products, arithmetic and copies ran while one was open for 10% -> 10% of each run, Pallas kernels for 21% -> 22%
where the time goes in v1:
time: 624 us; the launch traced here: 616 us
  waiting for transfers between devices  246 us (39%)
  Pallas kernels  169 us (27%)
  starting transfers between devices  90.2 us (14%)
  other arithmetic  45.2 us (7%)
  local copies, waits for them, and re-layouts  28.7 us (5%)
  between operations  15.6 us (2%)
  matrix products  11.6 us (2%)
  blocking collectives  9.64 us (2%)
    ppermute x21, waiting for transfers between devices, shift(): lax.ppermute(values, 'tensor', [(i, (i + step) % count) for i in range(co...  125 us
    ppermute x41, waiting for transfers between devices, swap(): return lax.ppermute(values, axis, [(i, i ^ 1 << bit) for i in range(count)])  111 us
    ppermute x21, starting transfers between devices, shift(): lax.ppermute(values, 'tensor', [(i, (i + step) % count) for i in range(co...  41.2 us
    ppermute x41, starting transfers between devices, swap(): return lax.ppermute(values, axis, [(i, i ^ 1 << bit) for i in range(count)])  36.1 us
    pallas_call x3, Pallas kernels, mlp_core(): pl.pallas_call(body, grid=(steps,), in_specs=[whole] * (2 * groups) + [pl...  26 us
    pallas_call x2, Pallas kernels, ranked_terms(): pl.pallas_call(body, in_specs=[in_smem()] + [in_vmem()] * (len(lefts) + 1...  19.3 us
    unnamed x147, local copies, waits for them, and re-layouts  18.9 us
    pallas_call x1, Pallas kernels, update_slots(): pl.pallas_call(body, grid_spec=pltpu.PrefetchScalarGridSpec(num_scalar_pr...  16.8 us
  transfers between devices with their start and end apart: 75, of which 39 were waited for; matrix products, arithmetic and copies ran while one was open for 10% of the time, Pallas kernels for 22%

profile of v1, /device:TPU:0, one launch (start us, length us, event | category | flops | bytes accessed | tf_op | source)
XLA Modules:
  0.0 615.7 jit_solution(11114695763633952745)
XLA Ops:
  12.7 3.9 pick_units.2
  16.6 4.4 pick_units.3
  24.2 6.4 %collective-permute-start.1 = (bf16[256,1152]{1,0:T(8,128)(2,1)S(1)}, bf16[256,1152]{1,0:T(8,128)(2,1)}, u32[]{:S(2)}, u32[]{:S(2)}) collective-permute-start(bf16[256,1152]{1,0:T(8,128)(2,1)S(1)} %fusion.6.refs_0_.refs_3_), channel_id=1, source_target_pairs={{0,1},{1,2},{2,3},{4,5},{5,6},{6,7},{8,9},{9,10},{10,11},{12,13},{... | collective-permute-start | bytes 1769480 | tf_op jit(solution)/shard_map/ppermute | solution.py:930
  30.6 9.6 %all-gather.1 = s32[8,1,120]{2,1,0:T(1,128)S(1)} all-gather(s32[1,1,120]{2,1,0:T(1,128)S(1)} %bitcast.150), channel_id=1, replica_groups=mesh['dp'=8,'tensor'=4] {'dp'}, dimensions={0}, use_global_device_ids=true | all-gather | bytes 4320 | tf_op jit(solution)/shard_map/all_gather | solution.py:1035
  42.7 4.1 slice_add_fusion
  57.8 29.4 %collective-permute-done.7 = bf16[4,120,288]{1,2,0:T(8,128)(2,1)S(1)} collective-permute-done((bf16[4,120,288]{1,2,0:T(8,128)(2,1)S(1)}, bf16[4,120,288]{1,2,0:T(8,128)(2,1)S(1)}, u32[]{:S(2)}, u32[]{:S(2)}) %collective-permute-start.7) | collective-permute-done | bytes 276512 | tf_op jit(solution)/shard_map/ppermute | solution.py:780
  94.6 6.8 %collective-permute-done.8 = bf16[2,72,1152]{2,1,0:T(8,128)(2,1)S(1)} collective-permute-done((bf16[2,72,1152]{2,1,0:T(8,128)(2,1)S(1)}, bf16[2,72,1152]{2,1,0:T(8,128)(2,1)S(1)}, u32[]{:S(2)}, u32[]{:S(2)}) %collective-permute-start.8) | collective-permute-done | bytes 331808 | tf_op jit(solution)/shard_map/ppermute | solution.py:780
  101.5 3.9 collective-permute-done.11.refs_6_
  115.2 8.5 %collective-permute-done.15 = bf16[1,72,1152]{2,1,0:T(8,128)(2,1)S(1)} collective-permute-done((bf16[1,72,1152]{2,1,0:T(8,128)(2,1)S(1)}, bf16[1,72,1152]{2,1,0:T(8,128)(2,1)S(1)}, u32[]{:S(2)}, u32[]{:S(2)}) %collective-permute-start.15) | collective-permute-done | bytes 165920 | tf_op jit(solution)/shard_map/ppermute | solution.py:780
  126.2 4.5 collective-permute-done.14
  150.5 3.7 place_blocks.2
  154.3 5.5 convolution_convert_fusion.qkv_ref
  160.4 8.3 %self_attend.1 = (bf16[1024,288]{1,0:T(8,128)(2,1)S(1)}, f32[4,1024]{1,0:T(4,128)S(1)}) custom-call(bf16[1024,1152]{1,0:T(8,128)(2,1)S(1)} %convolution_convert_fusion.qkv_ref), custom_call_target="tpu_custom_call" | custom-call | flops 1000 | bytes 1000 | tf_op jit(solution)/shard_map/self_attend/pallas_call | solution.py:106
  186.1 13.7 %collective-permute-done.31.refs_3_ = bf16[376,288]{1,0:T(8,128)(2,1)} collective-permute-done((bf16[376,288]{1,0:T(8,128)(2,1)S(1)}, bf16[376,288]{1,0:T(8,128)(2,1)}, u32[]{:S(2)}, u32[]{:S(2)}) %collective-permute-start.31) | collective-permute-done | bytes 216608 | tf_op jit(solution)/shard_map/ppermute | solution.py:58
  199.8 10.7 %collective-permute-done.29.refs_1_ = bf16[376,288]{1,0:T(8,128)(2,1)} collective-permute-done((bf16[376,288]{1,0:T(8,128)(2,1)S(1)}, bf16[376,288]{1,0:T(8,128)(2,1)}, u32[]{:S(2)}, u32[]{:S(2)}) %collective-permute-start.29) | collective-permute-done | bytes 216608 | tf_op jit(solution)/shard_map/ppermute | solution.py:58
  210.5 20.1 %collective-permute-done.30.refs_2_ = bf16[376,288]{1,0:T(8,128)(2,1)} collective-permute-done((bf16[376,288]{1,0:T(8,128)(2,1)S(1)}, bf16[376,288]{1,0:T(8,128)(2,1)}, u32[]{:S(2)}, u32[]{:S(2)}) %collective-permute-start.30) | collective-permute-done | bytes 216608 | tf_op jit(solution)/shard_map/ppermute | solution.py:58
  236.0 9.7 %place_blocks.3 = (bf16[16,72,1152]{2,1,0:T(8,128)(2,1)}, bf16[16,72,1152]{2,1,0:T(8,128)(2,1)}, bf16[16,72,1152]{2,1,0:T(8,128)(2,1)}, bf16[16,72,1152]{2,1,0:T(8,128)(2,1)}) custom-call(s32[64]{0:T(128)} %multiply_add_fusion.1.which_ref, s32[64]{0:T(128)} %get-tuple-element.403.position_ref, bf16[8,72,1152]{2,1,0:T(8,128)(2,1)} %pad_maximum_fusion.rest_0_, ...), custom_call_target="tpu_custom_call" | custom-call | flops 1000 | bytes 1000 | tf_op jit(solution)/shard_map/place_blocks/pallas_call | solution.py:888
  245.7 13.2 %cross_block.1 = (f32[256,1152]{1,0:T(8,128)}, bf16[256,1152]{1,0:T(8,128)(2,1)}, bf16[256,1152]{1,0:T(8,128)(2,1)}, bf16[120,1152]{1,0:T(8,128)(2,1)}, bf16[120...) custom-call(s32[2]{0:T(128)} %copy-done.10, ...), custom_call_target="tpu_custom_call" | custom-call | flops 1000 | bytes 1000 | tf_op jit(solution)/shard_map/cross_block/pallas_call | solution.py:377
  261.4 3.9 multiply_convert_fusion
  265.3 7.1 %mlp_core.3 = (bf16[256,1152]{1,0:T(8,128)(2,1)}, bf16[256,1152]{1,0:T(8,128)(2,1)}, bf16[256,1152]{1,0:T(8,128)(2,1)}) custom-call(bf16[256,1152]{1,0:T(8,128)(2,1)} %get-tuple-element.267.refs_0_.refs_6_, bf16[256,1152]{1,0:T(8,128)(2,1)} %get-tuple-element.415.refs_1_.refs_10_, bf16[2304,1152]{1,0:T(8,128)(2,1)} %bitcast.117, bf16[2304,1152]{1,0:T(8,128)(2,1)} %bitcast.118), custom_call_target="tpu_custom_call" | custom-call | flops 1000 | bytes 1000 | tf_op jit(solution)/shard_map/mlp_core/pallas_call | solution.py:212
  272.4 15.0 %collective-permute-done.37.refs_1_.refs_8_ = bf16[256,1152]{1,0:T(8,128)(2,1)} collective-permute-done((bf16[256,1152]{1,0:T(8,128)(2,1)}, bf16[256,1152]{1,0:T(8,128)(2,1)}, u32[]{:S(2)}, u32[]{:S(2)}) %collective-permute-start.37) | collective-permute-done | bytes 589856 | tf_op jit(solution)/shard_map/ppermute | solution.py:58
  287.4 11.8 %mlp_core.4 = (bf16[512,1152]{1,0:T(8,128)(2,1)}, bf16[512,1152]{1,0:T(8,128)(2,1)}, bf16[256,1152]{1,0:T(8,128)(2,1)}, bf16[256,1152]{1,0:T(8,128)(2,1)}) custom-call(bf16[256,1152]{1,0:T(8,128)(2,1)} %collective-permute-done.36.refs_0_.refs_7_, bf16[256,1152]{1,0:T(8,128)(2,1)} %collective-permute-done.37.refs_1_.refs_8_, ...), custom_call_target="tpu_custom_call" | custom-call | flops 1000 | bytes 1000 | tf_op jit(solution)/shard_map/mlp_core/pallas_call | solution.py:212
  300.5 11.4 %collective-permute-done.40.refs_0_.refs_9_ = bf16[256,1152]{1,0:T(8,128)(2,1)} collective-permute-done((bf16[256,1152]{1,0:T(8,128)(2,1)}, bf16[256,1152]{1,0:T(8,128)(2,1)}, u32[]{:S(2)}, u32[]{:S(2)}) %collective-permute-start.40) | collective-permute-done | bytes 589856 | tf_op jit(solution)/shard_map/ppermute | solution.py:58
  311.9 7.1 %mlp_core.5 = (bf16[256,1152]{1,0:T(8,128)(2,1)}, bf16[256,1152]{1,0:T(8,128)(2,1)}, bf16[256,1152]{1,0:T(8,128)(2,1)}) custom-call(bf16[256,1152]{1,0:T(8,128)(2,1)} %collective-permute-done.40.refs_0_.refs_9_, bf16[256,1152]{1,0:T(8,128)(2,1)} %get-tuple-element.395.refs_1_.refs_13_, bf16[2304,1152]{1,0:T(8,128)(2,1)} %bitcast.121, ...), custom_call_target="tpu_custom_call" | custom-call | flops 1000 | bytes 1000 | tf_op jit(solution)/shard_map/mlp_core/pallas_call | solution.py:212
  319.0 5.4 collective-permute-done.38.refs_1_.refs_14_
  324.4 12.2 %mlp_grads.1 = bf16[2304,1152]{1,0:T(8,128)(2,1)} custom-call(bf16[256,1152]{1,0:T(8,128)(2,1)} %get-tuple-element.323.refs_0_, bf16[512,1152]{1,0:T(8,128)(2,1)} %get-tuple-element.324.refs_1_, bf16[256,1152]{1,0:T(8,128)(2,1)} %get-tuple-element.325.refs_2_, bf16[256,1152]{1,0:T(8,128)(2,1)} %get-tuple-element.264.refs_6_.refs_0_.refs_3_, ...), custom_call_target="tpu_custom_call" | custom-call | flops 1000 | bytes 1000 | tf_op jit(solution)/shard_map/mlp_grads/pallas_call | solution.py:630
  336.7 8.1 %collective-permute-start.39 = (bf16[256,1152]{1,0:T(8,128)(2,1)}, bf16[256,1152]{1,0:T(8,128)(2,1)}, u32[]{:S(2)}, u32[]{:S(2)}) collective-permute-start(bf16[256,1152]{1,0:T(8,128)(2,1)} %get-tuple-element.266), channel_id=1, source_target_pairs={{0,1},{1,2},{2,3},{3,0},{4,5},{5,6},{6,7},{7,4},{8,9},{9,10},{10,1... | collective-permute-start | bytes 1769480 | tf_op jit(solution)/shard_map/ppermute | solution.py:58
  348.2 9.8 %mlp_out.1 = (bf16[4,256,1152]{2,1,0:T(8,128)(2,1)}, f32[2,1152]{1,0:T(2,128)}) custom-call(s32[2]{0:T(128)} %copy-done.10, bf16[256,1152]{1,0:T(8,128)(2,1)} %get-tuple-element.264.refs_6_.refs_0_.refs_3_, bf16[512,1152]{1,0:T(8,128)(2,1)} %get-tuple-element.268.refs_4_.refs_1_, bf16[256,1152]{1,0:T(8,128)(2,1)} %get-tuple-element.270.refs_2_.refs_5_, ...), custom_call_target="tpu_custom_call" | custom-call | flops 1000 | bytes 1000 | tf_op jit(solution)/shard_map/mlp_out/pallas_call | solution.py:668
  357.9 4.2 collective-permute-done.39.refs_2_
  362.1 24.6 %collective-permute-done.41.refs_3_ = bf16[256,1152]{1,0:T(8,128)(2,1)} collective-permute-done((bf16[256,1152]{1,0:T(8,128)(2,1)}, bf16[256,1152]{1,0:T(8,128)(2,1)}, u32[]{:S(2)}, u32[]{:S(2)}) %collective-permute-start.41) | collective-permute-done | bytes 589856 | tf_op jit(solution)/shard_map/ppermute | solution.py:58
  386.7 14.1 %cross_back.1 = (f32[256,1152]{1,0:T(8,128)}, bf16[256,1152]{1,0:T(8,128)(2,1)}, bf16[256,1152]{1,0:T(8,128)(2,1)}, bf16[256,1152]{1,0:T(8,128)(2,1)}, bf16[120,...) custom-call(s32[2]{0:T(128)} %copy-done.10, ...), custom_call_target="tpu_custom_call" | custom-call | flops 10000000000 | bytes 10000000 | tf_op jit(solution)/shard_map/cross_back/pallas_call | solution.py:497
  400.9 7.1 %full_grads.1 = (bf16[2,4,288,1152]{3,2,1,0:T(8,128)(2,1)}, bf16[2,4,288,1152]{3,2,1,0:T(8,128)(2,1)}) custom-call(s32[2]{0:T(128)} %copy-done.10, bf16[376,288]{1,0:T(8,128)(2,1)} %get-tuple-element.247.refs_0_, bf16[376,288]{1,0:T(8,128)(2,1)} %collective-permute-done.29.refs_1_, bf16[376,288]{1,0:T(8,128)(2,1)} %collective-permute-done.30.refs_2_, ...), custom_call_target="tpu_custom_call" | custom-call | flops 1000 | bytes 1000 | tf_op jit(solution)/shard_map/full_grads/pallas_call | solution.py:580
  408.4 3.7 collective-permute-start.44
  412.1 8.0 %collective-permute-done.42.refs_1_ = bf16[376,288]{1,0:T(8,128)(2,1)S(1)} collective-permute-done((bf16[376,288]{1,0:T(8,128)(2,1)}, bf16[376,288]{1,0:T(8,128)(2,1)S(1)}, u32[]{:S(2)}, u32[]{:S(2)}) %collective-permute-start.42) | collective-permute-done | bytes 216608 | tf_op jit(solution)/shard_map/ppermute | solution.py:58
  420.7 10.6 %collective-permute-done.43.refs_2_ = bf16[376,288]{1,0:T(8,128)(2,1)S(1)} collective-permute-done((bf16[376,288]{1,0:T(8,128)(2,1)S(1)}, bf16[376,288]{1,0:T(8,128)(2,1)S(1)}, u32[]{:S(2)}, u32[]{:S(2)}) %collective-permute-start.43) | collective-permute-done | bytes 216608 | tf_op jit(solution)/shard_map/ppermute | solution.py:58
  433.4 7.6 %sum_split.1 = (bf16[4,2,72,1152]{3,2,1,0:T(8,128)(2,1)}, bf16[4,2,72,1152]{3,2,1,0:T(8,128)(2,1)}, bf16[4,2,72,1152]{3,2,1,0:T(8,128)(2,1)}, bf16[4,2,72,1152]{3,2,1,0:T(8,128)(2,1)}) custom-call(s32[2]{0:T(128)} %pad_add_fusion.2.place_ref, bf16[2,4,2,2,72,1152]{5,4,3,2,1,0:T(8,128)(2,1)} %bitcast.151, bf16[2,4,2,2,72,1152]{5,4,3,2,1,0:T(8,128)(2,1)} %bitcast.31.two), custom_call_target="tpu_custom_call" | custom-call | flops 10000000000 | bytes 10000000 | tf_op jit(solution)/shard_map/sum_split/pallas_call | solution.py:698
  446.9 5.8 self_attend_back.2.refs_0_
  452.7 18.7 %collective-permute-done.46 = bf16[4,2,72,1152]{3,2,1,0:T(8,128)(2,1)} collective-permute-done((bf16[4,2,72,1152]{3,2,1,0:T(8,128)(2,1)}, bf16[4,2,72,1152]{3,2,1,0:T(8,128)(2,1)}, u32[]{:S(2)}, u32[]{:S(2)}) %collective-permute-start.46) | collective-permute-done | bytes 1327136 | tf_op jit(solution)/shard_map/ppermute | solution.py:780
  480.1 6.0 self_attend_back.3.refs_1_
  487.2 5.5 collective-permute-done.48
  499.8 6.2 %attn_grads.1 = (bf16[2,1,288,1152]{3,2,1,0:T(8,128)(2,1)}, bf16[2,1,288,1152]{3,2,1,0:T(8,128)(2,1)}) custom-call(s32[2]{0:T(128)} %copy-done.10, bf16[1024,432]{1,0:T(8,128)(2,1)} %copy-done.16, bf16[1024,432]{1,0:T(8,128)(2,1)} %copy-done.17, bf16[1024,1152]{1,0:T(8,128)(2,1)} %copy-done.11, bf16[120,288]{1,0:T(8,128)(2,1)} %add_convert_fusion.1.refs_3_, ...), custom_call_target="tpu_custom_call" | custom-call | flops 10000000000 | bytes 10000000 | tf_op jit(solution)/shard_map/attn_grads/pallas_call | solution.py:580
  506.1 7.3 %collective-permute-start.55 = (bf16[2,72,1152]{2,1,0:T(8,128)(2,1)}, bf16[2,72,1152]{2,1,0:T(8,128)(2,1)S(1)}, u32[]{:S(2)}, u32[]{:S(2)}) collective-permute-start(bf16[2,72,1152]{2,1,0:T(8,128)(2,1)} %get-tuple-element.350), channel_id=1, source_target_pairs={{0,1},{1,2},{2,3},{3,0},{4,5},{5,6},{6,7},{7,4},{8,9},{9,10},{10,1... | collective-permute-start | bytes 995336 | tf_op jit(solution)/shard_map/ppermute | solution.py:58
  515.9 9.5 %attn_terms.1 = (bf16[4,256,1152]{2,1,0:T(8,128)(2,1)}, f32[2,1152]{1,0:T(2,128)}) custom-call(s32[2]{0:T(128)} %copy-done.10, bf16[1024,432]{1,0:T(8,128)(2,1)} %copy-done.16, bf16[1024,432]{1,0:T(8,128)(2,1)} %copy-done.17, bf16[1152,1152]{1,0:T(8,128)(2,1)} %bitcast.128, bf16[256,1152]{1,0:T(8,128)(2,1)} %copy-done.2, bf16[256,1152]{1,0:T(8,128)(2,1)} %copy-done.13, ...), custom_call_target="tpu_custom_call" | custom-call | flops 10000000000 | bytes 10000000 | tf_op jit(solution)/shard_map/attn_terms/pallas_call | solution.py:668
  536.4 7.4 %collective-permute-done.52 = bf16[2,72,1152]{2,1,0:T(8,128)(2,1)S(1)} collective-permute-done((bf16[2,72,1152]{2,1,0:T(8,128)(2,1)S(1)}, bf16[2,72,1152]{2,1,0:T(8,128)(2,1)S(1)}, u32[]{:S(2)}, u32[]{:S(2)}) %collective-permute-start.52) | collective-permute-done | bytes 331808 | tf_op jit(solution)/shard_map/ppermute | solution.py:780
  566.5 5.2 collective-permute-done.66
  571.7 4.0 collective-permute-done.64
  583.2 16.8 %update_slots.1 = (f32[16,72,1152]{2,1,0:T(8,128)}, f32[16,72,1152]{2,1,0:T(8,128)}, f32[16,72,1152]{2,1,0:T(8,128)}) custom-call(s32[16]{0:T(128)} %convert_element_type.102.filled_ref, s32[16]{0:T(128)} %get-tuple-element.457.which_ref, s32[16]{0:T(128)} %get-tuple-element.456.position_ref, f32[16,72,1152]{2,1,0:T(8,128)} %weight.1, f32[16,72,1152]{2,1,0:T(8,128)} %one.1, ...), custom_call_target="tpu_custom_call" | custom-call | flops 1000 | bytes 1000 | tf_op jit(solution)/shard_map/update_slots/pallas_call | solution.py:750
  600.0 3.8 reduce-scatter.11.cloned.1.call-done
  (378 shorter events, 166.0 us)
Async XLA Ops:
  7.2 98.2 %reduce-scatter.5.cloned.1.call-start = ((), (), s32[]{:S(2)}) async-start(), calls=%async_computation.4 | async-start | bytes 5971968 | tf_op jit(solution)/shard_map/reduce_scatter | solution.py:1056
  21.1 152.5 %all-gather.6.cloned.1.call-start = ((), (), s32[]{:S(2)}) async-start(), calls=%async_computation.5 | async-start | bytes 5971968 | tf_op jit(solution)/shard_map/all_gather | solution.py:1082
  21.1 21.6 %collective-permute-start = (bf16[16,72,1152]{2,1,0:T(8,128)(2,1)}, bf16[16,72,1152]{2,1,0:T(8,128)(2,1)}, u32[]{:S(2)}, u32[]{:S(2)}) collective-permute-start(bf16[16,72,1152]{2,1,0:T(8,128)(2,1)} %get-tuple-element.199), channel_id=1, source_target_pairs={{0,4},{4,0},{8,12},{12,8},{16,20},{20,16},{24,28},{28,24},{1,5},{5... | collective-permute-start | bytes 7962632 | tf_op jit(solution)/shard_map/ppermute | solution.py:780
  22.9 18.6 %collective-permute-start.2 = (bf16[256,1152]{1,0:T(8,128)(2,1)S(1)}, bf16[256,1152]{1,0:T(8,128)(2,1)S(1)}, u32[]{:S(2)}, u32[]{:S(2)}) collective-permute-start(bf16[256,1152]{1,0:T(8,128)(2,1)S(1)} %fusion.6.refs_0_.refs_3_), channel_id=1, source_target_pairs={{1,0},{2,1},{3,2},{5,4},{6,5},{7,6},{9,8},{10,9},{11,10},{13,12},{... | collective-permute-start | bytes 1769480 | tf_op jit(solution)/shard_map/ppermute | solution.py:930
  24.2 18.5 %collective-permute-start.1 = (bf16[256,1152]{1,0:T(8,128)(2,1)S(1)}, bf16[256,1152]{1,0:T(8,128)(2,1)}, u32[]{:S(2)}, u32[]{:S(2)}) collective-permute-start(bf16[256,1152]{1,0:T(8,128)(2,1)S(1)} %fusion.6.refs_0_.refs_3_), channel_id=1, source_target_pairs={{0,1},{1,2},{2,3},{4,5},{5,6},{6,7},{8,9},{9,10},{10,11},{12,13},{... | collective-permute-start | bytes 1769480 | tf_op jit(solution)/shard_map/ppermute | solution.py:930
  46.9 40.3 %collective-permute-start.5 = (bf16[256,1152]{1,0:T(8,128)(2,1)}, bf16[256,1152]{1,0:T(8,128)(2,1)}, u32[]{:S(2)}, u32[]{:S(2)}) collective-permute-start(bf16[256,1152]{1,0:T(8,128)(2,1)} %collective-permute-done.1.refs_1_), channel_id=1, source_target_pairs={{1,2},{2,3},{5,6},{6,7},{9,10},{10,11},{13,14},{14,15},{17,18},{18... | collective-permute-start | bytes 1769480 | tf_op jit(solution)/shard_map/ppermute | solution.py:930
  48.3 38.9 %collective-permute-start.6 = (bf16[256,1152]{1,0:T(8,128)(2,1)S(1)}, bf16[256,1152]{1,0:T(8,128)(2,1)}, u32[]{:S(2)}, u32[]{:S(2)}) collective-permute-start(bf16[256,1152]{1,0:T(8,128)(2,1)S(1)} %collective-permute-done.2.refs_4_), channel_id=1, source_target_pairs={{1,0},{2,1},{5,4},{6,5},{9,8},{10,9},{13,12},{14,13},{17,16},{18,1... | collective-permute-start | bytes 1769480 | tf_op jit(solution)/shard_map/ppermute | solution.py:930
  49.6 37.6 %collective-permute-start.3 = (bf16[4,72,1152]{2,1,0:T(8,128)(2,1)}, bf16[4,72,1152]{2,1,0:T(8,128)(2,1)}, u32[]{:S(2)}, u32[]{:S(2)}) collective-permute-start(bf16[4,72,1152]{2,1,0:T(8,128)(2,1)} %get-tuple-element.203), channel_id=1, source_target_pairs={{0,8},{4,12},{8,0},{12,4},{16,24},{20,28},{24,16},{28,20},{1,9},{5... | collective-permute-start | bytes 1990664 | tf_op jit(solution)/shard_map/ppermute | solution.py:780
  51.8 35.4 %collective-permute-start.4 = (bf16[4,72,1152]{2,1,0:T(8,128)(2,1)}, bf16[4,72,1152]{2,1,0:T(8,128)(2,1)}, u32[]{:S(2)}, u32[]{:S(2)}) collective-permute-start(bf16[4,72,1152]{2,1,0:T(8,128)(2,1)} %get-tuple-element.205), channel_id=1, source_target_pairs={{0,16},{4,20},{8,24},{12,28},{16,0},{20,4},{24,8},{28,12},{1,17},{... | collective-permute-start | bytes 1990664 | tf_op jit(solution)/shard_map/ppermute | solution.py:780
  56.9 30.2 %collective-permute-start.7 = (bf16[4,120,288]{1,2,0:T(8,128)(2,1)S(1)}, bf16[4,120,288]{1,2,0:T(8,128)(2,1)S(1)}, u32[]{:S(2)}, u32[]{:S(2)}) collective-permute-start(bf16[4,120,288]{1,2,0:T(8,128)(2,1)S(1)} %copy.61), channel_id=1, source_target_pairs={{0,16},{4,20},{8,24},{12,28},{16,0},{20,4},{24,8},{28,12},{1,17},{... | collective-permute-start | bytes 829448 | tf_op jit(solution)/shard_map/ppermute | solution.py:780
  89.2 16.2 %collective-permute-start.11 = (bf16[256,1152]{1,0:T(8,128)(2,1)}, bf16[256,1152]{1,0:T(8,128)(2,1)S(1)}, u32[]{:S(2)}, u32[]{:S(2)}) collective-permute-start(bf16[256,1152]{1,0:T(8,128)(2,1)} %collective-permute-done.6.refs_5_), channel_id=1, source_target_pairs={{1,0},{5,4},{9,8},{13,12},{17,16},{21,20},{25,24},{29,28}} | collective-permute-start | bytes 1769480 | tf_op jit(solution)/shard_map/ppermute | solution.py:930
  105.4 140.3 %all-gather.10.cloned.1.call-start = ((), (), s32[]{:S(2)}) async-start(), calls=%async_computation.10 | async-start | bytes 2949120 | tf_op jit(solution)/shard_map/all_gather | solution.py:1097
  109.6 30.7 %collective-permute-start.20 = (bf16[2,72,1152]{2,1,0:T(8,128)(2,1)S(1)}, bf16[2,72,1152]{2,1,0:T(8,128)(2,1)S(1)}, u32[]{:S(2)}, u32[]{:S(2)}) collective-permute-start(bf16[2,72,1152]{2,1,0:T(8,128)(2,1)S(1)} %add.300.refs_0_), channel_id=1, source_target_pairs={{0,3},{1,0},{2,1},{3,2},{4,7},{5,4},{6,5},{7,6},{8,11},{9,8},{10,9... | collective-permute-start | bytes 995336 | tf_op jit(solution)/shard_map/ppermute | solution.py:58
  112.4 27.9 %collective-permute-start.19 = (bf16[2,72,1152]{2,1,0:T(8,128)(2,1)S(1)}, bf16[2,72,1152]{2,1,0:T(8,128)(2,1)S(1)}, u32[]{:S(2)}, u32[]{:S(2)}) collective-permute-start(bf16[2,72,1152]{2,1,0:T(8,128)(2,1)S(1)} %add.300.refs_0_), channel_id=1, source_target_pairs={{0,2},{1,3},{2,0},{3,1},{4,6},{5,7},{6,4},{7,5},{8,10},{9,11},{10,... | collective-permute-start | bytes 995336 | tf_op jit(solution)/shard_map/ppermute | solution.py:58
  112.4 29.3 %collective-permute-start.18 = (bf16[2,72,1152]{2,1,0:T(8,128)(2,1)S(1)}, bf16[2,72,1152]{2,1,0:T(8,128)(2,1)}, u32[]{:S(2)}, u32[]{:S(2)}) collective-permute-start(bf16[2,72,1152]{2,1,0:T(8,128)(2,1)S(1)} %add.300.refs_0_), channel_id=1, source_target_pairs={{0,1},{1,2},{2,3},{3,0},{4,5},{5,6},{6,7},{7,4},{8,9},{9,10},{10,1... | collective-permute-start | bytes 995336 | tf_op jit(solution)/shard_map/ppermute | solution.py:58
  114.5 16.1 %collective-permute-start.14 = (bf16[2,72,1152]{2,1,0:T(8,128)(2,1)S(1)}, bf16[2,72,1152]{2,1,0:T(8,128)(2,1)S(1)}, u32[]{:S(2)}, u32[]{:S(2)}) collective-permute-start(bf16[2,72,1152]{2,1,0:T(8,128)(2,1)S(1)} %pad_maximum_fusion.8), channel_id=1, source_target_pairs={{0,16},{4,20},{8,24},{12,28},{16,0},{20,4},{24,8},{28,12},{1,17},{... | collective-permute-start | bytes 995336 | tf_op jit(solution)/shard_map/ppermute | solution.py:780
  144.2 29.3 %collective-permute-start.26 = (bf16[120,288]{0,1:T(8,128)(2,1)S(1)}, bf16[120,288]{0,1:T(8,128)(2,1)S(1)}, u32[]{:S(2)}, u32[]{:S(2)}) collective-permute-start(bf16[120,288]{0,1:T(8,128)(2,1)S(1)} %bitcast_add_fusion), channel_id=1, source_target_pairs={{0,3},{1,0},{2,1},{3,2},{4,7},{5,4},{6,5},{7,6},{8,11},{9,8},{10,9... | collective-permute-start | bytes 207368 | tf_op jit(solution)/shard_map/ppermute | solution.py:58
  147.7 25.8 %collective-permute-start.25 = (bf16[120,288]{0,1:T(8,128)(2,1)S(1)}, bf16[120,288]{0,1:T(8,128)(2,1)S(1)}, u32[]{:S(2)}, u32[]{:S(2)}) collective-permute-start(bf16[120,288]{0,1:T(8,128)(2,1)S(1)} %bitcast_add_fusion), channel_id=1, source_target_pairs={{0,2},{1,3},{2,0},{3,1},{4,6},{5,7},{6,4},{7,5},{8,10},{9,11},{10,... | collective-permute-start | bytes 207368 | tf_op jit(solution)/shard_map/ppermute | solution.py:58
  148.2 20.6 %collective-permute-start.22 = (bf16[4,72,1152]{2,1,0:T(8,128)(2,1)}, bf16[4,72,1152]{2,1,0:T(8,128)(2,1)}, u32[]{:S(2)}, u32[]{:S(2)}) collective-permute-start(bf16[4,72,1152]{2,1,0:T(8,128)(2,1)} %get-tuple-element.230), channel_id=1, source_target_pairs={{0,8},{4,12},{8,0},{12,4},{16,24},{20,28},{24,16},{28,20},{1,9},{5... | collective-permute-start | bytes 1990664 | tf_op jit(solution)/shard_map/ppermute | solution.py:780
  149.9 21.2 %collective-permute-start.23 = (bf16[4,72,1152]{2,1,0:T(8,128)(2,1)}, bf16[4,72,1152]{2,1,0:T(8,128)(2,1)}, u32[]{:S(2)}, u32[]{:S(2)}) collective-permute-start(bf16[4,72,1152]{2,1,0:T(8,128)(2,1)} %get-tuple-element.231), channel_id=1, source_target_pairs={{0,16},{4,20},{8,24},{12,28},{16,0},{20,4},{24,8},{28,12},{1,17},{... | collective-permute-start | bytes 1990664 | tf_op jit(solution)/shard_map/ppermute | solution.py:780
  150.3 343.7 %reduce-scatter.7.cloned.1.call-start = ((), (), s32[]{:S(2)}) async-start(), calls=%async_computation.6 | async-start | bytes 5971968 | tf_op jit(solution)/shard_map/reduce_scatter | solution.py:1218
  173.5 57.1 %collective-permute-start.27 = (bf16[8,72,1152]{2,1,0:T(8,128)(2,1)}, bf16[8,72,1152]{2,1,0:T(8,128)(2,1)}, u32[]{:S(2)}, u32[]{:S(2)}) collective-permute-start(bf16[8,72,1152]{2,1,0:T(8,128)(2,1)} %pad_maximum_fusion.rest_0_), channel_id=1, source_target_pairs={{0,16},{4,20},{8,24},{12,28},{16,0},{20,4},{24,8},{28,12},{1,17},{... | collective-permute-start | bytes 3981320 | tf_op jit(solution)/shard_map/ppermute | solution.py:780
  175.1 55.6 %collective-permute-start.28 = (bf16[8,72,1152]{2,1,0:T(8,128)(2,1)}, bf16[8,72,1152]{2,1,0:T(8,128)(2,1)}, u32[]{:S(2)}, u32[]{:S(2)}) collective-permute-start(bf16[8,72,1152]{2,1,0:T(8,128)(2,1)} %pad_maximum_fusion.1.rest_2_), channel_id=1, source_target_pairs={{0,8},{4,12},{8,0},{12,4},{16,24},{20,28},{24,16},{28,20},{1,9},{5... | collective-permute-start | bytes 3981320 | tf_op jit(solution)/shard_map/ppermute | solution.py:780
  182.0 17.8 %collective-permute-start.31 = (bf16[376,288]{1,0:T(8,128)(2,1)S(1)}, bf16[376,288]{1,0:T(8,128)(2,1)}, u32[]{:S(2)}, u32[]{:S(2)}) collective-permute-start(bf16[376,288]{1,0:T(8,128)(2,1)S(1)} %get-tuple-element.450), channel_id=1, source_target_pairs={{0,1},{1,2},{2,3},{3,0},{4,5},{5,6},{6,7},{7,4},{8,9},{9,10},{10,1... | collective-permute-start | bytes 649736 | tf_op jit(solution)/shard_map/ppermute | solution.py:58
  184.3 26.3 %collective-permute-start.29 = (bf16[376,288]{1,0:T(8,128)(2,1)S(1)}, bf16[376,288]{1,0:T(8,128)(2,1)}, u32[]{:S(2)}, u32[]{:S(2)}) collective-permute-start(bf16[376,288]{1,0:T(8,128)(2,1)S(1)} %get-tuple-element.451), channel_id=1, source_target_pairs={{0,3},{1,0},{2,1},{3,2},{4,7},{5,4},{6,5},{7,6},{8,11},{9,8},{10,9... | collective-permute-start | bytes 649736 | tf_op jit(solution)/shard_map/ppermute | solution.py:58
  186.1 44.6 %collective-permute-start.30 = (bf16[376,288]{1,0:T(8,128)(2,1)S(1)}, bf16[376,288]{1,0:T(8,128)(2,1)}, u32[]{:S(2)}, u32[]{:S(2)}) collective-permute-start(bf16[376,288]{1,0:T(8,128)(2,1)S(1)} %get-tuple-element.452), channel_id=1, source_target_pairs={{0,2},{1,3},{2,0},{3,1},{4,6},{5,7},{6,4},{7,5},{8,10},{9,11},{10,... | collective-permute-start | bytes 649736 | tf_op jit(solution)/shard_map/ppermute | solution.py:58
  199.8 34.0 %collective-permute-start.32 = (bf16[8,72,1152]{2,1,0:T(8,128)(2,1)}, bf16[8,72,1152]{2,1,0:T(8,128)(2,1)}, u32[]{:S(2)}, u32[]{:S(2)}) collective-permute-start(bf16[8,72,1152]{2,1,0:T(8,128)(2,1)} %pad_maximum_fusion.rest_0_), channel_id=1, source_target_pairs={{0,4},{4,0},{8,12},{12,8},{16,20},{20,16},{24,28},{28,24},{1,5},{5... | collective-permute-start | bytes 3981320 | tf_op jit(solution)/shard_map/ppermute | solution.py:780
  210.5 23.3 %collective-permute-start.34 = (bf16[8,72,1152]{2,1,0:T(8,128)(2,1)}, bf16[8,72,1152]{2,1,0:T(8,128)(2,1)}, u32[]{:S(2)}, u32[]{:S(2)}) collective-permute-start(bf16[8,72,1152]{2,1,0:T(8,128)(2,1)} %pad_maximum_fusion.1.rest_2_), channel_id=1, source_target_pairs={{0,4},{4,0},{8,12},{12,8},{16,20},{20,16},{24,28},{28,24},{1,5},{5... | collective-permute-start | bytes 3981320 | tf_op jit(solution)/shard_map/ppermute | solution.py:780
  258.9 28.5 %collective-permute-start.37 = (bf16[256,1152]{1,0:T(8,128)(2,1)}, bf16[256,1152]{1,0:T(8,128)(2,1)}, u32[]{:S(2)}, u32[]{:S(2)}) collective-permute-start(bf16[256,1152]{1,0:T(8,128)(2,1)} %get-tuple-element.267.refs_0_.refs_6_), channel_id=1, source_target_pairs={{0,3},{1,0},{2,1},{3,2},{4,7},{5,4},{6,5},{7,6},{8,11},{9,8},{10,9... | collective-permute-start | bytes 1769480 | tf_op jit(solution)/shard_map/ppermute | solution.py:58
  259.8 27.6 %collective-permute-start.36 = (bf16[256,1152]{1,0:T(8,128)(2,1)}, bf16[256,1152]{1,0:T(8,128)(2,1)}, u32[]{:S(2)}, u32[]{:S(2)}) collective-permute-start(bf16[256,1152]{1,0:T(8,128)(2,1)} %get-tuple-element.267.refs_0_.refs_6_), channel_id=1, source_target_pairs={{0,1},{1,2},{2,3},{3,0},{4,5},{5,6},{6,7},{7,4},{8,9},{9,10},{10,1... | collective-permute-start | bytes 1769480 | tf_op jit(solution)/shard_map/ppermute | solution.py:58
  272.4 39.5 %collective-permute-start.40 = (bf16[256,1152]{1,0:T(8,128)(2,1)}, bf16[256,1152]{1,0:T(8,128)(2,1)}, u32[]{:S(2)}, u32[]{:S(2)}) collective-permute-start(bf16[256,1152]{1,0:T(8,128)(2,1)} %get-tuple-element.267.refs_0_.refs_6_), channel_id=1, source_target_pairs={{0,2},{1,3},{2,0},{3,1},{4,6},{5,7},{6,4},{7,5},{8,10},{9,11},{10,... | collective-permute-start | bytes 1769480 | tf_op jit(solution)/shard_map/ppermute | solution.py:58
  299.2 25.2 %collective-permute-start.38 = (bf16[256,1152]{1,0:T(8,128)(2,1)}, bf16[256,1152]{1,0:T(8,128)(2,1)}, u32[]{:S(2)}, u32[]{:S(2)}) collective-permute-start(bf16[256,1152]{1,0:T(8,128)(2,1)} %get-tuple-element.265), channel_id=1, source_target_pairs={{0,3},{1,0},{2,1},{3,2},{4,7},{5,4},{6,5},{7,6},{8,11},{9,8},{10,9... | collective-permute-start | bytes 1769480 | tf_op jit(solution)/shard_map/ppermute | solution.py:58
  336.6 189.6 %reduce-scatter.9.cloned.1.call-start = ((), (), s32[]{:S(2)}) async-start(), calls=%async_computation.7 | async-start | bytes 2949120 | tf_op jit(solution)/shard_map/reduce_scatter | solution.py:1289
  336.7 25.5 %collective-permute-start.39 = (bf16[256,1152]{1,0:T(8,128)(2,1)}, bf16[256,1152]{1,0:T(8,128)(2,1)}, u32[]{:S(2)}, u32[]{:S(2)}) collective-permute-start(bf16[256,1152]{1,0:T(8,128)(2,1)} %get-tuple-element.266), channel_id=1, source_target_pairs={{0,1},{1,2},{2,3},{3,0},{4,5},{5,6},{6,7},{7,4},{8,9},{9,10},{10,1... | collective-permute-start | bytes 1769480 | tf_op jit(solution)/shard_map/ppermute | solution.py:58
  344.8 41.9 %collective-permute-start.41 = (bf16[256,1152]{1,0:T(8,128)(2,1)}, bf16[256,1152]{1,0:T(8,128)(2,1)}, u32[]{:S(2)}, u32[]{:S(2)}) collective-permute-start(bf16[256,1152]{1,0:T(8,128)(2,1)} %get-tuple-element.269), channel_id=1, source_target_pairs={{0,2},{1,3},{2,0},{3,1},{4,6},{5,7},{6,4},{7,5},{8,10},{9,11},{10,... | collective-permute-start | bytes 1769480 | tf_op jit(solution)/shard_map/ppermute | solution.py:58
  408.0 24.7 %collective-permute-start.45 = (bf16[2,4,288,1152]{3,2,1,0:T(8,128)(2,1)}, bf16[2,4,288,1152]{3,2,1,0:T(8,128)(2,1)}, u32[]{:S(2)}, u32[]{:S(2)}) collective-permute-start(bf16[2,4,288,1152]{3,2,1,0:T(8,128)(2,1)} %get-tuple-element.293), channel_id=1, source_target_pairs={{0,4},{4,0},{8,12},{12,8},{16,20},{20,16},{24,28},{28,24},{1,5},{5... | collective-permute-start | bytes 15925256 | tf_op jit(solution)/shard_map/ppermute | solution.py:780
  408.2 23.1 %collective-permute-start.43 = (bf16[376,288]{1,0:T(8,128)(2,1)S(1)}, bf16[376,288]{1,0:T(8,128)(2,1)S(1)}, u32[]{:S(2)}, u32[]{:S(2)}) collective-permute-start(bf16[376,288]{1,0:T(8,128)(2,1)S(1)} %copy-done.68), channel_id=1, source_target_pairs={{0,2},{1,3},{2,0},{3,1},{4,6},{5,7},{6,4},{7,5},{8,10},{9,11},{10,... | collective-permute-start | bytes 649736 | tf_op jit(solution)/shard_map/ppermute | solution.py:58
  408.4 23.6 %collective-permute-start.44 = (bf16[376,288]{1,0:T(8,128)(2,1)S(1)}, bf16[376,288]{1,0:T(8,128)(2,1)S(1)}, u32[]{:S(2)}, u32[]{:S(2)}) collective-permute-start(bf16[376,288]{1,0:T(8,128)(2,1)S(1)} %copy-done.67), channel_id=1, source_target_pairs={{0,3},{1,0},{2,1},{3,2},{4,7},{5,4},{6,5},{7,6},{8,11},{9,8},{10,9... | collective-permute-start | bytes 649736 | tf_op jit(solution)/shard_map/ppermute | solution.py:58
  432.7 119.6 %all-gather.8.cloned.1.call-start = ((), (), s32[]{:S(2)}) async-start(), calls=%async_computation.9 | async-start | bytes 5971968 | tf_op jit(solution)/shard_map/all_gather | solution.py:1312
  441.0 30.3 %collective-permute-start.46 = (bf16[4,2,72,1152]{3,2,1,0:T(8,128)(2,1)}, bf16[4,2,72,1152]{3,2,1,0:T(8,128)(2,1)}, u32[]{:S(2)}, u32[]{:S(2)}) collective-permute-start(bf16[4,2,72,1152]{3,2,1,0:T(8,128)(2,1)} %get-tuple-element.298), channel_id=1, source_target_pairs={{0,8},{4,12},{8,0},{12,4},{16,24},{20,28},{24,16},{28,20},{1,9},{5... | collective-permute-start | bytes 3981320 | tf_op jit(solution)/shard_map/ppermute | solution.py:780
  442.6 30.0 %collective-permute-start.47 = (bf16[4,2,72,1152]{3,2,1,0:T(8,128)(2,1)}, bf16[4,2,72,1152]{3,2,1,0:T(8,128)(2,1)}, u32[]{:S(2)}, u32[]{:S(2)}) collective-permute-start(bf16[4,2,72,1152]{3,2,1,0:T(8,128)(2,1)} %get-tuple-element.300), channel_id=1, source_target_pairs={{0,16},{4,20},{8,24},{12,28},{16,0},{20,4},{24,8},{28,12},{1,17},{... | collective-permute-start | bytes 3981320 | tf_op jit(solution)/shard_map/ppermute | solution.py:780
  478.0 14.7 %collective-permute-start.48 = (bf16[4,72,1152]{2,1,0:T(8,128)(2,1)S(1)}, bf16[4,72,1152]{2,1,0:T(8,128)(2,1)}, u32[]{:S(2)}, u32[]{:S(2)}) collective-permute-start(bf16[4,72,1152]{2,1,0:T(8,128)(2,1)S(1)} %get-tuple-element.315), channel_id=1, source_target_pairs={{0,16},{4,20},{8,24},{12,28},{16,0},{20,4},{24,8},{28,12},{1,17},{... | collective-permute-start | bytes 1990664 | tf_op jit(solution)/shard_map/ppermute | solution.py:780
  479.5 14.4 %collective-permute-start.49 = (bf16[4,72,1152]{2,1,0:T(8,128)(2,1)S(1)}, bf16[4,72,1152]{2,1,0:T(8,128)(2,1)}, u32[]{:S(2)}, u32[]{:S(2)}) collective-permute-start(bf16[4,72,1152]{2,1,0:T(8,128)(2,1)S(1)} %get-tuple-element.317), channel_id=1, source_target_pairs={{0,8},{4,12},{8,0},{12,4},{16,24},{20,28},{24,16},{28,20},{1,9},{5... | collective-permute-start | bytes 1990664 | tf_op jit(solution)/shard_map/ppermute | solution.py:780
  494.0 109.9 %reduce-scatter.11.cloned.1.call-start = ((), (), s32[]{:S(2)}) async-start(), calls=%async_computation.8 | async-start | bytes 2949120 | tf_op jit(solution)/shard_map/reduce_scatter | solution.py:1324
  506.0 20.2 %collective-permute-start.50 = (bf16[2,1,288,1152]{3,2,1,0:T(8,128)(2,1)}, bf16[2,1,288,1152]{3,2,1,0:T(8,128)(2,1)S(1)}, u32[]{:S(2)}, u32[]{:S(2)}) collective-permute-start(bf16[2,1,288,1152]{3,2,1,0:T(8,128)(2,1)} %get-tuple-element.335), channel_id=1, source_target_pairs={{0,4},{4,0},{8,12},{12,8},{16,20},{20,16},{24,28},{28,24},{1,5},{5... | collective-permute-start | bytes 3981320 | tf_op jit(solution)/shard_map/ppermute | solution.py:780
  506.1 29.2 %collective-permute-start.55 = (bf16[2,72,1152]{2,1,0:T(8,128)(2,1)}, bf16[2,72,1152]{2,1,0:T(8,128)(2,1)S(1)}, u32[]{:S(2)}, u32[]{:S(2)}) collective-permute-start(bf16[2,72,1152]{2,1,0:T(8,128)(2,1)} %get-tuple-element.350), channel_id=1, source_target_pairs={{0,1},{1,2},{2,3},{3,0},{4,5},{5,6},{6,7},{7,4},{8,9},{9,10},{10,1... | collective-permute-start | bytes 995336 | tf_op jit(solution)/shard_map/ppermute | solution.py:58
  513.5 22.9 %collective-permute-start.56 = (bf16[2,72,1152]{2,1,0:T(8,128)(2,1)}, bf16[2,72,1152]{2,1,0:T(8,128)(2,1)S(1)}, u32[]{:S(2)}, u32[]{:S(2)}) collective-permute-start(bf16[2,72,1152]{2,1,0:T(8,128)(2,1)} %get-tuple-element.351), channel_id=1, source_target_pairs={{0,2},{1,3},{2,0},{3,1},{4,6},{5,7},{6,4},{7,5},{8,10},{9,11},{10,... | collective-permute-start | bytes 995336 | tf_op jit(solution)/shard_map/ppermute | solution.py:58
  513.9 22.4 %collective-permute-start.57 = (bf16[2,72,1152]{2,1,0:T(8,128)(2,1)}, bf16[2,72,1152]{2,1,0:T(8,128)(2,1)S(1)}, u32[]{:S(2)}, u32[]{:S(2)}) collective-permute-start(bf16[2,72,1152]{2,1,0:T(8,128)(2,1)} %get-tuple-element.352), channel_id=1, source_target_pairs={{0,3},{1,0},{2,1},{3,2},{4,7},{5,4},{6,5},{7,6},{8,11},{9,8},{10,9... | collective-permute-start | bytes 995336 | tf_op jit(solution)/shard_map/ppermute | solution.py:58
  (97 other events, 1109.2 us)
Sparse Core Ops, SparseCore 0:
  21.2 72.0 reduce-scatter.4
  105.5 46.4 all-gather.5
  153.6 75.2 all-gather.9
  336.8 65.3 reduce-scatter.6
  432.9 51.1 reduce-scatter.8
  494.1 47.7 all-gather.7
  556.3 47.4 reduce-scatter.10

commit v2 on v1

--- a/solution.py
+++ b/solution.py
@@ -1201,7 +1201,7 @@
         acts,
         [h_slots[k] for k in order],
         [grad_slots[k] for k in order],
-        grad_terms[1:2],
+        grad_terms[1:],
     ).reshape(-1, unit_rows, width)
     hidden_share = w_mlp.shape[0] // 2
     pieces = [
@@ -1213,7 +1213,6 @@
         where, acts, order, pieces, w_mlp, [out_slots[k] for k in order], "mlp_out"
     )
     branch_row = branch_sums[1]
-    grad_terms, branch_terms = fence((grad_terms, branch_terms))
     if plane:
         mlp_sum = lax.psum_scatter(mlp_grad, "dp", scatter_dimension=0, tiled=True)
 

time: 624 us -> 613 us (0.982)
  starting transfers between devices: 90.2 us -> 78.1 us
    ppermute x21, starting transfers between devices: 41.2 us -> 30.1 us  [shift(): lax.ppermute(values, 'tensor', [(i, (i + step) % count) for i in range(co...]
    unnamed x147 -> x139, local copies, waits for them, and re-layouts: 18.9 us -> 16 us
  transfers between devices with their start and end apart: 75 -> 75, of which waited for: 39 -> 39; matrix products, arithmetic and copies ran while one was open for 10% -> 10% of each run, Pallas kernels for 22% -> 23%
where the time goes in v2:
time: 613 us; the launch traced here: 603 us
  waiting for transfers between devices  246 us (40%)
  Pallas kernels  171 us (28%)
  starting transfers between devices  78.1 us (13%)
  other arithmetic  45.2 us (7%)
  local copies, waits for them, and re-layouts  25.8 us (4%)
  between operations  15.6 us (3%)
  matrix products  11.6 us (2%)
  blocking collectives  10 us (2%)
    ppermute x21, waiting for transfers between devices, shift(): lax.ppermute(values, 'tensor', [(i, (i + step) % count) for i in range(co...  124 us
    ppermute x41, waiting for transfers between devices, swap(): return lax.ppermute(values, axis, [(i, i ^ 1 << bit) for i in range(count)])  115 us
    ppermute x41, starting transfers between devices, swap(): return lax.ppermute(values, axis, [(i, i ^ 1 << bit) for i in range(count)])  35 us
    ppermute x21, starting transfers between devices, shift(): lax.ppermute(values, 'tensor', [(i, (i + step) % count) for i in range(co...  30.1 us
    pallas_call x3, Pallas kernels, mlp_core(): pl.pallas_call(body, grid=(steps,), in_specs=[whole] * (2 * groups) + [pl...  25.9 us
    pallas_call x2, Pallas kernels, ranked_terms(): pl.pallas_call(body, in_specs=[in_smem()] + [in_vmem()] * (len(lefts) + 1...  18.9 us
    pallas_call x1, Pallas kernels, update_slots(): pl.pallas_call(body, grid_spec=pltpu.PrefetchScalarGridSpec(num_scalar_pr...  16.8 us
    unnamed x139, local copies, waits for them, and re-layouts  16 us
  transfers between devices with their start and end apart: 75, of which 39 were waited for; matrix products, arithmetic and copies ran while one was open for 10% of the time, Pallas kernels for 23%

profile of v2, /device:TPU:0, one launch (start us, length us, event | category | flops | bytes accessed | tf_op | source)
XLA Modules:
  0.0 603.4 jit_solution(11906998028921049639)
XLA Ops:
  12.8 4.3 pick_units.2
  17.1 4.5 pick_units.3
  24.7 6.4 %collective-permute-start.1 = (bf16[256,1152]{1,0:T(8,128)(2,1)S(1)}, bf16[256,1152]{1,0:T(8,128)(2,1)}, u32[]{:S(2)}, u32[]{:S(2)}) collective-permute-start(bf16[256,1152]{1,0:T(8,128)(2,1)S(1)} %fusion.6.refs_0_.refs_3_), channel_id=1, source_target_pairs={{0,1},{1,2},{2,3},{4,5},{5,6},{6,7},{8,9},{9,10},{10,11},{12,13},{... | collective-permute-start | bytes 1769480 | tf_op jit(solution)/shard_map/ppermute | solution.py:930
  31.1 10.0 %all-gather.1 = s32[8,1,120]{2,1,0:T(1,128)S(1)} all-gather(s32[1,1,120]{2,1,0:T(1,128)S(1)} %bitcast.150), channel_id=1, replica_groups=mesh['dp'=8,'tensor'=4] {'dp'}, dimensions={0}, use_global_device_ids=true | all-gather | bytes 4320 | tf_op jit(solution)/shard_map/all_gather | solution.py:1035
  42.7 4.1 slice_add_fusion
  53.7 3.2 fusion.10
  58.2 27.6 %collective-permute-done.7 = bf16[4,120,288]{1,2,0:T(8,128)(2,1)S(1)} collective-permute-done((bf16[4,120,288]{1,2,0:T(8,128)(2,1)S(1)}, bf16[4,120,288]{1,2,0:T(8,128)(2,1)S(1)}, u32[]{:S(2)}, u32[]{:S(2)}) %collective-permute-start.7) | collective-permute-done | bytes 276512 | tf_op jit(solution)/shard_map/ppermute | solution.py:780
  96.3 3.8 collective-permute-done.8
  114.2 8.5 %collective-permute-done.15 = bf16[1,72,1152]{2,1,0:T(8,128)(2,1)S(1)} collective-permute-done((bf16[1,72,1152]{2,1,0:T(8,128)(2,1)S(1)}, bf16[1,72,1152]{2,1,0:T(8,128)(2,1)S(1)}, u32[]{:S(2)}, u32[]{:S(2)}) %collective-permute-start.15) | collective-permute-done | bytes 165920 | tf_op jit(solution)/shard_map/ppermute | solution.py:780
  125.0 5.6 collective-permute-done.14
  144.1 3.2 collective-permute-start.26
  150.2 3.6 place_blocks.2
  153.9 5.5 convolution_convert_fusion.qkv_ref
  160.5 8.3 %self_attend.1 = (bf16[1024,288]{1,0:T(8,128)(2,1)S(1)}, f32[4,1024]{1,0:T(4,128)S(1)}) custom-call(bf16[1024,1152]{1,0:T(8,128)(2,1)S(1)} %convolution_convert_fusion.qkv_ref), custom_call_target="tpu_custom_call" | custom-call | flops 1000 | bytes 1000 | tf_op jit(solution)/shard_map/self_attend/pallas_call | solution.py:106
  185.5 13.7 %collective-permute-done.31.refs_3_ = bf16[376,288]{1,0:T(8,128)(2,1)} collective-permute-done((bf16[376,288]{1,0:T(8,128)(2,1)S(1)}, bf16[376,288]{1,0:T(8,128)(2,1)}, u32[]{:S(2)}, u32[]{:S(2)}) %collective-permute-start.31) | collective-permute-done | bytes 216608 | tf_op jit(solution)/shard_map/ppermute | solution.py:58
  199.2 11.6 %collective-permute-done.29.refs_1_ = bf16[376,288]{1,0:T(8,128)(2,1)} collective-permute-done((bf16[376,288]{1,0:T(8,128)(2,1)S(1)}, bf16[376,288]{1,0:T(8,128)(2,1)}, u32[]{:S(2)}, u32[]{:S(2)}) %collective-permute-start.29) | collective-permute-done | bytes 216608 | tf_op jit(solution)/shard_map/ppermute | solution.py:58
  210.8 17.9 %collective-permute-done.30.refs_2_ = bf16[376,288]{1,0:T(8,128)(2,1)} collective-permute-done((bf16[376,288]{1,0:T(8,128)(2,1)S(1)}, bf16[376,288]{1,0:T(8,128)(2,1)}, u32[]{:S(2)}, u32[]{:S(2)}) %collective-permute-start.30) | collective-permute-done | bytes 216608 | tf_op jit(solution)/shard_map/ppermute | solution.py:58
  233.9 9.7 %place_blocks.3 = (bf16[16,72,1152]{2,1,0:T(8,128)(2,1)}, bf16[16,72,1152]{2,1,0:T(8,128)(2,1)}, bf16[16,72,1152]{2,1,0:T(8,128)(2,1)}, bf16[16,72,1152]{2,1,0:T(8,128)(2,1)}) custom-call(s32[64]{0:T(128)} %multiply_add_fusion.1.which_ref, s32[64]{0:T(128)} %get-tuple-element.393.position_ref, bf16[8,72,1152]{2,1,0:T(8,128)(2,1)} %pad_maximum_fusion.rest_0_, ...), custom_call_target="tpu_custom_call" | custom-call | flops 1000 | bytes 1000 | tf_op jit(solution)/shard_map/place_blocks/pallas_call | solution.py:888
  243.7 13.2 %cross_block.1 = (f32[256,1152]{1,0:T(8,128)}, bf16[256,1152]{1,0:T(8,128)(2,1)}, bf16[256,1152]{1,0:T(8,128)(2,1)}, bf16[120,1152]{1,0:T(8,128)(2,1)}, bf16[120...) custom-call(s32[2]{0:T(128)} %copy-done.8, ...), custom_call_target="tpu_custom_call" | custom-call | flops 1000 | bytes 1000 | tf_op jit(solution)/shard_map/cross_block/pallas_call | solution.py:377
  259.5 4.0 multiply_convert_fusion
  263.4 7.1 %mlp_core.3 = (bf16[256,1152]{1,0:T(8,128)(2,1)}, bf16[256,1152]{1,0:T(8,128)(2,1)}, bf16[256,1152]{1,0:T(8,128)(2,1)}) custom-call(bf16[256,1152]{1,0:T(8,128)(2,1)} %get-tuple-element.262.refs_0_.refs_6_, bf16[256,1152]{1,0:T(8,128)(2,1)} %get-tuple-element.405.refs_1_.refs_10_, bf16[2304,1152]{1,0:T(8,128)(2,1)} %bitcast.117, bf16[2304,1152]{1,0:T(8,128)(2,1)} %bitcast.118), custom_call_target="tpu_custom_call" | custom-call | flops 1000 | bytes 1000 | tf_op jit(solution)/shard_map/mlp_core/pallas_call | solution.py:212
  270.6 14.7 %collective-permute-done.37.refs_1_.refs_8_ = bf16[256,1152]{1,0:T(8,128)(2,1)} collective-permute-done((bf16[256,1152]{1,0:T(8,128)(2,1)}, bf16[256,1152]{1,0:T(8,128)(2,1)}, u32[]{:S(2)}, u32[]{:S(2)}) %collective-permute-start.37) | collective-permute-done | bytes 589856 | tf_op jit(solution)/shard_map/ppermute | solution.py:58
  285.6 11.7 %mlp_core.4 = (bf16[512,1152]{1,0:T(8,128)(2,1)}, bf16[512,1152]{1,0:T(8,128)(2,1)}, bf16[256,1152]{1,0:T(8,128)(2,1)}, bf16[256,1152]{1,0:T(8,128)(2,1)}) custom-call(bf16[256,1152]{1,0:T(8,128)(2,1)} %collective-permute-done.36.refs_0_.refs_7_, bf16[256,1152]{1,0:T(8,128)(2,1)} %collective-permute-done.37.refs_1_.refs_8_, ...), custom_call_target="tpu_custom_call" | custom-call | flops 1000 | bytes 1000 | tf_op jit(solution)/shard_map/mlp_core/pallas_call | solution.py:212
  299.4 11.0 %collective-permute-done.40.refs_0_.refs_9_ = bf16[256,1152]{1,0:T(8,128)(2,1)} collective-permute-done((bf16[256,1152]{1,0:T(8,128)(2,1)}, bf16[256,1152]{1,0:T(8,128)(2,1)}, u32[]{:S(2)}, u32[]{:S(2)}) %collective-permute-start.40) | collective-permute-done | bytes 589856 | tf_op jit(solution)/shard_map/ppermute | solution.py:58
  310.5 7.1 %mlp_core.5 = (bf16[256,1152]{1,0:T(8,128)(2,1)}, bf16[256,1152]{1,0:T(8,128)(2,1)}, bf16[256,1152]{1,0:T(8,128)(2,1)}) custom-call(bf16[256,1152]{1,0:T(8,128)(2,1)} %collective-permute-done.40.refs_0_.refs_9_, bf16[256,1152]{1,0:T(8,128)(2,1)} %get-tuple-element.385.refs_1_.refs_13_, bf16[2304,1152]{1,0:T(8,128)(2,1)} %bitcast.121, ...), custom_call_target="tpu_custom_call" | custom-call | flops 1000 | bytes 1000 | tf_op jit(solution)/shard_map/mlp_core/pallas_call | solution.py:212
  317.6 18.0 %collective-permute-done.38.refs_1_.refs_14_ = bf16[256,1152]{1,0:T(8,128)(2,1)} collective-permute-done((bf16[256,1152]{1,0:T(8,128)(2,1)}, bf16[256,1152]{1,0:T(8,128)(2,1)}, u32[]{:S(2)}, u32[]{:S(2)}) %collective-permute-start.38) | collective-permute-done | bytes 589856 | tf_op jit(solution)/shard_map/ppermute | solution.py:58
  335.6 25.3 %collective-permute-done.41.refs_3_.refs_16_ = bf16[256,1152]{1,0:T(8,128)(2,1)} collective-permute-done((bf16[256,1152]{1,0:T(8,128)(2,1)}, bf16[256,1152]{1,0:T(8,128)(2,1)}, u32[]{:S(2)}, u32[]{:S(2)}) %collective-permute-start.41) | collective-permute-done | bytes 589856 | tf_op jit(solution)/shard_map/ppermute | solution.py:58
  360.9 12.2 %mlp_grads.1 = bf16[2304,1152]{1,0:T(8,128)(2,1)} custom-call(bf16[256,1152]{1,0:T(8,128)(2,1)} %get-tuple-element.313.refs_0_, bf16[512,1152]{1,0:T(8,128)(2,1)} %get-tuple-element.314.refs_1_, bf16[256,1152]{1,0:T(8,128)(2,1)} %get-tuple-element.315.refs_2_, bf16[256,1152]{1,0:T(8,128)(2,1)} %get-tuple-element.259.refs_6_.refs_0_.refs_3_, ...), custom_call_target="tpu_custom_call" | custom-call | flops 1000 | bytes 1000 | tf_op jit(solution)/shard_map/mlp_grads/pallas_call | solution.py:630
  373.4 14.1 %cross_back.1 = (f32[256,1152]{1,0:T(8,128)}, bf16[256,1152]{1,0:T(8,128)(2,1)}, bf16[256,1152]{1,0:T(8,128)(2,1)}, bf16[256,1152]{1,0:T(8,128)(2,1)}, bf16[120,...) custom-call(s32[2]{0:T(128)} %copy-done.8, ...), custom_call_target="tpu_custom_call" | custom-call | flops 10000000000 | bytes 10000000 | tf_op jit(solution)/shard_map/cross_back/pallas_call | solution.py:497
  387.5 7.2 %full_grads.1 = (bf16[2,4,288,1152]{3,2,1,0:T(8,128)(2,1)}, bf16[2,4,288,1152]{3,2,1,0:T(8,128)(2,1)}) custom-call(s32[2]{0:T(128)} %copy-done.8, bf16[376,288]{1,0:T(8,128)(2,1)} %get-tuple-element.242.refs_0_, bf16[376,288]{1,0:T(8,128)(2,1)} %collective-permute-done.29.refs_1_, bf16[376,288]{1,0:T(8,128)(2,1)} %collective-permute-done.30.refs_2_, ...), custom_call_target="tpu_custom_call" | custom-call | flops 1000 | bytes 1000 | tf_op jit(solution)/shard_map/full_grads/pallas_call | solution.py:580
  395.3 3.2 collective-permute-start.43
  398.7 9.4 %mlp_out.1 = (bf16[4,256,1152]{2,1,0:T(8,128)(2,1)}, f32[2,1152]{1,0:T(2,128)}) custom-call(s32[2]{0:T(128)} %copy-done.8, bf16[256,1152]{1,0:T(8,128)(2,1)} %get-tuple-element.259.refs_6_.refs_0_.refs_3_, bf16[512,1152]{1,0:T(8,128)(2,1)} %get-tuple-element.263.refs_4_.refs_1_, bf16[256,1152]{1,0:T(8,128)(2,1)} %get-tuple-element.283.refs_2_.refs_5_, ...), custom_call_target="tpu_custom_call" | custom-call | flops 1000 | bytes 1000 | tf_op jit(solution)/shard_map/mlp_out/pallas_call | solution.py:668
  408.7 9.8 %collective-permute-done.43.refs_2_ = bf16[376,288]{1,0:T(8,128)(2,1)S(1)} collective-permute-done((bf16[376,288]{1,0:T(8,128)(2,1)}, bf16[376,288]{1,0:T(8,128)(2,1)S(1)}, u32[]{:S(2)}, u32[]{:S(2)}) %collective-permute-start.43) | collective-permute-done | bytes 216608 | tf_op jit(solution)/shard_map/ppermute | solution.py:58
  419.3 8.0 %sum_split.1 = (bf16[4,2,72,1152]{3,2,1,0:T(8,128)(2,1)}, bf16[4,2,72,1152]{3,2,1,0:T(8,128)(2,1)}, bf16[4,2,72,1152]{3,2,1,0:T(8,128)(2,1)}, bf16[4,2,72,1152]{3,2,1,0:T(8,128)(2,1)}) custom-call(s32[2]{0:T(128)} %pad_add_fusion.2.place_ref, bf16[2,4,2,2,72,1152]{5,4,3,2,1,0:T(8,128)(2,1)} %bitcast.151, bf16[2,4,2,2,72,1152]{5,4,3,2,1,0:T(8,128)(2,1)} %bitcast.31.two), custom_call_target="tpu_custom_call" | custom-call | flops 10000000000 | bytes 10000000 | tf_op jit(solution)/shard_map/sum_split/pallas_call | solution.py:698
  432.1 6.8 %self_attend_back.2.refs_0_ = bf16[1024,432]{1,0:T(8,128)(2,1)S(1)} custom-call(bf16[1024,1152]{1,0:T(8,128)(2,1)S(1)} %convolution_convert_fusion.qkv_ref, bf16[1024,288]{1,0:T(8,128)(2,1)S(1)} %get-tuple-element.236.mixed_ref, f32[4,1024]{1,0:T(4,128)S(1)} %get-tuple-element.291.log_ref, bf16[376,288]{1,0:T(8,128)(2,1)S(1)} %copy-done.3, ...), custom_call_target="tpu_custom_call" | custom-call | flops 10000000000 | bytes 10000000 | tf_op jit(solution)/shard_map/self_attend_back/pallas_call | solution.py:157
  438.9 19.8 %collective-permute-done.46 = bf16[4,2,72,1152]{3,2,1,0:T(8,128)(2,1)} collective-permute-done((bf16[4,2,72,1152]{3,2,1,0:T(8,128)(2,1)}, bf16[4,2,72,1152]{3,2,1,0:T(8,128)(2,1)}, u32[]{:S(2)}, u32[]{:S(2)}) %collective-permute-start.46) | collective-permute-done | bytes 1327136 | tf_op jit(solution)/shard_map/ppermute | solution.py:780
  467.1 7.0 %self_attend_back.3.refs_1_ = bf16[1024,432]{1,0:T(8,128)(2,1)S(1)} custom-call(bf16[1024,1152]{1,0:T(8,128)(2,1)S(1)} %convolution_convert_fusion.qkv_ref, bf16[1024,288]{1,0:T(8,128)(2,1)S(1)} %get-tuple-element.236.mixed_ref, f32[4,1024]{1,0:T(4,128)S(1)} %get-tuple-element.291.log_ref, bf16[376,288]{1,0:T(8,128)(2,1)S(1)} %copy-done.3, ...), custom_call_target="tpu_custom_call" | custom-call | flops 10000000000 | bytes 10000000 | tf_op jit(solution)/shard_map/self_attend_back/pallas_call | solution.py:157
  475.1 5.7 collective-permute-done.48
  488.1 6.2 %attn_grads.1 = (bf16[2,1,288,1152]{3,2,1,0:T(8,128)(2,1)}, bf16[2,1,288,1152]{3,2,1,0:T(8,128)(2,1)}) custom-call(s32[2]{0:T(128)} %copy-done.8, bf16[1024,432]{1,0:T(8,128)(2,1)} %copy-done.14, bf16[1024,432]{1,0:T(8,128)(2,1)} %copy-done.15, bf16[1024,1152]{1,0:T(8,128)(2,1)} %copy-done.9, bf16[120,288]{1,0:T(8,128)(2,1)} %add_convert_fusion.1.refs_3_, ...), custom_call_target="tpu_custom_call" | custom-call | flops 10000000000 | bytes 10000000 | tf_op jit(solution)/shard_map/attn_grads/pallas_call | solution.py:580
  494.4 6.8 %collective-permute-start.55 = (bf16[2,72,1152]{2,1,0:T(8,128)(2,1)}, bf16[2,72,1152]{2,1,0:T(8,128)(2,1)S(1)}, u32[]{:S(2)}, u32[]{:S(2)}) collective-permute-start(bf16[2,72,1152]{2,1,0:T(8,128)(2,1)} %get-tuple-element.340), channel_id=1, source_target_pairs={{0,1},{1,2},{2,3},{3,0},{4,5},{5,6},{6,7},{7,4},{8,9},{9,10},{10,1... | collective-permute-start | bytes 995336 | tf_op jit(solution)/shard_map/ppermute | solution.py:58
  503.6 9.6 %attn_terms.1 = (bf16[4,256,1152]{2,1,0:T(8,128)(2,1)}, f32[2,1152]{1,0:T(2,128)}) custom-call(s32[2]{0:T(128)} %copy-done.8, bf16[1024,432]{1,0:T(8,128)(2,1)} %copy-done.14, bf16[1024,432]{1,0:T(8,128)(2,1)} %copy-done.15, bf16[1152,1152]{1,0:T(8,128)(2,1)} %bitcast.128, bf16[256,1152]{1,0:T(8,128)(2,1)} %copy-done.2, bf16[256,1152]{1,0:T(8,128)(2,1)} %copy-done.11, ...), custom_call_target="tpu_custom_call" | custom-call | flops 10000000000 | bytes 10000000 | tf_op jit(solution)/shard_map/attn_terms/pallas_call | solution.py:668
  517.3 3.6 collective-permute-done.54
  523.4 8.0 %collective-permute-done.52 = bf16[2,72,1152]{2,1,0:T(8,128)(2,1)S(1)} collective-permute-done((bf16[2,72,1152]{2,1,0:T(8,128)(2,1)S(1)}, bf16[2,72,1152]{2,1,0:T(8,128)(2,1)S(1)}, u32[]{:S(2)}, u32[]{:S(2)}) %collective-permute-start.52) | collective-permute-done | bytes 331808 | tf_op jit(solution)/shard_map/ppermute | solution.py:780
  536.5 3.3 collective-permute-done.58
  554.2 5.1 collective-permute-done.66
  559.3 4.0 collective-permute-done.64
  570.9 16.8 %update_slots.1 = (f32[16,72,1152]{2,1,0:T(8,128)}, f32[16,72,1152]{2,1,0:T(8,128)}, f32[16,72,1152]{2,1,0:T(8,128)}) custom-call(s32[16]{0:T(128)} %convert_element_type.102.filled_ref, s32[16]{0:T(128)} %get-tuple-element.447.which_ref, s32[16]{0:T(128)} %get-tuple-element.446.position_ref, f32[16,72,1152]{2,1,0:T(8,128)} %weight.1, f32[16,72,1152]{2,1,0:T(8,128)} %one.1, ...), custom_call_target="tpu_custom_call" | custom-call | flops 1000 | bytes 1000 | tf_op jit(solution)/shard_map/update_slots/pallas_call | solution.py:750
  587.7 3.8 reduce-scatter.11.cloned.1.call-done
  (370 shorter events, 153.9 us)
Async XLA Ops:
  7.2 97.0 %reduce-scatter.5.cloned.1.call-start = ((), (), s32[]{:S(2)}) async-start(), calls=%async_computation.4 | async-start | bytes 5971968 | tf_op jit(solution)/shard_map/reduce_scatter | solution.py:1056
  21.6 152.0 %all-gather.6.cloned.1.call-start = ((), (), s32[]{:S(2)}) async-start(), calls=%async_computation.5 | async-start | bytes 5971968 | tf_op jit(solution)/shard_map/all_gather | solution.py:1082
  21.7 21.0 %collective-permute-start = (bf16[16,72,1152]{2,1,0:T(8,128)(2,1)}, bf16[16,72,1152]{2,1,0:T(8,128)(2,1)}, u32[]{:S(2)}, u32[]{:S(2)}) collective-permute-start(bf16[16,72,1152]{2,1,0:T(8,128)(2,1)} %get-tuple-element.194), channel_id=1, source_target_pairs={{0,4},{4,0},{8,12},{12,8},{16,20},{20,16},{24,28},{28,24},{1,5},{5... | collective-permute-start | bytes 7962632 | tf_op jit(solution)/shard_map/ppermute | solution.py:780
  23.4 18.3 %collective-permute-start.2 = (bf16[256,1152]{1,0:T(8,128)(2,1)S(1)}, bf16[256,1152]{1,0:T(8,128)(2,1)S(1)}, u32[]{:S(2)}, u32[]{:S(2)}) collective-permute-start(bf16[256,1152]{1,0:T(8,128)(2,1)S(1)} %fusion.6.refs_0_.refs_3_), channel_id=1, source_target_pairs={{1,0},{2,1},{3,2},{5,4},{6,5},{7,6},{9,8},{10,9},{11,10},{13,12},{... | collective-permute-start | bytes 1769480 | tf_op jit(solution)/shard_map/ppermute | solution.py:930
  24.7 18.0 %collective-permute-start.1 = (bf16[256,1152]{1,0:T(8,128)(2,1)S(1)}, bf16[256,1152]{1,0:T(8,128)(2,1)}, u32[]{:S(2)}, u32[]{:S(2)}) collective-permute-start(bf16[256,1152]{1,0:T(8,128)(2,1)S(1)} %fusion.6.refs_0_.refs_3_), channel_id=1, source_target_pairs={{0,1},{1,2},{2,3},{4,5},{5,6},{6,7},{8,9},{9,10},{10,11},{12,13},{... | collective-permute-start | bytes 1769480 | tf_op jit(solution)/shard_map/ppermute | solution.py:930
  46.9 39.0 %collective-permute-start.5 = (bf16[256,1152]{1,0:T(8,128)(2,1)}, bf16[256,1152]{1,0:T(8,128)(2,1)}, u32[]{:S(2)}, u32[]{:S(2)}) collective-permute-start(bf16[256,1152]{1,0:T(8,128)(2,1)} %collective-permute-done.1.refs_1_), channel_id=1, source_target_pairs={{1,2},{2,3},{5,6},{6,7},{9,10},{10,11},{13,14},{14,15},{17,18},{18... | collective-permute-start | bytes 1769480 | tf_op jit(solution)/shard_map/ppermute | solution.py:930
  48.4 37.5 %collective-permute-start.6 = (bf16[256,1152]{1,0:T(8,128)(2,1)S(1)}, bf16[256,1152]{1,0:T(8,128)(2,1)}, u32[]{:S(2)}, u32[]{:S(2)}) collective-permute-start(bf16[256,1152]{1,0:T(8,128)(2,1)S(1)} %collective-permute-done.2.refs_4_), channel_id=1, source_target_pairs={{1,0},{2,1},{5,4},{6,5},{9,8},{10,9},{13,12},{14,13},{17,16},{18,1... | collective-permute-start | bytes 1769480 | tf_op jit(solution)/shard_map/ppermute | solution.py:930
  49.7 36.2 %collective-permute-start.3 = (bf16[4,72,1152]{2,1,0:T(8,128)(2,1)}, bf16[4,72,1152]{2,1,0:T(8,128)(2,1)}, u32[]{:S(2)}, u32[]{:S(2)}) collective-permute-start(bf16[4,72,1152]{2,1,0:T(8,128)(2,1)} %get-tuple-element.198), channel_id=1, source_target_pairs={{0,8},{4,12},{8,0},{12,4},{16,24},{20,28},{24,16},{28,20},{1,9},{5... | collective-permute-start | bytes 1990664 | tf_op jit(solution)/shard_map/ppermute | solution.py:780
  52.2 33.6 %collective-permute-start.4 = (bf16[4,72,1152]{2,1,0:T(8,128)(2,1)}, bf16[4,72,1152]{2,1,0:T(8,128)(2,1)}, u32[]{:S(2)}, u32[]{:S(2)}) collective-permute-start(bf16[4,72,1152]{2,1,0:T(8,128)(2,1)} %get-tuple-element.200), channel_id=1, source_target_pairs={{0,16},{4,20},{8,24},{12,28},{16,0},{20,4},{24,8},{28,12},{1,17},{... | collective-permute-start | bytes 1990664 | tf_op jit(solution)/shard_map/ppermute | solution.py:780
  57.4 28.4 %collective-permute-start.7 = (bf16[4,120,288]{1,2,0:T(8,128)(2,1)S(1)}, bf16[4,120,288]{1,2,0:T(8,128)(2,1)S(1)}, u32[]{:S(2)}, u32[]{:S(2)}) collective-permute-start(bf16[4,120,288]{1,2,0:T(8,128)(2,1)S(1)} %copy.61), channel_id=1, source_target_pairs={{0,16},{4,20},{8,24},{12,28},{16,0},{20,4},{24,8},{28,12},{1,17},{... | collective-permute-start | bytes 829448 | tf_op jit(solution)/shard_map/ppermute | solution.py:780
  88.2 16.0 %collective-permute-start.11 = (bf16[256,1152]{1,0:T(8,128)(2,1)}, bf16[256,1152]{1,0:T(8,128)(2,1)S(1)}, u32[]{:S(2)}, u32[]{:S(2)}) collective-permute-start(bf16[256,1152]{1,0:T(8,128)(2,1)} %collective-permute-done.6.refs_5_), channel_id=1, source_target_pairs={{1,0},{5,4},{9,8},{13,12},{17,16},{21,20},{25,24},{29,28}} | collective-permute-start | bytes 1769480 | tf_op jit(solution)/shard_map/ppermute | solution.py:930
  104.2 139.5 %all-gather.10.cloned.1.call-start = ((), (), s32[]{:S(2)}) async-start(), calls=%async_computation.10 | async-start | bytes 2949120 | tf_op jit(solution)/shard_map/all_gather | solution.py:1097
  108.5 31.6 %collective-permute-start.20 = (bf16[2,72,1152]{2,1,0:T(8,128)(2,1)S(1)}, bf16[2,72,1152]{2,1,0:T(8,128)(2,1)S(1)}, u32[]{:S(2)}, u32[]{:S(2)}) collective-permute-start(bf16[2,72,1152]{2,1,0:T(8,128)(2,1)S(1)} %add.300.refs_0_), channel_id=1, source_target_pairs={{0,3},{1,0},{2,1},{3,2},{4,7},{5,4},{6,5},{7,6},{8,11},{9,8},{10,9... | collective-permute-start | bytes 995336 | tf_op jit(solution)/shard_map/ppermute | solution.py:58
  111.2 29.0 %collective-permute-start.19 = (bf16[2,72,1152]{2,1,0:T(8,128)(2,1)S(1)}, bf16[2,72,1152]{2,1,0:T(8,128)(2,1)S(1)}, u32[]{:S(2)}, u32[]{:S(2)}) collective-permute-start(bf16[2,72,1152]{2,1,0:T(8,128)(2,1)S(1)} %add.300.refs_0_), channel_id=1, source_target_pairs={{0,2},{1,3},{2,0},{3,1},{4,6},{5,7},{6,4},{7,5},{8,10},{9,11},{10,... | collective-permute-start | bytes 995336 | tf_op jit(solution)/shard_map/ppermute | solution.py:58
  111.2 30.4 %collective-permute-start.18 = (bf16[2,72,1152]{2,1,0:T(8,128)(2,1)S(1)}, bf16[2,72,1152]{2,1,0:T(8,128)(2,1)}, u32[]{:S(2)}, u32[]{:S(2)}) collective-permute-start(bf16[2,72,1152]{2,1,0:T(8,128)(2,1)S(1)} %add.300.refs_0_), channel_id=1, source_target_pairs={{0,1},{1,2},{2,3},{3,0},{4,5},{5,6},{6,7},{7,4},{8,9},{9,10},{10,1... | collective-permute-start | bytes 995336 | tf_op jit(solution)/shard_map/ppermute | solution.py:58
  113.6 16.9 %collective-permute-start.14 = (bf16[2,72,1152]{2,1,0:T(8,128)(2,1)S(1)}, bf16[2,72,1152]{2,1,0:T(8,128)(2,1)S(1)}, u32[]{:S(2)}, u32[]{:S(2)}) collective-permute-start(bf16[2,72,1152]{2,1,0:T(8,128)(2,1)S(1)} %pad_maximum_fusion.8), channel_id=1, source_target_pairs={{0,16},{4,20},{8,24},{12,28},{16,0},{20,4},{24,8},{28,12},{1,17},{... | collective-permute-start | bytes 995336 | tf_op jit(solution)/shard_map/ppermute | solution.py:780
  144.1 29.5 %collective-permute-start.26 = (bf16[120,288]{0,1:T(8,128)(2,1)S(1)}, bf16[120,288]{0,1:T(8,128)(2,1)S(1)}, u32[]{:S(2)}, u32[]{:S(2)}) collective-permute-start(bf16[120,288]{0,1:T(8,128)(2,1)S(1)} %bitcast_add_fusion), channel_id=1, source_target_pairs={{0,3},{1,0},{2,1},{3,2},{4,7},{5,4},{6,5},{7,6},{8,11},{9,8},{10,9... | collective-permute-start | bytes 207368 | tf_op jit(solution)/shard_map/ppermute | solution.py:58
  147.2 26.3 %collective-permute-start.25 = (bf16[120,288]{0,1:T(8,128)(2,1)S(1)}, bf16[120,288]{0,1:T(8,128)(2,1)S(1)}, u32[]{:S(2)}, u32[]{:S(2)}) collective-permute-start(bf16[120,288]{0,1:T(8,128)(2,1)S(1)} %bitcast_add_fusion), channel_id=1, source_target_pairs={{0,2},{1,3},{2,0},{3,1},{4,6},{5,7},{6,4},{7,5},{8,10},{9,11},{10,... | collective-permute-start | bytes 207368 | tf_op jit(solution)/shard_map/ppermute | solution.py:58
  147.5 21.4 %collective-permute-start.22 = (bf16[4,72,1152]{2,1,0:T(8,128)(2,1)}, bf16[4,72,1152]{2,1,0:T(8,128)(2,1)}, u32[]{:S(2)}, u32[]{:S(2)}) collective-permute-start(bf16[4,72,1152]{2,1,0:T(8,128)(2,1)} %get-tuple-element.225), channel_id=1, source_target_pairs={{0,8},{4,12},{8,0},{12,4},{16,24},{20,28},{24,16},{28,20},{1,9},{5... | collective-permute-start | bytes 1990664 | tf_op jit(solution)/shard_map/ppermute | solution.py:780
  149.0 22.3 %collective-permute-start.23 = (bf16[4,72,1152]{2,1,0:T(8,128)(2,1)}, bf16[4,72,1152]{2,1,0:T(8,128)(2,1)}, u32[]{:S(2)}, u32[]{:S(2)}) collective-permute-start(bf16[4,72,1152]{2,1,0:T(8,128)(2,1)} %get-tuple-element.226), channel_id=1, source_target_pairs={{0,16},{4,20},{8,24},{12,28},{16,0},{20,4},{24,8},{28,12},{1,17},{... | collective-permute-start | bytes 1990664 | tf_op jit(solution)/shard_map/ppermute | solution.py:780
  149.9 332.3 %reduce-scatter.7.cloned.1.call-start = ((), (), s32[]{:S(2)}) async-start(), calls=%async_computation.6 | async-start | bytes 5971968 | tf_op jit(solution)/shard_map/reduce_scatter | solution.py:1217
  173.6 55.0 %collective-permute-start.27 = (bf16[8,72,1152]{2,1,0:T(8,128)(2,1)}, bf16[8,72,1152]{2,1,0:T(8,128)(2,1)}, u32[]{:S(2)}, u32[]{:S(2)}) collective-permute-start(bf16[8,72,1152]{2,1,0:T(8,128)(2,1)} %pad_maximum_fusion.rest_0_), channel_id=1, source_target_pairs={{0,16},{4,20},{8,24},{12,28},{16,0},{20,4},{24,8},{28,12},{1,17},{... | collective-permute-start | bytes 3981320 | tf_op jit(solution)/shard_map/ppermute | solution.py:780
  174.5 54.1 %collective-permute-start.28 = (bf16[8,72,1152]{2,1,0:T(8,128)(2,1)}, bf16[8,72,1152]{2,1,0:T(8,128)(2,1)}, u32[]{:S(2)}, u32[]{:S(2)}) collective-permute-start(bf16[8,72,1152]{2,1,0:T(8,128)(2,1)} %pad_maximum_fusion.1.rest_2_), channel_id=1, source_target_pairs={{0,8},{4,12},{8,0},{12,4},{16,24},{20,28},{24,16},{28,20},{1,9},{5... | collective-permute-start | bytes 3981320 | tf_op jit(solution)/shard_map/ppermute | solution.py:780
  181.4 17.8 %collective-permute-start.31 = (bf16[376,288]{1,0:T(8,128)(2,1)S(1)}, bf16[376,288]{1,0:T(8,128)(2,1)}, u32[]{:S(2)}, u32[]{:S(2)}) collective-permute-start(bf16[376,288]{1,0:T(8,128)(2,1)S(1)} %get-tuple-element.440), channel_id=1, source_target_pairs={{0,1},{1,2},{2,3},{3,0},{4,5},{5,6},{6,7},{7,4},{8,9},{9,10},{10,1... | collective-permute-start | bytes 649736 | tf_op jit(solution)/shard_map/ppermute | solution.py:58
  183.8 27.0 %collective-permute-start.29 = (bf16[376,288]{1,0:T(8,128)(2,1)S(1)}, bf16[376,288]{1,0:T(8,128)(2,1)}, u32[]{:S(2)}, u32[]{:S(2)}) collective-permute-start(bf16[376,288]{1,0:T(8,128)(2,1)S(1)} %get-tuple-element.441), channel_id=1, source_target_pairs={{0,3},{1,0},{2,1},{3,2},{4,7},{5,4},{6,5},{7,6},{8,11},{9,8},{10,9... | collective-permute-start | bytes 649736 | tf_op jit(solution)/shard_map/ppermute | solution.py:58
  185.5 43.2 %collective-permute-start.30 = (bf16[376,288]{1,0:T(8,128)(2,1)S(1)}, bf16[376,288]{1,0:T(8,128)(2,1)}, u32[]{:S(2)}, u32[]{:S(2)}) collective-permute-start(bf16[376,288]{1,0:T(8,128)(2,1)S(1)} %get-tuple-element.442), channel_id=1, source_target_pairs={{0,2},{1,3},{2,0},{3,1},{4,6},{5,7},{6,4},{7,5},{8,10},{9,11},{10,... | collective-permute-start | bytes 649736 | tf_op jit(solution)/shard_map/ppermute | solution.py:58
  199.2 32.6 %collective-permute-start.32 = (bf16[8,72,1152]{2,1,0:T(8,128)(2,1)}, bf16[8,72,1152]{2,1,0:T(8,128)(2,1)}, u32[]{:S(2)}, u32[]{:S(2)}) collective-permute-start(bf16[8,72,1152]{2,1,0:T(8,128)(2,1)} %pad_maximum_fusion.rest_0_), channel_id=1, source_target_pairs={{0,4},{4,0},{8,12},{12,8},{16,20},{20,16},{24,28},{28,24},{1,5},{5... | collective-permute-start | bytes 3981320 | tf_op jit(solution)/shard_map/ppermute | solution.py:780
  210.8 21.0 %collective-permute-start.34 = (bf16[8,72,1152]{2,1,0:T(8,128)(2,1)}, bf16[8,72,1152]{2,1,0:T(8,128)(2,1)}, u32[]{:S(2)}, u32[]{:S(2)}) collective-permute-start(bf16[8,72,1152]{2,1,0:T(8,128)(2,1)} %pad_maximum_fusion.1.rest_2_), channel_id=1, source_target_pairs={{0,4},{4,0},{8,12},{12,8},{16,20},{20,16},{24,28},{28,24},{1,5},{5... | collective-permute-start | bytes 3981320 | tf_op jit(solution)/shard_map/ppermute | solution.py:780
  256.9 28.3 %collective-permute-start.37 = (bf16[256,1152]{1,0:T(8,128)(2,1)}, bf16[256,1152]{1,0:T(8,128)(2,1)}, u32[]{:S(2)}, u32[]{:S(2)}) collective-permute-start(bf16[256,1152]{1,0:T(8,128)(2,1)} %get-tuple-element.262.refs_0_.refs_6_), channel_id=1, source_target_pairs={{0,3},{1,0},{2,1},{3,2},{4,7},{5,4},{6,5},{7,6},{8,11},{9,8},{10,9... | collective-permute-start | bytes 1769480 | tf_op jit(solution)/shard_map/ppermute | solution.py:58
  258.4 27.2 %collective-permute-start.36 = (bf16[256,1152]{1,0:T(8,128)(2,1)}, bf16[256,1152]{1,0:T(8,128)(2,1)}, u32[]{:S(2)}, u32[]{:S(2)}) collective-permute-start(bf16[256,1152]{1,0:T(8,128)(2,1)} %get-tuple-element.262.refs_0_.refs_6_), channel_id=1, source_target_pairs={{0,1},{1,2},{2,3},{3,0},{4,5},{5,6},{6,7},{7,4},{8,9},{9,10},{10,1... | collective-permute-start | bytes 1769480 | tf_op jit(solution)/shard_map/ppermute | solution.py:58
  270.5 40.0 %collective-permute-start.40 = (bf16[256,1152]{1,0:T(8,128)(2,1)}, bf16[256,1152]{1,0:T(8,128)(2,1)}, u32[]{:S(2)}, u32[]{:S(2)}) collective-permute-start(bf16[256,1152]{1,0:T(8,128)(2,1)} %get-tuple-element.262.refs_0_.refs_6_), channel_id=1, source_target_pairs={{0,2},{1,3},{2,0},{3,1},{4,6},{5,7},{6,4},{7,5},{8,10},{9,11},{10,... | collective-permute-start | bytes 1769480 | tf_op jit(solution)/shard_map/ppermute | solution.py:58
  297.3 38.3 %collective-permute-start.38 = (bf16[256,1152]{1,0:T(8,128)(2,1)}, bf16[256,1152]{1,0:T(8,128)(2,1)}, u32[]{:S(2)}, u32[]{:S(2)}) collective-permute-start(bf16[256,1152]{1,0:T(8,128)(2,1)} %get-tuple-element.260), channel_id=1, source_target_pairs={{0,3},{1,0},{2,1},{3,2},{4,7},{5,4},{6,5},{7,6},{8,11},{9,8},{10,9... | collective-permute-start | bytes 1769480 | tf_op jit(solution)/shard_map/ppermute | solution.py:58
  299.1 36.5 %collective-permute-start.39 = (bf16[256,1152]{1,0:T(8,128)(2,1)}, bf16[256,1152]{1,0:T(8,128)(2,1)}, u32[]{:S(2)}, u32[]{:S(2)}) collective-permute-start(bf16[256,1152]{1,0:T(8,128)(2,1)} %get-tuple-element.261), channel_id=1, source_target_pairs={{0,1},{1,2},{2,3},{3,0},{4,5},{5,6},{6,7},{7,4},{8,9},{9,10},{10,1... | collective-permute-start | bytes 1769480 | tf_op jit(solution)/shard_map/ppermute | solution.py:58
  317.6 43.4 %collective-permute-start.41 = (bf16[256,1152]{1,0:T(8,128)(2,1)}, bf16[256,1152]{1,0:T(8,128)(2,1)}, u32[]{:S(2)}, u32[]{:S(2)}) collective-permute-start(bf16[256,1152]{1,0:T(8,128)(2,1)} %get-tuple-element.264), channel_id=1, source_target_pairs={{0,2},{1,3},{2,0},{3,1},{4,6},{5,7},{6,4},{7,5},{8,10},{9,11},{10,... | collective-permute-start | bytes 1769480 | tf_op jit(solution)/shard_map/ppermute | solution.py:58
  373.2 140.8 %reduce-scatter.9.cloned.1.call-start = ((), (), s32[]{:S(2)}) async-start(), calls=%async_computation.7 | async-start | bytes 2949120 | tf_op jit(solution)/shard_map/reduce_scatter | solution.py:1288
  394.7 23.9 %collective-permute-start.45 = (bf16[2,4,288,1152]{3,2,1,0:T(8,128)(2,1)}, bf16[2,4,288,1152]{3,2,1,0:T(8,128)(2,1)}, u32[]{:S(2)}, u32[]{:S(2)}) collective-permute-start(bf16[2,4,288,1152]{3,2,1,0:T(8,128)(2,1)} %get-tuple-element.282), channel_id=1, source_target_pairs={{0,4},{4,0},{8,12},{12,8},{16,20},{20,16},{24,28},{28,24},{1,5},{5... | collective-permute-start | bytes 15925256 | tf_op jit(solution)/shard_map/ppermute | solution.py:780
  395.3 23.3 %collective-permute-start.43 = (bf16[376,288]{1,0:T(8,128)(2,1)}, bf16[376,288]{1,0:T(8,128)(2,1)S(1)}, u32[]{:S(2)}, u32[]{:S(2)}) collective-permute-start(bf16[376,288]{1,0:T(8,128)(2,1)} %get-tuple-element.273), channel_id=1, source_target_pairs={{0,2},{1,3},{2,0},{3,1},{4,6},{5,7},{6,4},{7,5},{8,10},{9,11},{10,... | collective-permute-start | bytes 649736 | tf_op jit(solution)/shard_map/ppermute | solution.py:58
  398.5 20.1 %collective-permute-start.44 = (bf16[376,288]{1,0:T(8,128)(2,1)}, bf16[376,288]{1,0:T(8,128)(2,1)}, u32[]{:S(2)}, u32[]{:S(2)}) collective-permute-start(bf16[376,288]{1,0:T(8,128)(2,1)} %get-tuple-element.274), channel_id=1, source_target_pairs={{0,3},{1,0},{2,1},{3,2},{4,7},{5,4},{6,5},{7,6},{8,11},{9,8},{10,9... | collective-permute-start | bytes 649736 | tf_op jit(solution)/shard_map/ppermute | solution.py:58
  418.6 121.4 %all-gather.8.cloned.1.call-start = ((), (), s32[]{:S(2)}) async-start(), calls=%async_computation.9 | async-start | bytes 5971968 | tf_op jit(solution)/shard_map/all_gather | solution.py:1311
  427.3 31.4 %collective-permute-start.46 = (bf16[4,2,72,1152]{3,2,1,0:T(8,128)(2,1)}, bf16[4,2,72,1152]{3,2,1,0:T(8,128)(2,1)}, u32[]{:S(2)}, u32[]{:S(2)}) collective-permute-start(bf16[4,2,72,1152]{3,2,1,0:T(8,128)(2,1)} %get-tuple-element.288), channel_id=1, source_target_pairs={{0,8},{4,12},{8,0},{12,4},{16,24},{20,28},{24,16},{28,20},{1,9},{5... | collective-permute-start | bytes 3981320 | tf_op jit(solution)/shard_map/ppermute | solution.py:780
  428.9 30.9 %collective-permute-start.47 = (bf16[4,2,72,1152]{3,2,1,0:T(8,128)(2,1)}, bf16[4,2,72,1152]{3,2,1,0:T(8,128)(2,1)}, u32[]{:S(2)}, u32[]{:S(2)}) collective-permute-start(bf16[4,2,72,1152]{3,2,1,0:T(8,128)(2,1)} %get-tuple-element.290), channel_id=1, source_target_pairs={{0,16},{4,20},{8,24},{12,28},{16,0},{20,4},{24,8},{28,12},{1,17},{... | collective-permute-start | bytes 3981320 | tf_op jit(solution)/shard_map/ppermute | solution.py:780
  465.2 15.6 %collective-permute-start.48 = (bf16[4,72,1152]{2,1,0:T(8,128)(2,1)S(1)}, bf16[4,72,1152]{2,1,0:T(8,128)(2,1)}, u32[]{:S(2)}, u32[]{:S(2)}) collective-permute-start(bf16[4,72,1152]{2,1,0:T(8,128)(2,1)S(1)} %get-tuple-element.305), channel_id=1, source_target_pairs={{0,16},{4,20},{8,24},{12,28},{16,0},{20,4},{24,8},{28,12},{1,17},{... | collective-permute-start | bytes 1990664 | tf_op jit(solution)/shard_map/ppermute | solution.py:780
  466.7 15.5 %collective-permute-start.49 = (bf16[4,72,1152]{2,1,0:T(8,128)(2,1)S(1)}, bf16[4,72,1152]{2,1,0:T(8,128)(2,1)}, u32[]{:S(2)}, u32[]{:S(2)}) collective-permute-start(bf16[4,72,1152]{2,1,0:T(8,128)(2,1)S(1)} %get-tuple-element.307), channel_id=1, source_target_pairs={{0,8},{4,12},{8,0},{12,4},{16,24},{20,28},{24,16},{28,20},{1,9},{5... | collective-permute-start | bytes 1990664 | tf_op jit(solution)/shard_map/ppermute | solution.py:780
  482.2 109.3 %reduce-scatter.11.cloned.1.call-start = ((), (), s32[]{:S(2)}) async-start(), calls=%async_computation.8 | async-start | bytes 2949120 | tf_op jit(solution)/shard_map/reduce_scatter | solution.py:1323
  494.3 19.6 %collective-permute-start.50 = (bf16[2,1,288,1152]{3,2,1,0:T(8,128)(2,1)}, bf16[2,1,288,1152]{3,2,1,0:T(8,128)(2,1)}, u32[]{:S(2)}, u32[]{:S(2)}) collective-permute-start(bf16[2,1,288,1152]{3,2,1,0:T(8,128)(2,1)} %get-tuple-element.325), channel_id=1, source_target_pairs={{0,4},{4,0},{8,12},{12,8},{16,20},{20,16},{24,28},{28,24},{1,5},{5... | collective-permute-start | bytes 3981320 | tf_op jit(solution)/shard_map/ppermute | solution.py:780
  494.4 27.3 %collective-permute-start.55 = (bf16[2,72,1152]{2,1,0:T(8,128)(2,1)}, bf16[2,72,1152]{2,1,0:T(8,128)(2,1)S(1)}, u32[]{:S(2)}, u32[]{:S(2)}) collective-permute-start(bf16[2,72,1152]{2,1,0:T(8,128)(2,1)} %get-tuple-element.340), channel_id=1, source_target_pairs={{0,1},{1,2},{2,3},{3,0},{4,5},{5,6},{6,7},{7,4},{8,9},{9,10},{10,1... | collective-permute-start | bytes 995336 | tf_op jit(solution)/shard_map/ppermute | solution.py:58
  501.2 21.3 %collective-permute-start.56 = (bf16[2,72,1152]{2,1,0:T(8,128)(2,1)}, bf16[2,72,1152]{2,1,0:T(8,128)(2,1)S(1)}, u32[]{:S(2)}, u32[]{:S(2)}) collective-permute-start(bf16[2,72,1152]{2,1,0:T(8,128)(2,1)} %get-tuple-element.341), channel_id=1, source_target_pairs={{0,2},{1,3},{2,0},{3,1},{4,6},{5,7},{6,4},{7,5},{8,10},{9,11},{10,... | collective-permute-start | bytes 995336 | tf_op jit(solution)/shard_map/ppermute | solution.py:58
  501.2 22.3 %collective-permute-start.57 = (bf16[2,72,1152]{2,1,0:T(8,128)(2,1)}, bf16[2,72,1152]{2,1,0:T(8,128)(2,1)S(1)}, u32[]{:S(2)}, u32[]{:S(2)}) collective-permute-start(bf16[2,72,1152]{2,1,0:T(8,128)(2,1)} %get-tuple-element.342), channel_id=1, source_target_pairs={{0,3},{1,0},{2,1},{3,2},{4,7},{5,4},{6,5},{7,6},{8,11},{9,8},{10,9... | collective-permute-start | bytes 995336 | tf_op jit(solution)/shard_map/ppermute | solution.py:58
  (93 other events, 1105.4 us)
Sparse Core Ops, SparseCore 0:
  21.7 75.6 reduce-scatter.4
  104.3 46.0 all-gather.5
  152.0 74.3 all-gather.9
  373.3 57.2 reduce-scatter.6
  432.7 48.0 reduce-scatter.8
  482.6 48.2 all-gather.7
  544.0 47.4 reduce-scatter.10

commit v3 on v2

--- a/solution.py
+++ b/solution.py
@@ -1062,7 +1062,6 @@
         attn_got = swap(attn_send, "dp", 1)
         full_got = swap(full_send, "dp", 2)
         text = caption_terms(ids)
-        text = text[0:4] + swap(text[4:8], "dp", 2)
         n_up.append(up), n_down.append(down)
         attn_two, attn_got, full_two, full_got, up, down, text = fence(
             (attn_two, attn_got, full_two, full_got, up, down, text)
@@ -1072,7 +1071,7 @@
         up, down = hops(up, 1, 3), hops(down, -1, 3)
         attn_got = swap(attn_send, "dp", 2)
         full_got = swap(full_send, "dp", 1)
-        text = text[0:2] + swap(text[2:4], "dp", 1)
+        text = text[0:4] + swap(text[4:8], "dp", 2)
         n_up.append(up), n_down.append(down)
         attn_one, attn_got, full_one, full_got, up, down, text, mlp_part = fence(
             (attn_one, attn_got, full_one, full_got, up, down, text, mlp_part)
@@ -1085,6 +1084,7 @@
         second = jnp.concatenate([attn_one[1:2], swap(attn_one[1:2], "dp", 2)])
         pool = jnp.concatenate([first, swap(first, "dp", 2), second, swap(second, "dp", 1)])
         other = swap(pool, "dp", 0)
+        text = text[0:2] + swap(text[2:4], "dp", 1)
         text = text[0] + swap(text[1], "dp", 0)
         *n_slots, h_one_all = line_slots(
             where, n_low, n_up, n_down, jnp.concatenate([mod_row(0), mod_row(1)])

time: 613 us -> 615 us (level)
  starting transfers between devices: 78.1 us -> 84.6 us
    ppermute x6, waiting for transfers between devices: 2.72 us -> 14.6 us  [hops(): return lax.ppermute(values, 'tensor', pairs)]
    ppermute x41, waiting for transfers between devices: 115 us -> 105 us  [swap(): return lax.ppermute(values, axis, [(i, i ^ 1 << bit) for i in range(count)])]
    unnamed x139 -> x143, local copies, waits for them, and re-layouts: 16 us -> 16.7 us
  transfers between devices with their start and end apart: 75 -> 75, of which waited for: 39 -> 41; matrix products, arithmetic and copies ran while one was open for 10% -> 10% of each run, Pallas kernels for 23% -> 23%
where the time goes in v3:
time: 615 us; the launch traced here: 607 us
  waiting for transfers between devices  242 us (39%)
  Pallas kernels  172 us (28%)
  starting transfers between devices  84.6 us (14%)
  other arithmetic  43.5 us (7%)
  local copies, waits for them, and re-layouts  28 us (5%)
  between operations  15.5 us (3%)
  matrix products  12.4 us (2%)
  blocking collectives  9.32 us (2%)
    ppermute x21, waiting for transfers between devices, shift(): lax.ppermute(values, 'tensor', [(i, (i + step) % count) for i in range(co...  118 us
    ppermute x41, waiting for transfers between devices, swap(): return lax.ppermute(values, axis, [(i, i ^ 1 << bit) for i in range(count)])  105 us
    ppermute x41, starting transfers between devices, swap(): return lax.ppermute(values, axis, [(i, i ^ 1 << bit) for i in range(count)])  39.5 us
    ppermute x21, starting transfers between devices, shift(): lax.ppermute(values, 'tensor', [(i, (i + step) % count) for i in range(co...  31.9 us
    pallas_call x3, Pallas kernels, mlp_core(): pl.pallas_call(body, grid=(steps,), in_specs=[whole] * (2 * groups) + [pl...  25.9 us
    pallas_call x2, Pallas kernels, ranked_terms(): pl.pallas_call(body, in_specs=[in_smem()] + [in_vmem()] * (len(lefts) + 1...  18.9 us
    pallas_call x1, Pallas kernels, update_slots(): pl.pallas_call(body, grid_spec=pltpu.PrefetchScalarGridSpec(num_scalar_pr...  16.8 us
    unnamed x143, local copies, waits for them, and re-layouts  16.7 us
  transfers between devices with their start and end apart: 75, of which 41 were waited for; matrix products, arithmetic and copies ran while one was open for 10% of the time, Pallas kernels for 23%

profile of v3, /device:TPU:0, one launch (start us, length us, event | category | flops | bytes accessed | tf_op | source)
XLA Modules:
  0.0 606.7 jit_solution(17808363072021422669)
XLA Ops:
  12.8 4.2 pick_units.2
  17.0 4.5 pick_units.3
  24.7 6.4 %collective-permute-start.1 = (bf16[256,1152]{1,0:T(8,128)(2,1)S(1)}, bf16[256,1152]{1,0:T(8,128)(2,1)}, u32[]{:S(2)}, u32[]{:S(2)}) collective-permute-start(bf16[256,1152]{1,0:T(8,128)(2,1)S(1)} %fusion.6.refs_0_.refs_3_), channel_id=1, source_target_pairs={{0,1},{1,2},{2,3},{4,5},{5,6},{6,7},{8,9},{9,10},{10,11},{12,13},{... | collective-permute-start | bytes 1769480 | tf_op jit(solution)/shard_map/ppermute | solution.py:930
  31.1 9.3 %all-gather.1 = s32[8,1,120]{2,1,0:T(1,128)S(1)} all-gather(s32[1,1,120]{2,1,0:T(1,128)S(1)} %bitcast.150), channel_id=1, replica_groups=mesh['dp'=8,'tensor'=4] {'dp'}, dimensions={0}, use_global_device_ids=true | all-gather | bytes 4320 | tf_op jit(solution)/shard_map/all_gather | solution.py:1035
  42.8 4.1 slice_add_fusion
  54.4 4.1 fusion.10
  60.5 12.7 %collective-permute-done.6.refs_5_ = bf16[256,1152]{1,0:T(8,128)(2,1)} collective-permute-done((bf16[256,1152]{1,0:T(8,128)(2,1)S(1)}, bf16[256,1152]{1,0:T(8,128)(2,1)}, u32[]{:S(2)}, u32[]{:S(2)}) %collective-permute-start.6) | collective-permute-done | bytes 589856 | tf_op jit(solution)/shard_map/ppermute | solution.py:930
  73.2 4.0 collective-permute-done.3
  87.1 5.0 collective-permute-done.11
  92.1 10.0 %collective-permute-done.7 = bf16[2,72,1152]{2,1,0:T(8,128)(2,1)S(1)} collective-permute-done((bf16[2,72,1152]{2,1,0:T(8,128)(2,1)S(1)}, bf16[2,72,1152]{2,1,0:T(8,128)(2,1)S(1)}, u32[]{:S(2)}, u32[]{:S(2)}) %collective-permute-start.7) | collective-permute-done | bytes 331808 | tf_op jit(solution)/shard_map/ppermute | solution.py:780
  112.9 5.1 collective-permute-done.20
  120.5 6.0 collective-permute-done.12
  129.2 7.1 %collective-permute-done.13 = bf16[2,72,1152]{2,1,0:T(8,128)(2,1)S(1)} collective-permute-done((bf16[2,72,1152]{2,1,0:T(8,128)(2,1)S(1)}, bf16[2,72,1152]{2,1,0:T(8,128)(2,1)S(1)}, u32[]{:S(2)}, u32[]{:S(2)}) %collective-permute-start.13) | collective-permute-done | bytes 331808 | tf_op jit(solution)/shard_map/ppermute | solution.py:780
  151.0 4.4 collective-permute-start.25
  160.1 5.6 convolution_convert_fusion.qkv_ref
  165.9 8.3 %self_attend.1 = (bf16[1024,288]{1,0:T(8,128)(2,1)S(1)}, f32[4,1024]{1,0:T(4,128)S(1)}) custom-call(bf16[1024,1152]{1,0:T(8,128)(2,1)S(1)} %convolution_convert_fusion.qkv_ref), custom_call_target="tpu_custom_call" | custom-call | flops 1000 | bytes 1000 | tf_op jit(solution)/shard_map/self_attend/pallas_call | solution.py:106
  193.2 13.1 %collective-permute-done.31.refs_3_ = bf16[376,288]{1,0:T(8,128)(2,1)} collective-permute-done((bf16[376,288]{1,0:T(8,128)(2,1)S(1)}, bf16[376,288]{1,0:T(8,128)(2,1)}, u32[]{:S(2)}, u32[]{:S(2)}) %collective-permute-start.31) | collective-permute-done | bytes 216608 | tf_op jit(solution)/shard_map/ppermute | solution.py:58
  206.3 10.0 %collective-permute-done.29.refs_1_ = bf16[376,288]{1,0:T(8,128)(2,1)} collective-permute-done((bf16[376,288]{1,0:T(8,128)(2,1)S(1)}, bf16[376,288]{1,0:T(8,128)(2,1)}, u32[]{:S(2)}, u32[]{:S(2)}) %collective-permute-start.29) | collective-permute-done | bytes 216608 | tf_op jit(solution)/shard_map/ppermute | solution.py:58
  216.3 15.2 %collective-permute-done.30.refs_2_ = bf16[376,288]{1,0:T(8,128)(2,1)} collective-permute-done((bf16[376,288]{1,0:T(8,128)(2,1)S(1)}, bf16[376,288]{1,0:T(8,128)(2,1)}, u32[]{:S(2)}, u32[]{:S(2)}) %collective-permute-start.30) | collective-permute-done | bytes 216608 | tf_op jit(solution)/shard_map/ppermute | solution.py:58
  236.9 9.7 %place_blocks.3 = (bf16[16,72,1152]{2,1,0:T(8,128)(2,1)}, bf16[16,72,1152]{2,1,0:T(8,128)(2,1)}, bf16[16,72,1152]{2,1,0:T(8,128)(2,1)}, bf16[16,72,1152]{2,1,0:T(8,128)(2,1)}) custom-call(s32[64]{0:T(128)} %multiply_add_fusion.1.which_ref, s32[64]{0:T(128)} %get-tuple-element.393.position_ref, bf16[8,72,1152]{2,1,0:T(8,128)(2,1)} %pad_maximum_fusion.rest_0_, ...), custom_call_target="tpu_custom_call" | custom-call | flops 1000 | bytes 1000 | tf_op jit(solution)/shard_map/place_blocks/pallas_call | solution.py:888
  246.6 13.2 %cross_block.1 = (f32[256,1152]{1,0:T(8,128)}, bf16[256,1152]{1,0:T(8,128)(2,1)}, bf16[256,1152]{1,0:T(8,128)(2,1)}, bf16[120,1152]{1,0:T(8,128)(2,1)}, bf16[120...) custom-call(s32[2]{0:T(128)} %copy-done.8, ...), custom_call_target="tpu_custom_call" | custom-call | flops 1000 | bytes 1000 | tf_op jit(solution)/shard_map/cross_block/pallas_call | solution.py:377
  262.4 3.9 multiply_convert_fusion
  266.3 7.1 %mlp_core.3 = (bf16[256,1152]{1,0:T(8,128)(2,1)}, bf16[256,1152]{1,0:T(8,128)(2,1)}, bf16[256,1152]{1,0:T(8,128)(2,1)}) custom-call(bf16[256,1152]{1,0:T(8,128)(2,1)} %get-tuple-element.262.refs_0_.refs_6_, bf16[256,1152]{1,0:T(8,128)(2,1)} %get-tuple-element.405.refs_1_.refs_10_, bf16[2304,1152]{1,0:T(8,128)(2,1)} %bitcast.117, bf16[2304,1152]{1,0:T(8,128)(2,1)} %bitcast.118), custom_call_target="tpu_custom_call" | custom-call | flops 1000 | bytes 1000 | tf_op jit(solution)/shard_map/mlp_core/pallas_call | solution.py:212
  273.5 14.8 %collective-permute-done.37.refs_1_.refs_8_ = bf16[256,1152]{1,0:T(8,128)(2,1)} collective-permute-done((bf16[256,1152]{1,0:T(8,128)(2,1)}, bf16[256,1152]{1,0:T(8,128)(2,1)}, u32[]{:S(2)}, u32[]{:S(2)}) %collective-permute-start.37) | collective-permute-done | bytes 589856 | tf_op jit(solution)/shard_map/ppermute | solution.py:58
  288.4 11.8 %mlp_core.4 = (bf16[512,1152]{1,0:T(8,128)(2,1)}, bf16[512,1152]{1,0:T(8,128)(2,1)}, bf16[256,1152]{1,0:T(8,128)(2,1)}, bf16[256,1152]{1,0:T(8,128)(2,1)}) custom-call(bf16[256,1152]{1,0:T(8,128)(2,1)} %collective-permute-done.36.refs_0_.refs_7_, bf16[256,1152]{1,0:T(8,128)(2,1)} %collective-permute-done.37.refs_1_.refs_8_, ...), custom_call_target="tpu_custom_call" | custom-call | flops 1000 | bytes 1000 | tf_op jit(solution)/shard_map/mlp_core/pallas_call | solution.py:212
  302.2 10.6 %collective-permute-done.40.refs_0_.refs_9_ = bf16[256,1152]{1,0:T(8,128)(2,1)} collective-permute-done((bf16[256,1152]{1,0:T(8,128)(2,1)}, bf16[256,1152]{1,0:T(8,128)(2,1)}, u32[]{:S(2)}, u32[]{:S(2)}) %collective-permute-start.40) | collective-permute-done | bytes 589856 | tf_op jit(solution)/shard_map/ppermute | solution.py:58
  312.8 7.1 %mlp_core.5 = (bf16[256,1152]{1,0:T(8,128)(2,1)}, bf16[256,1152]{1,0:T(8,128)(2,1)}, bf16[256,1152]{1,0:T(8,128)(2,1)}) custom-call(bf16[256,1152]{1,0:T(8,128)(2,1)} %collective-permute-done.40.refs_0_.refs_9_, bf16[256,1152]{1,0:T(8,128)(2,1)} %get-tuple-element.385.refs_1_.refs_13_, bf16[2304,1152]{1,0:T(8,128)(2,1)} %bitcast.121, ...), custom_call_target="tpu_custom_call" | custom-call | flops 1000 | bytes 1000 | tf_op jit(solution)/shard_map/mlp_core/pallas_call | solution.py:212
  319.9 18.0 %collective-permute-done.38.refs_1_.refs_14_ = bf16[256,1152]{1,0:T(8,128)(2,1)} collective-permute-done((bf16[256,1152]{1,0:T(8,128)(2,1)}, bf16[256,1152]{1,0:T(8,128)(2,1)}, u32[]{:S(2)}, u32[]{:S(2)}) %collective-permute-start.38) | collective-permute-done | bytes 589856 | tf_op jit(solution)/shard_map/ppermute | solution.py:58
  337.9 25.3 %collective-permute-done.41.refs_3_.refs_16_ = bf16[256,1152]{1,0:T(8,128)(2,1)} collective-permute-done((bf16[256,1152]{1,0:T(8,128)(2,1)}, bf16[256,1152]{1,0:T(8,128)(2,1)}, u32[]{:S(2)}, u32[]{:S(2)}) %collective-permute-start.41) | collective-permute-done | bytes 589856 | tf_op jit(solution)/shard_map/ppermute | solution.py:58
  363.2 12.2 %mlp_grads.1 = bf16[2304,1152]{1,0:T(8,128)(2,1)} custom-call(bf16[256,1152]{1,0:T(8,128)(2,1)} %get-tuple-element.313.refs_0_, bf16[512,1152]{1,0:T(8,128)(2,1)} %get-tuple-element.314.refs_1_, bf16[256,1152]{1,0:T(8,128)(2,1)} %get-tuple-element.315.refs_2_, bf16[256,1152]{1,0:T(8,128)(2,1)} %get-tuple-element.259.refs_6_.refs_0_.refs_3_, ...), custom_call_target="tpu_custom_call" | custom-call | flops 1000 | bytes 1000 | tf_op jit(solution)/shard_map/mlp_grads/pallas_call | solution.py:630
  375.7 14.1 %cross_back.1 = (f32[256,1152]{1,0:T(8,128)}, bf16[256,1152]{1,0:T(8,128)(2,1)}, bf16[256,1152]{1,0:T(8,128)(2,1)}, bf16[256,1152]{1,0:T(8,128)(2,1)}, bf16[120,...) custom-call(s32[2]{0:T(128)} %copy-done.8, ...), custom_call_target="tpu_custom_call" | custom-call | flops 10000000000 | bytes 10000000 | tf_op jit(solution)/shard_map/cross_back/pallas_call | solution.py:497
  389.8 7.3 %full_grads.1 = (bf16[2,4,288,1152]{3,2,1,0:T(8,128)(2,1)}, bf16[2,4,288,1152]{3,2,1,0:T(8,128)(2,1)}) custom-call(s32[2]{0:T(128)} %copy-done.8, bf16[376,288]{1,0:T(8,128)(2,1)} %get-tuple-element.242.refs_0_, bf16[376,288]{1,0:T(8,128)(2,1)} %collective-permute-done.29.refs_1_, bf16[376,288]{1,0:T(8,128)(2,1)} %collective-permute-done.30.refs_2_, ...), custom_call_target="tpu_custom_call" | custom-call | flops 1000 | bytes 1000 | tf_op jit(solution)/shard_map/full_grads/pallas_call | solution.py:580
  401.3 9.3 %mlp_out.1 = (bf16[4,256,1152]{2,1,0:T(8,128)(2,1)}, f32[2,1152]{1,0:T(2,128)}) custom-call(s32[2]{0:T(128)} %copy-done.8, bf16[256,1152]{1,0:T(8,128)(2,1)} %get-tuple-element.259.refs_6_.refs_0_.refs_3_, bf16[512,1152]{1,0:T(8,128)(2,1)} %get-tuple-element.263.refs_4_.refs_1_, bf16[256,1152]{1,0:T(8,128)(2,1)} %get-tuple-element.283.refs_2_.refs_5_, ...), custom_call_target="tpu_custom_call" | custom-call | flops 1000 | bytes 1000 | tf_op jit(solution)/shard_map/mlp_out/pallas_call | solution.py:668
  411.3 9.6 %collective-permute-done.43.refs_2_ = bf16[376,288]{1,0:T(8,128)(2,1)S(1)} collective-permute-done((bf16[376,288]{1,0:T(8,128)(2,1)}, bf16[376,288]{1,0:T(8,128)(2,1)S(1)}, u32[]{:S(2)}, u32[]{:S(2)}) %collective-permute-start.43) | collective-permute-done | bytes 216608 | tf_op jit(solution)/shard_map/ppermute | solution.py:58
  421.6 8.4 %sum_split.1 = (bf16[4,2,72,1152]{3,2,1,0:T(8,128)(2,1)}, bf16[4,2,72,1152]{3,2,1,0:T(8,128)(2,1)}, bf16[4,2,72,1152]{3,2,1,0:T(8,128)(2,1)}, bf16[4,2,72,1152]{3,2,1,0:T(8,128)(2,1)}) custom-call(s32[2]{0:T(128)} %pad_add_fusion.2.place_ref, bf16[2,4,2,2,72,1152]{5,4,3,2,1,0:T(8,128)(2,1)} %bitcast.151, bf16[2,4,2,2,72,1152]{5,4,3,2,1,0:T(8,128)(2,1)} %bitcast.31.two), custom_call_target="tpu_custom_call" | custom-call | flops 10000000000 | bytes 10000000 | tf_op jit(solution)/shard_map/sum_split/pallas_call | solution.py:698
  435.3 6.8 %self_attend_back.2.refs_0_ = bf16[1024,432]{1,0:T(8,128)(2,1)S(1)} custom-call(bf16[1024,1152]{1,0:T(8,128)(2,1)S(1)} %convolution_convert_fusion.qkv_ref, bf16[1024,288]{1,0:T(8,128)(2,1)S(1)} %get-tuple-element.236.mixed_ref, f32[4,1024]{1,0:T(4,128)S(1)} %get-tuple-element.291.log_ref, bf16[376,288]{1,0:T(8,128)(2,1)S(1)} %copy-done.3, ...), custom_call_target="tpu_custom_call" | custom-call | flops 10000000000 | bytes 10000000 | tf_op jit(solution)/shard_map/self_attend_back/pallas_call | solution.py:157
  442.1 19.3 %collective-permute-done.46 = bf16[4,2,72,1152]{3,2,1,0:T(8,128)(2,1)} collective-permute-done((bf16[4,2,72,1152]{3,2,1,0:T(8,128)(2,1)}, bf16[4,2,72,1152]{3,2,1,0:T(8,128)(2,1)}, u32[]{:S(2)}, u32[]{:S(2)}) %collective-permute-start.46) | collective-permute-done | bytes 1327136 | tf_op jit(solution)/shard_map/ppermute | solution.py:780
  470.5 7.0 %self_attend_back.3.refs_1_ = bf16[1024,432]{1,0:T(8,128)(2,1)S(1)} custom-call(bf16[1024,1152]{1,0:T(8,128)(2,1)S(1)} %convolution_convert_fusion.qkv_ref, bf16[1024,288]{1,0:T(8,128)(2,1)S(1)} %get-tuple-element.236.mixed_ref, f32[4,1024]{1,0:T(4,128)S(1)} %get-tuple-element.291.log_ref, bf16[376,288]{1,0:T(8,128)(2,1)S(1)} %copy-done.3, ...), custom_call_target="tpu_custom_call" | custom-call | flops 10000000000 | bytes 10000000 | tf_op jit(solution)/shard_map/self_attend_back/pallas_call | solution.py:157
  478.4 5.7 collective-permute-done.48
  491.2 6.2 %attn_grads.1 = (bf16[2,1,288,1152]{3,2,1,0:T(8,128)(2,1)}, bf16[2,1,288,1152]{3,2,1,0:T(8,128)(2,1)}) custom-call(s32[2]{0:T(128)} %copy-done.8, bf16[1024,432]{1,0:T(8,128)(2,1)} %copy-done.14, bf16[1024,432]{1,0:T(8,128)(2,1)} %copy-done.15, bf16[1024,1152]{1,0:T(8,128)(2,1)} %copy-done.9, bf16[120,288]{1,0:T(8,128)(2,1)} %add_convert_fusion.1.refs_3_, ...), custom_call_target="tpu_custom_call" | custom-call | flops 10000000000 | bytes 10000000 | tf_op jit(solution)/shard_map/attn_grads/pallas_call | solution.py:580
  497.6 6.8 %collective-permute-start.55 = (bf16[2,72,1152]{2,1,0:T(8,128)(2,1)}, bf16[2,72,1152]{2,1,0:T(8,128)(2,1)S(1)}, u32[]{:S(2)}, u32[]{:S(2)}) collective-permute-start(bf16[2,72,1152]{2,1,0:T(8,128)(2,1)} %get-tuple-element.340), channel_id=1, source_target_pairs={{0,1},{1,2},{2,3},{3,0},{4,5},{5,6},{6,7},{7,4},{8,9},{9,10},{10,1... | collective-permute-start | bytes 995336 | tf_op jit(solution)/shard_map/ppermute | solution.py:58
  506.8 9.6 %attn_terms.1 = (bf16[4,256,1152]{2,1,0:T(8,128)(2,1)}, f32[2,1152]{1,0:T(2,128)}) custom-call(s32[2]{0:T(128)} %copy-done.8, bf16[1024,432]{1,0:T(8,128)(2,1)} %copy-done.14, bf16[1024,432]{1,0:T(8,128)(2,1)} %copy-done.15, bf16[1152,1152]{1,0:T(8,128)(2,1)} %bitcast.128, bf16[256,1152]{1,0:T(8,128)(2,1)} %copy-done.2, bf16[256,1152]{1,0:T(8,128)(2,1)} %copy-done.11, ...), custom_call_target="tpu_custom_call" | custom-call | flops 10000000000 | bytes 10000000 | tf_op jit(solution)/shard_map/attn_terms/pallas_call | solution.py:668
  520.4 3.7 collective-permute-done.54
  526.6 8.0 %collective-permute-done.52 = bf16[2,72,1152]{2,1,0:T(8,128)(2,1)S(1)} collective-permute-done((bf16[2,72,1152]{2,1,0:T(8,128)(2,1)S(1)}, bf16[2,72,1152]{2,1,0:T(8,128)(2,1)S(1)}, u32[]{:S(2)}, u32[]{:S(2)}) %collective-permute-start.52) | collective-permute-done | bytes 331808 | tf_op jit(solution)/shard_map/ppermute | solution.py:780
  557.4 5.1 collective-permute-done.66
  562.5 4.0 collective-permute-done.64
  574.1 16.8 %update_slots.1 = (f32[16,72,1152]{2,1,0:T(8,128)}, f32[16,72,1152]{2,1,0:T(8,128)}, f32[16,72,1152]{2,1,0:T(8,128)}) custom-call(s32[16]{0:T(128)} %convert_element_type.102.filled_ref, s32[16]{0:T(128)} %get-tuple-element.445.which_ref, s32[16]{0:T(128)} %get-tuple-element.444.position_ref, f32[16,72,1152]{2,1,0:T(8,128)} %weight.1, f32[16,72,1152]{2,1,0:T(8,128)} %one.1, ...), custom_call_target="tpu_custom_call" | custom-call | flops 1000 | bytes 1000 | tf_op jit(solution)/shard_map/update_slots/pallas_call | solution.py:750
  590.9 3.8 reduce-scatter.11.cloned.1.call-done
  (373 shorter events, 166.8 us)
Async XLA Ops:
  7.2 95.8 %reduce-scatter.5.cloned.1.call-start = ((), (), s32[]{:S(2)}) async-start(), calls=%async_computation.4 | async-start | bytes 5971968 | tf_op jit(solution)/shard_map/reduce_scatter | solution.py:1056
  21.6 157.4 %all-gather.6.cloned.1.call-start = ((), (), s32[]{:S(2)}) async-start(), calls=%async_computation.5 | async-start | bytes 5971968 | tf_op jit(solution)/shard_map/all_gather | solution.py:1081
  21.6 21.2 %collective-permute-start = (bf16[16,72,1152]{2,1,0:T(8,128)(2,1)}, bf16[16,72,1152]{2,1,0:T(8,128)(2,1)}, u32[]{:S(2)}, u32[]{:S(2)}) collective-permute-start(bf16[16,72,1152]{2,1,0:T(8,128)(2,1)} %get-tuple-element.194), channel_id=1, source_target_pairs={{0,4},{4,0},{8,12},{12,8},{16,20},{20,16},{24,28},{28,24},{1,5},{5... | collective-permute-start | bytes 7962632 | tf_op jit(solution)/shard_map/ppermute | solution.py:780
  23.4 18.2 %collective-permute-start.2 = (bf16[256,1152]{1,0:T(8,128)(2,1)S(1)}, bf16[256,1152]{1,0:T(8,128)(2,1)S(1)}, u32[]{:S(2)}, u32[]{:S(2)}) collective-permute-start(bf16[256,1152]{1,0:T(8,128)(2,1)S(1)} %fusion.6.refs_0_.refs_3_), channel_id=1, source_target_pairs={{1,0},{2,1},{3,2},{5,4},{6,5},{7,6},{9,8},{10,9},{11,10},{13,12},{... | collective-permute-start | bytes 1769480 | tf_op jit(solution)/shard_map/ppermute | solution.py:930
  24.7 18.1 %collective-permute-start.1 = (bf16[256,1152]{1,0:T(8,128)(2,1)S(1)}, bf16[256,1152]{1,0:T(8,128)(2,1)}, u32[]{:S(2)}, u32[]{:S(2)}) collective-permute-start(bf16[256,1152]{1,0:T(8,128)(2,1)S(1)} %fusion.6.refs_0_.refs_3_), channel_id=1, source_target_pairs={{0,1},{1,2},{2,3},{4,5},{5,6},{6,7},{8,9},{9,10},{10,11},{12,13},{... | collective-permute-start | bytes 1769480 | tf_op jit(solution)/shard_map/ppermute | solution.py:930
  46.9 30.3 %collective-permute-start.3 = (bf16[4,72,1152]{2,1,0:T(8,128)(2,1)}, bf16[4,72,1152]{2,1,0:T(8,128)(2,1)}, u32[]{:S(2)}, u32[]{:S(2)}) collective-permute-start(bf16[4,72,1152]{2,1,0:T(8,128)(2,1)} %get-tuple-element.198), channel_id=1, source_target_pairs={{0,8},{4,12},{8,0},{12,4},{16,24},{20,28},{24,16},{28,20},{1,9},{5... | collective-permute-start | bytes 1990664 | tf_op jit(solution)/shard_map/ppermute | solution.py:780
  48.6 30.5 %collective-permute-start.4 = (bf16[4,72,1152]{2,1,0:T(8,128)(2,1)}, bf16[4,72,1152]{2,1,0:T(8,128)(2,1)}, u32[]{:S(2)}, u32[]{:S(2)}) collective-permute-start(bf16[4,72,1152]{2,1,0:T(8,128)(2,1)} %get-tuple-element.200), channel_id=1, source_target_pairs={{0,16},{4,20},{8,24},{12,28},{16,0},{20,4},{24,8},{28,12},{1,17},{... | collective-permute-start | bytes 1990664 | tf_op jit(solution)/shard_map/ppermute | solution.py:780
  53.1 20.1 %collective-permute-start.6 = (bf16[256,1152]{1,0:T(8,128)(2,1)S(1)}, bf16[256,1152]{1,0:T(8,128)(2,1)}, u32[]{:S(2)}, u32[]{:S(2)}) collective-permute-start(bf16[256,1152]{1,0:T(8,128)(2,1)S(1)} %collective-permute-done.2.refs_4_), channel_id=1, source_target_pairs={{1,0},{2,1},{5,4},{6,5},{9,8},{10,9},{13,12},{14,13},{17,16},{18,1... | collective-permute-start | bytes 1769480 | tf_op jit(solution)/shard_map/ppermute | solution.py:930
  80.7 21.4 %collective-permute-start.9 = (bf16[256,1152]{1,0:T(8,128)(2,1)}, bf16[256,1152]{1,0:T(8,128)(2,1)S(1)}, u32[]{:S(2)}, u32[]{:S(2)}) collective-permute-start(bf16[256,1152]{1,0:T(8,128)(2,1)} %collective-permute-done.5.refs_2_), channel_id=1, source_target_pairs={{2,3},{6,7},{10,11},{14,15},{18,19},{22,23},{26,27},{30,31}} | collective-permute-start | bytes 1769480 | tf_op jit(solution)/shard_map/ppermute | solution.py:930
  81.4 21.5 %collective-permute-start.10 = (bf16[256,1152]{1,0:T(8,128)(2,1)}, bf16[256,1152]{1,0:T(8,128)(2,1)S(1)}, u32[]{:S(2)}, u32[]{:S(2)}) collective-permute-start(bf16[256,1152]{1,0:T(8,128)(2,1)} %collective-permute-done.6.refs_5_), channel_id=1, source_target_pairs={{1,0},{5,4},{9,8},{13,12},{17,16},{21,20},{25,24},{29,28}} | collective-permute-start | bytes 1769480 | tf_op jit(solution)/shard_map/ppermute | solution.py:930
  85.0 17.1 %collective-permute-start.7 = (bf16[2,72,1152]{2,1,0:T(8,128)(2,1)S(1)}, bf16[2,72,1152]{2,1,0:T(8,128)(2,1)S(1)}, u32[]{:S(2)}, u32[]{:S(2)}) collective-permute-start(bf16[2,72,1152]{2,1,0:T(8,128)(2,1)S(1)} %get-tuple-element.209), channel_id=1, source_target_pairs={{0,16},{4,20},{8,24},{12,28},{16,0},{20,4},{24,8},{28,12},{1,17},{... | collective-permute-start | bytes 995336 | tf_op jit(solution)/shard_map/ppermute | solution.py:780
  85.6 16.5 %collective-permute-start.8 = (bf16[2,72,1152]{2,1,0:T(8,128)(2,1)S(1)}, bf16[2,72,1152]{2,1,0:T(8,128)(2,1)S(1)}, u32[]{:S(2)}, u32[]{:S(2)}) collective-permute-start(bf16[2,72,1152]{2,1,0:T(8,128)(2,1)S(1)} %get-tuple-element.211), channel_id=1, source_target_pairs={{0,8},{4,12},{8,0},{12,4},{16,24},{20,28},{24,16},{28,20},{1,9},{5... | collective-permute-start | bytes 995336 | tf_op jit(solution)/shard_map/ppermute | solution.py:780
  103.0 143.7 %all-gather.10.cloned.1.call-start = ((), (), s32[]{:S(2)}) async-start(), calls=%async_computation.10 | async-start | bytes 2949120 | tf_op jit(solution)/shard_map/all_gather | solution.py:1097
  105.4 41.8 %collective-permute-start.19 = (bf16[2,72,1152]{2,1,0:T(8,128)(2,1)S(1)}, bf16[2,72,1152]{2,1,0:T(8,128)(2,1)S(1)}, u32[]{:S(2)}, u32[]{:S(2)}) collective-permute-start(bf16[2,72,1152]{2,1,0:T(8,128)(2,1)S(1)} %add.299.refs_0_), channel_id=1, source_target_pairs={{0,3},{1,0},{2,1},{3,2},{4,7},{5,4},{6,5},{7,6},{8,11},{9,8},{10,9... | collective-permute-start | bytes 995336 | tf_op jit(solution)/shard_map/ppermute | solution.py:58
  108.8 38.3 %collective-permute-start.18 = (bf16[2,72,1152]{2,1,0:T(8,128)(2,1)S(1)}, bf16[2,72,1152]{2,1,0:T(8,128)(2,1)S(1)}, u32[]{:S(2)}, u32[]{:S(2)}) collective-permute-start(bf16[2,72,1152]{2,1,0:T(8,128)(2,1)S(1)} %add.299.refs_0_), channel_id=1, source_target_pairs={{0,2},{1,3},{2,0},{3,1},{4,6},{5,7},{6,4},{7,5},{8,10},{9,11},{10,... | collective-permute-start | bytes 995336 | tf_op jit(solution)/shard_map/ppermute | solution.py:58
  108.9 39.8 %collective-permute-start.17 = (bf16[2,72,1152]{2,1,0:T(8,128)(2,1)S(1)}, bf16[2,72,1152]{2,1,0:T(8,128)(2,1)}, u32[]{:S(2)}, u32[]{:S(2)}) collective-permute-start(bf16[2,72,1152]{2,1,0:T(8,128)(2,1)S(1)} %add.299.refs_0_), channel_id=1, source_target_pairs={{0,1},{1,2},{2,3},{3,0},{4,5},{5,6},{6,7},{7,4},{8,9},{9,10},{10,1... | collective-permute-start | bytes 995336 | tf_op jit(solution)/shard_map/ppermute | solution.py:58
  112.4 16.0 %collective-permute-start.14 = (bf16[1,72,1152]{2,1,0:T(8,128)(2,1)S(1)}, bf16[1,72,1152]{2,1,0:T(8,128)(2,1)S(1)}, u32[]{:S(2)}, u32[]{:S(2)}) collective-permute-start(bf16[1,72,1152]{2,1,0:T(8,128)(2,1)S(1)} %get-tuple-element.435), channel_id=1, source_target_pairs={{0,16},{4,20},{8,24},{12,28},{16,0},{20,4},{24,8},{28,12},{1,17},{... | collective-permute-start | bytes 497672 | tf_op jit(solution)/shard_map/ppermute | solution.py:780
  151.0 27.9 %collective-permute-start.26 = (bf16[120,288]{0,1:T(8,128)(2,1)S(1)}, bf16[120,288]{0,1:T(8,128)(2,1)S(1)}, u32[]{:S(2)}, u32[]{:S(2)}) collective-permute-start(bf16[120,288]{0,1:T(8,128)(2,1)S(1)} %fusion.18), channel_id=1, source_target_pairs={{0,3},{1,0},{2,1},{3,2},{4,7},{5,4},{6,5},{7,6},{8,11},{9,8},{10,9... | collective-permute-start | bytes 207368 | tf_op jit(solution)/shard_map/ppermute | solution.py:58
  151.0 27.9 %collective-permute-start.25 = (bf16[120,288]{0,1:T(8,128)(2,1)S(1)}, bf16[120,288]{0,1:T(8,128)(2,1)S(1)}, u32[]{:S(2)}, u32[]{:S(2)}) collective-permute-start(bf16[120,288]{0,1:T(8,128)(2,1)S(1)} %fusion.18), channel_id=1, source_target_pairs={{0,2},{1,3},{2,0},{3,1},{4,6},{5,7},{6,4},{7,5},{8,10},{9,11},{10,... | collective-permute-start | bytes 207368 | tf_op jit(solution)/shard_map/ppermute | solution.py:58
  155.4 18.9 %collective-permute-start.22 = (bf16[4,72,1152]{2,1,0:T(8,128)(2,1)}, bf16[4,72,1152]{2,1,0:T(8,128)(2,1)}, u32[]{:S(2)}, u32[]{:S(2)}) collective-permute-start(bf16[4,72,1152]{2,1,0:T(8,128)(2,1)} %get-tuple-element.225), channel_id=1, source_target_pairs={{0,8},{4,12},{8,0},{12,4},{16,24},{20,28},{24,16},{28,20},{1,9},{5... | collective-permute-start | bytes 1990664 | tf_op jit(solution)/shard_map/ppermute | solution.py:780
  155.4 21.2 %collective-permute-start.23 = (bf16[4,72,1152]{2,1,0:T(8,128)(2,1)}, bf16[4,72,1152]{2,1,0:T(8,128)(2,1)}, u32[]{:S(2)}, u32[]{:S(2)}) collective-permute-start(bf16[4,72,1152]{2,1,0:T(8,128)(2,1)} %get-tuple-element.226), channel_id=1, source_target_pairs={{0,16},{4,20},{8,24},{12,28},{16,0},{20,4},{24,8},{28,12},{1,17},{... | collective-permute-start | bytes 1990664 | tf_op jit(solution)/shard_map/ppermute | solution.py:780
  156.1 329.2 %reduce-scatter.7.cloned.1.call-start = ((), (), s32[]{:S(2)}) async-start(), calls=%async_computation.6 | async-start | bytes 5971968 | tf_op jit(solution)/shard_map/reduce_scatter | solution.py:1217
  179.0 52.6 %collective-permute-start.27 = (bf16[8,72,1152]{2,1,0:T(8,128)(2,1)}, bf16[8,72,1152]{2,1,0:T(8,128)(2,1)}, u32[]{:S(2)}, u32[]{:S(2)}) collective-permute-start(bf16[8,72,1152]{2,1,0:T(8,128)(2,1)} %pad_maximum_fusion.rest_0_), channel_id=1, source_target_pairs={{0,16},{4,20},{8,24},{12,28},{16,0},{20,4},{24,8},{28,12},{1,17},{... | collective-permute-start | bytes 3981320 | tf_op jit(solution)/shard_map/ppermute | solution.py:780
  180.1 51.4 %collective-permute-start.28 = (bf16[8,72,1152]{2,1,0:T(8,128)(2,1)}, bf16[8,72,1152]{2,1,0:T(8,128)(2,1)}, u32[]{:S(2)}, u32[]{:S(2)}) collective-permute-start(bf16[8,72,1152]{2,1,0:T(8,128)(2,1)} %pad_maximum_fusion.1.rest_2_), channel_id=1, source_target_pairs={{0,8},{4,12},{8,0},{12,4},{16,24},{20,28},{24,16},{28,20},{1,9},{5... | collective-permute-start | bytes 3981320 | tf_op jit(solution)/shard_map/ppermute | solution.py:780
  188.5 17.8 %collective-permute-start.31 = (bf16[376,288]{1,0:T(8,128)(2,1)S(1)}, bf16[376,288]{1,0:T(8,128)(2,1)}, u32[]{:S(2)}, u32[]{:S(2)}) collective-permute-start(bf16[376,288]{1,0:T(8,128)(2,1)S(1)} %get-tuple-element.438), channel_id=1, source_target_pairs={{0,1},{1,2},{2,3},{3,0},{4,5},{5,6},{6,7},{7,4},{8,9},{9,10},{10,1... | collective-permute-start | bytes 649736 | tf_op jit(solution)/shard_map/ppermute | solution.py:58
  189.0 27.3 %collective-permute-start.29 = (bf16[376,288]{1,0:T(8,128)(2,1)S(1)}, bf16[376,288]{1,0:T(8,128)(2,1)}, u32[]{:S(2)}, u32[]{:S(2)}) collective-permute-start(bf16[376,288]{1,0:T(8,128)(2,1)S(1)} %get-tuple-element.439), channel_id=1, source_target_pairs={{0,3},{1,0},{2,1},{3,2},{4,7},{5,4},{6,5},{7,6},{8,11},{9,8},{10,9... | collective-permute-start | bytes 649736 | tf_op jit(solution)/shard_map/ppermute | solution.py:58
  192.6 39.0 %collective-permute-start.30 = (bf16[376,288]{1,0:T(8,128)(2,1)S(1)}, bf16[376,288]{1,0:T(8,128)(2,1)}, u32[]{:S(2)}, u32[]{:S(2)}) collective-permute-start(bf16[376,288]{1,0:T(8,128)(2,1)S(1)} %get-tuple-element.440), channel_id=1, source_target_pairs={{0,2},{1,3},{2,0},{3,1},{4,6},{5,7},{6,4},{7,5},{8,10},{9,11},{10,... | collective-permute-start | bytes 649736 | tf_op jit(solution)/shard_map/ppermute | solution.py:58
  206.3 28.4 %collective-permute-start.32 = (bf16[8,72,1152]{2,1,0:T(8,128)(2,1)}, bf16[8,72,1152]{2,1,0:T(8,128)(2,1)}, u32[]{:S(2)}, u32[]{:S(2)}) collective-permute-start(bf16[8,72,1152]{2,1,0:T(8,128)(2,1)} %pad_maximum_fusion.rest_0_), channel_id=1, source_target_pairs={{0,4},{4,0},{8,12},{12,8},{16,20},{20,16},{24,28},{28,24},{1,5},{5... | collective-permute-start | bytes 3981320 | tf_op jit(solution)/shard_map/ppermute | solution.py:780
  216.3 18.4 %collective-permute-start.34 = (bf16[8,72,1152]{2,1,0:T(8,128)(2,1)}, bf16[8,72,1152]{2,1,0:T(8,128)(2,1)}, u32[]{:S(2)}, u32[]{:S(2)}) collective-permute-start(bf16[8,72,1152]{2,1,0:T(8,128)(2,1)} %pad_maximum_fusion.1.rest_2_), channel_id=1, source_target_pairs={{0,4},{4,0},{8,12},{12,8},{16,20},{20,16},{24,28},{28,24},{1,5},{5... | collective-permute-start | bytes 3981320 | tf_op jit(solution)/shard_map/ppermute | solution.py:780
  259.8 28.5 %collective-permute-start.37 = (bf16[256,1152]{1,0:T(8,128)(2,1)}, bf16[256,1152]{1,0:T(8,128)(2,1)}, u32[]{:S(2)}, u32[]{:S(2)}) collective-permute-start(bf16[256,1152]{1,0:T(8,128)(2,1)} %get-tuple-element.262.refs_0_.refs_6_), channel_id=1, source_target_pairs={{0,3},{1,0},{2,1},{3,2},{4,7},{5,4},{6,5},{7,6},{8,11},{9,8},{10,9... | collective-permute-start | bytes 1769480 | tf_op jit(solution)/shard_map/ppermute | solution.py:58
  260.7 27.7 %collective-permute-start.36 = (bf16[256,1152]{1,0:T(8,128)(2,1)}, bf16[256,1152]{1,0:T(8,128)(2,1)}, u32[]{:S(2)}, u32[]{:S(2)}) collective-permute-start(bf16[256,1152]{1,0:T(8,128)(2,1)} %get-tuple-element.262.refs_0_.refs_6_), channel_id=1, source_target_pairs={{0,1},{1,2},{2,3},{3,0},{4,5},{5,6},{6,7},{7,4},{8,9},{9,10},{10,1... | collective-permute-start | bytes 1769480 | tf_op jit(solution)/shard_map/ppermute | solution.py:58
  273.4 39.3 %collective-permute-start.40 = (bf16[256,1152]{1,0:T(8,128)(2,1)}, bf16[256,1152]{1,0:T(8,128)(2,1)}, u32[]{:S(2)}, u32[]{:S(2)}) collective-permute-start(bf16[256,1152]{1,0:T(8,128)(2,1)} %get-tuple-element.262.refs_0_.refs_6_), channel_id=1, source_target_pairs={{0,2},{1,3},{2,0},{3,1},{4,6},{5,7},{6,4},{7,5},{8,10},{9,11},{10,... | collective-permute-start | bytes 1769480 | tf_op jit(solution)/shard_map/ppermute | solution.py:58
  300.1 37.8 %collective-permute-start.38 = (bf16[256,1152]{1,0:T(8,128)(2,1)}, bf16[256,1152]{1,0:T(8,128)(2,1)}, u32[]{:S(2)}, u32[]{:S(2)}) collective-permute-start(bf16[256,1152]{1,0:T(8,128)(2,1)} %get-tuple-element.260), channel_id=1, source_target_pairs={{0,3},{1,0},{2,1},{3,2},{4,7},{5,4},{6,5},{7,6},{8,11},{9,8},{10,9... | collective-permute-start | bytes 1769480 | tf_op jit(solution)/shard_map/ppermute | solution.py:58
  301.4 36.5 %collective-permute-start.39 = (bf16[256,1152]{1,0:T(8,128)(2,1)}, bf16[256,1152]{1,0:T(8,128)(2,1)}, u32[]{:S(2)}, u32[]{:S(2)}) collective-permute-start(bf16[256,1152]{1,0:T(8,128)(2,1)} %get-tuple-element.261), channel_id=1, source_target_pairs={{0,1},{1,2},{2,3},{3,0},{4,5},{5,6},{6,7},{7,4},{8,9},{9,10},{10,1... | collective-permute-start | bytes 1769480 | tf_op jit(solution)/shard_map/ppermute | solution.py:58
  319.8 43.4 %collective-permute-start.41 = (bf16[256,1152]{1,0:T(8,128)(2,1)}, bf16[256,1152]{1,0:T(8,128)(2,1)}, u32[]{:S(2)}, u32[]{:S(2)}) collective-permute-start(bf16[256,1152]{1,0:T(8,128)(2,1)} %get-tuple-element.264), channel_id=1, source_target_pairs={{0,2},{1,3},{2,0},{3,1},{4,6},{5,7},{6,4},{7,5},{8,10},{9,11},{10,... | collective-permute-start | bytes 1769480 | tf_op jit(solution)/shard_map/ppermute | solution.py:58
  375.5 141.6 %reduce-scatter.9.cloned.1.call-start = ((), (), s32[]{:S(2)}) async-start(), calls=%async_computation.7 | async-start | bytes 2949120 | tf_op jit(solution)/shard_map/reduce_scatter | solution.py:1288
  397.1 23.8 %collective-permute-start.45 = (bf16[2,4,288,1152]{3,2,1,0:T(8,128)(2,1)}, bf16[2,4,288,1152]{3,2,1,0:T(8,128)(2,1)}, u32[]{:S(2)}, u32[]{:S(2)}) collective-permute-start(bf16[2,4,288,1152]{3,2,1,0:T(8,128)(2,1)} %get-tuple-element.282), channel_id=1, source_target_pairs={{0,4},{4,0},{8,12},{12,8},{16,20},{20,16},{24,28},{28,24},{1,5},{5... | collective-permute-start | bytes 15925256 | tf_op jit(solution)/shard_map/ppermute | solution.py:780
  398.1 22.8 %collective-permute-start.43 = (bf16[376,288]{1,0:T(8,128)(2,1)}, bf16[376,288]{1,0:T(8,128)(2,1)S(1)}, u32[]{:S(2)}, u32[]{:S(2)}) collective-permute-start(bf16[376,288]{1,0:T(8,128)(2,1)} %get-tuple-element.273), channel_id=1, source_target_pairs={{0,2},{1,3},{2,0},{3,1},{4,6},{5,7},{6,4},{7,5},{8,10},{9,11},{10,... | collective-permute-start | bytes 649736 | tf_op jit(solution)/shard_map/ppermute | solution.py:58
  401.3 19.6 %collective-permute-start.44 = (bf16[376,288]{1,0:T(8,128)(2,1)}, bf16[376,288]{1,0:T(8,128)(2,1)}, u32[]{:S(2)}, u32[]{:S(2)}) collective-permute-start(bf16[376,288]{1,0:T(8,128)(2,1)} %get-tuple-element.274), channel_id=1, source_target_pairs={{0,3},{1,0},{2,1},{3,2},{4,7},{5,4},{6,5},{7,6},{8,11},{9,8},{10,9... | collective-permute-start | bytes 649736 | tf_op jit(solution)/shard_map/ppermute | solution.py:58
  420.9 122.3 %all-gather.8.cloned.1.call-start = ((), (), s32[]{:S(2)}) async-start(), calls=%async_computation.9 | async-start | bytes 5971968 | tf_op jit(solution)/shard_map/all_gather | solution.py:1311
  430.0 31.5 %collective-permute-start.46 = (bf16[4,2,72,1152]{3,2,1,0:T(8,128)(2,1)}, bf16[4,2,72,1152]{3,2,1,0:T(8,128)(2,1)}, u32[]{:S(2)}, u32[]{:S(2)}) collective-permute-start(bf16[4,2,72,1152]{3,2,1,0:T(8,128)(2,1)} %get-tuple-element.288), channel_id=1, source_target_pairs={{0,8},{4,12},{8,0},{12,4},{16,24},{20,28},{24,16},{28,20},{1,9},{5... | collective-permute-start | bytes 3981320 | tf_op jit(solution)/shard_map/ppermute | solution.py:780
  431.8 31.1 %collective-permute-start.47 = (bf16[4,2,72,1152]{3,2,1,0:T(8,128)(2,1)}, bf16[4,2,72,1152]{3,2,1,0:T(8,128)(2,1)}, u32[]{:S(2)}, u32[]{:S(2)}) collective-permute-start(bf16[4,2,72,1152]{3,2,1,0:T(8,128)(2,1)} %get-tuple-element.290), channel_id=1, source_target_pairs={{0,16},{4,20},{8,24},{12,28},{16,0},{20,4},{24,8},{28,12},{1,17},{... | collective-permute-start | bytes 3981320 | tf_op jit(solution)/shard_map/ppermute | solution.py:780
  468.4 15.8 %collective-permute-start.48 = (bf16[4,72,1152]{2,1,0:T(8,128)(2,1)S(1)}, bf16[4,72,1152]{2,1,0:T(8,128)(2,1)}, u32[]{:S(2)}, u32[]{:S(2)}) collective-permute-start(bf16[4,72,1152]{2,1,0:T(8,128)(2,1)S(1)} %get-tuple-element.305), channel_id=1, source_target_pairs={{0,16},{4,20},{8,24},{12,28},{16,0},{20,4},{24,8},{28,12},{1,17},{... | collective-permute-start | bytes 1990664 | tf_op jit(solution)/shard_map/ppermute | solution.py:780
  485.4 109.3 %reduce-scatter.11.cloned.1.call-start = ((), (), s32[]{:S(2)}) async-start(), calls=%async_computation.8 | async-start | bytes 2949120 | tf_op jit(solution)/shard_map/reduce_scatter | solution.py:1323
  497.5 19.6 %collective-permute-start.50 = (bf16[2,1,288,1152]{3,2,1,0:T(8,128)(2,1)}, bf16[2,1,288,1152]{3,2,1,0:T(8,128)(2,1)}, u32[]{:S(2)}, u32[]{:S(2)}) collective-permute-start(bf16[2,1,288,1152]{3,2,1,0:T(8,128)(2,1)} %get-tuple-element.325), channel_id=1, source_target_pairs={{0,4},{4,0},{8,12},{12,8},{16,20},{20,16},{24,28},{28,24},{1,5},{5... | collective-permute-start | bytes 3981320 | tf_op jit(solution)/shard_map/ppermute | solution.py:780
  497.6 27.3 %collective-permute-start.55 = (bf16[2,72,1152]{2,1,0:T(8,128)(2,1)}, bf16[2,72,1152]{2,1,0:T(8,128)(2,1)S(1)}, u32[]{:S(2)}, u32[]{:S(2)}) collective-permute-start(bf16[2,72,1152]{2,1,0:T(8,128)(2,1)} %get-tuple-element.340), channel_id=1, source_target_pairs={{0,1},{1,2},{2,3},{3,0},{4,5},{5,6},{6,7},{7,4},{8,9},{9,10},{10,1... | collective-permute-start | bytes 995336 | tf_op jit(solution)/shard_map/ppermute | solution.py:58
  504.3 21.3 %collective-permute-start.56 = (bf16[2,72,1152]{2,1,0:T(8,128)(2,1)}, bf16[2,72,1152]{2,1,0:T(8,128)(2,1)S(1)}, u32[]{:S(2)}, u32[]{:S(2)}) collective-permute-start(bf16[2,72,1152]{2,1,0:T(8,128)(2,1)} %get-tuple-element.341), channel_id=1, source_target_pairs={{0,2},{1,3},{2,0},{3,1},{4,6},{5,7},{6,4},{7,5},{8,10},{9,11},{10,... | collective-permute-start | bytes 995336 | tf_op jit(solution)/shard_map/ppermute | solution.py:58
  504.3 22.3 %collective-permute-start.57 = (bf16[2,72,1152]{2,1,0:T(8,128)(2,1)}, bf16[2,72,1152]{2,1,0:T(8,128)(2,1)S(1)}, u32[]{:S(2)}, u32[]{:S(2)}) collective-permute-start(bf16[2,72,1152]{2,1,0:T(8,128)(2,1)} %get-tuple-element.342), channel_id=1, source_target_pairs={{0,3},{1,0},{2,1},{3,2},{4,7},{5,4},{6,5},{7,6},{8,11},{9,8},{10,9... | collective-permute-start | bytes 995336 | tf_op jit(solution)/shard_map/ppermute | solution.py:58
  (95 other events, 1145.2 us)
Sparse Core Ops, SparseCore 0:
  21.7 80.1 reduce-scatter.4
  103.9 47.4 all-gather.5
  156.3 70.6 all-gather.9
  375.6 58.1 reduce-scatter.6
  436.0 48.0 reduce-scatter.8
  485.8 48.1 all-gather.7
  547.2 47.4 reduce-scatter.10
